TPU v7x, 32 devices: a whole 2x2x4 slice. The times are simulated.
32 devices in a mesh: dp: 16 (over z, y, core), tensor: 2 (over x).
Axes of the slice: x: 2, y: 2, z: 4, core: 2. Of those that a mesh axis runs over, the one named last changes fastest.
Arguments:
- tokens_in: bfloat16 [2, 16, 4, 512, 1024], P(None, 'dp', None, 'tensor'), may hold values from -6 to 6
- piece_starts: int32 [2, 16, 2], P(None, 'dp'), may hold values from 0 to 1792, as said below
- cotangent: bfloat16 [2, 16, 4, 512, 1024], P(None, 'dp', None, 'tensor'), may hold values from -6 to 6
- gain_tokens: bfloat16 [1024], P('dp'), may hold values from 0.099609375 to 1.8984375
- gain_mlp: bfloat16 [1024], P('dp'), may hold values from 0.099609375 to 1.8984375
- gain_state: bfloat16 [1024], P('dp'), may hold values from 0.099609375 to 1.8984375
- gate_bias: bfloat16 [1024], P('dp'), may hold values from -2 to 3
- w_query: bfloat16 [1024, 1024], P('dp', 'tensor'), may hold values from -0.1875 to 0.1875
- w_key: bfloat16 [1024, 1024], P('dp', 'tensor'), may hold values from -0.1875 to 0.1875
- w_value: bfloat16 [1024, 1024], P('dp', 'tensor'), may hold values from -0.1875 to 0.1875
- w_out: bfloat16 [1024, 1024], P('tensor', 'dp'), may hold values from -3 to 3
- w_state_query: bfloat16 [1024, 1024], P('dp', 'tensor'), may hold values from -0.1875 to 0.1875
- w_state_key: bfloat16 [1024, 1024], P('dp', 'tensor'), may hold values from -0.1875 to 0.1875
- w_state_value: bfloat16 [1024, 1024], P('dp', 'tensor'), may hold values from -0.1875 to 0.1875
- w_state_out: bfloat16 [1024, 1024], P('tensor', 'dp'), may hold values from -3 to 3
- w_gate: bfloat16 [1024, 1024], P('dp', 'tensor'), may hold values from -0.1875 to 0.1875
- w_up: bfloat16 [1024, 4096], P('dp', 'tensor'), may hold values from -0.1875 to 0.1875
- w_down: bfloat16 [4096, 1024], P('tensor', 'dp'), may hold values from -0.09375 to 0.09375
- state_init: bfloat16 [512, 1024], P('dp', 'tensor'), may hold values from -6 to 6
Outputs:
- output: bfloat16 [2, 16, 4, 512, 1024], P(None, 'dp', None, 'tensor')
- grad_tokens: bfloat16 [2, 16, 4, 512, 1024], P(None, 'dp', None, 'tensor')
- grad_gain_tokens: float32 [1024], P('dp')
- grad_gain_mlp: float32 [1024], P('dp')
- grad_gain_state: float32 [1024], P('dp')
- grad_gate_bias: float32 [1024], P('dp')
- grad_w_query: float32 [1024, 1024], P('dp', 'tensor')
- grad_w_key: float32 [1024, 1024], P('dp', 'tensor')
- grad_w_value: float32 [1024, 1024], P('dp', 'tensor')
- grad_w_out: float32 [1024, 1024], P('tensor', 'dp')
- grad_w_state_query: float32 [1024, 1024], P('dp', 'tensor')
- grad_w_state_key: float32 [1024, 1024], P('dp', 'tensor')
- grad_w_state_value: float32 [1024, 1024], P('dp', 'tensor')
- grad_w_state_out: float32 [1024, 1024], P('tensor', 'dp')
- grad_w_gate: float32 [1024, 1024], P('dp', 'tensor')
- grad_w_up: float32 [1024, 4096], P('dp', 'tensor')
- grad_w_down: float32 [4096, 1024], P('tensor', 'dp')
- grad_state_init: float32 [512, 1024], P('dp', 'tensor')
Inputs may be any that keep to these rules, and one draw needn't show every extreme that they name: `piece_starts`: each sequence has 2 distinct picture pieces; every start is a multiple of 256.
All inputs are finite; a program needn't handle non-finite values.
Results may differ from a plain program's by a relative error of at most 0.025.
Values may be sent and summed in bfloat16 or wider, within the bound.
No kernel may reach another device: no remote copies, remote signals or barrier semaphores. Data moves between devices by JAX's collectives and lax.ppermute only.
A program may use at most 472 MiB of HBM per device.

v0:
```python
import math

import jax
import jax.numpy as jnp
from jax import lax
from jax.sharding import PartitionSpec as P

D = 1024
HEAD = 128
W = 512
S = 512
PIECE = 256
MICRO = 2
NB = 4


epsilon = 1e-06
masked_score = -1e30


def rms_scale(values):
    return values * lax.rsqrt(jnp.mean(values * values, axis=-1, keepdims=True) + epsilon)


def normed_rows(values, gain):
    return rms_scale(values) * gain


def matmul(left, right):
    return jnp.dot(left, right, preferred_element_type=jnp.float32)


def mlp_local(full_in, full_up, full_down):
    hidden = matmul(full_in, full_up)
    active = jax.nn.gelu(hidden).astype(jnp.bfloat16)
    return (hidden, active, matmul(active, full_down))


def mlp_back_local(full_grad, active, hidden, full_in, full_down, full_up):
    grad_down_w = jnp.einsum("...f,...d->fd", active, full_grad, preferred_element_type=jnp.float32)
    grad_active = jnp.einsum(
        "...d,fd->...f", full_grad, full_down, preferred_element_type=jnp.float32
    )
    unused_value, gelu_back = jax.vjp(jax.nn.gelu, hidden)
    grad_hidden = gelu_back(grad_active)[0].astype(jnp.bfloat16)
    grad_up_w = jnp.einsum(
        "...d,...f->df", full_in, grad_hidden, preferred_element_type=jnp.float32
    )
    mlp_part = jnp.einsum("...f,df->...d", grad_hidden, full_up, preferred_element_type=jnp.float32)
    return (grad_down_w, grad_up_w, mlp_part)


def piece_labels(starts):
    positions = jnp.arange(NB * W, dtype=jnp.int32)
    inside = (positions[None, None, :] >= starts[:, :, None]) & (
        positions[None, None, :] < starts[:, :, None] + PIECE
    )
    numbers = jnp.arange(1, starts.shape[1] + 1, dtype=jnp.int32)
    return jnp.sum(jnp.where(inside, numbers[None, :, None], 0), axis=1)


def token_mask(labels, block):
    batch = labels.shape[0]
    own = labels[:, block * W : (block + 1) * W]
    local = jnp.arange(W, dtype=jnp.int32)
    causal = (local[None, :] <= local[:, None])[None]
    together = (own[:, :, None] == own[:, None, :]) & (own[:, :, None] > 0)
    current = causal | together
    earlier = jnp.full((batch, W, W), block > 0)
    state_part = jnp.ones((batch, W, S), dtype=bool)
    return jnp.concatenate([earlier, current, state_part], axis=2)[:, None]


def split_heads(values):
    return values.reshape(values.shape[0], values.shape[1], values.shape[2] // HEAD, HEAD)


def scores_of(query, keys, allowed):
    scores = jnp.einsum(
        "brhe,bkhe->bhrk", split_heads(query), split_heads(keys), preferred_element_type=jnp.float32
    ) * (1.0 / math.sqrt(HEAD))
    return jnp.where(allowed, scores, masked_score)


def attend(query, keys, values, allowed):
    scores = scores_of(query, keys, allowed)
    top = jnp.max(scores, axis=-1, keepdims=True)
    total = top + jnp.log(jnp.sum(jnp.exp(scores - top), axis=-1, keepdims=True))
    weights = jnp.exp(scores - total).astype(jnp.bfloat16)
    mixed = jnp.einsum(
        "bhrk,bkhe->brhe", weights, split_heads(values), preferred_element_type=jnp.float32
    )
    return (mixed.reshape(query.shape).astype(jnp.bfloat16), total)


def attend_back(query, keys, values, allowed, total, grad_mixed):
    scale = 1.0 / math.sqrt(HEAD)
    weights = jnp.exp(scores_of(query, keys, allowed) - total)
    grad_heads = split_heads(grad_mixed)
    grad_weights = jnp.einsum(
        "brhe,bkhe->bhrk", grad_heads, split_heads(values), preferred_element_type=jnp.float32
    )
    grad_scores = (
        weights * (grad_weights - jnp.sum(weights * grad_weights, axis=-1, keepdims=True))
    ).astype(jnp.bfloat16)
    grad_query = (
        jnp.einsum(
            "bhrk,bkhe->brhe", grad_scores, split_heads(keys), preferred_element_type=jnp.float32
        )
        * scale
    )
    grad_keys = (
        jnp.einsum(
            "bhrk,brhe->bkhe", grad_scores, split_heads(query), preferred_element_type=jnp.float32
        )
        * scale
    )
    grad_values = jnp.einsum(
        "bhrk,brhe->bkhe",
        weights.astype(jnp.bfloat16),
        grad_heads,
        preferred_element_type=jnp.float32,
    )
    return (
        grad_query.reshape(query.shape),
        grad_keys.reshape(keys.shape),
        grad_values.reshape(values.shape),
    )


def body(
    tokens_in,
    piece_starts,
    cotangent,
    gain_tokens,
    gain_mlp,
    gain_state,
    gate_bias,
    w_query,
    w_key,
    w_value,
    w_out,
    w_state_query,
    w_state_key,
    w_state_value,
    w_state_out,
    w_gate,
    w_up,
    w_down,
    state_init,
):
    width_local = w_query.shape[1]
    column_start = lax.axis_index("tensor") * width_local

    def collect():
        return (
            lax.all_gather(w_query, "dp", axis=0, tiled=True),
            lax.all_gather(w_key, "dp", axis=0, tiled=True),
            lax.all_gather(w_value, "dp", axis=0, tiled=True),
            lax.all_gather(w_state_query, "dp", axis=0, tiled=True),
            lax.all_gather(w_state_key, "dp", axis=0, tiled=True),
            lax.all_gather(w_state_value, "dp", axis=0, tiled=True),
            lax.all_gather(w_gate, "dp", axis=0, tiled=True),
            lax.all_gather(w_up, "dp", axis=0, tiled=True),
            lax.all_gather(state_init, "dp", axis=0, tiled=True),
            lax.all_gather(w_out, "dp", axis=1, tiled=True),
            lax.all_gather(w_state_out, "dp", axis=1, tiled=True),
            lax.all_gather(w_down, "dp", axis=1, tiled=True),
            lax.all_gather(gain_tokens, "dp", axis=0, tiled=True),
            lax.all_gather(gain_mlp, "dp", axis=0, tiled=True),
            lax.all_gather(gain_state, "dp", axis=0, tiled=True),
            lax.all_gather(gate_bias, "dp", axis=0, tiled=True),
        )

    def unpack_gains(weights):
        token_gain = weights[12].astype(jnp.float32)
        mlp_gain = weights[13].astype(jnp.float32)
        state_gain = lax.dynamic_slice_in_dim(
            weights[14].astype(jnp.float32), column_start, width_local
        )
        bias_columns = lax.dynamic_slice_in_dim(
            weights[15].astype(jnp.float32), column_start, width_local
        )
        return (token_gain, mlp_gain, state_gain, bias_columns)

    outputs = []
    input_grads = []
    totals = None
    for micro in range(MICRO):
        forward_weights = collect()
        forward_rows_in = tokens_in[micro]
        (
            forward_full_query,
            forward_full_key,
            forward_full_value,
            forward_full_state_query,
            forward_full_state_key,
            forward_full_state_value,
            forward_full_gate,
            forward_full_up,
            forward_full_init,
            forward_full_out,
            forward_full_state_out,
            forward_full_down,
        ) = forward_weights[:12]
        forward_token_gain, forward_mlp_gain, forward_state_gain, forward_bias_columns = (
            unpack_gains(forward_weights)
        )
        forward_batch = forward_rows_in.shape[0]
        forward_labels = piece_labels(piece_starts[micro])
        forward_state = jnp.broadcast_to(
            forward_full_init.astype(jnp.float32), (forward_batch, S, width_local)
        )
        zero_keys = jnp.zeros((forward_batch, W, width_local), jnp.bfloat16)
        forward_earlier_key = zero_keys
        forward_earlier_value = zero_keys
        forward_kept = []
        middles = []
        for forward_block in range(NB):
            forward_rows = forward_rows_in[:, forward_block].astype(jnp.float32)
            normed = normed_rows(forward_rows, forward_token_gain).astype(jnp.bfloat16)
            square_sum = lax.psum(jnp.sum(forward_state * forward_state, axis=-1), "tensor")
            forward_inverse = lax.rsqrt(square_sum / D + epsilon)[..., None]
            forward_scaled = forward_state * forward_inverse
            state_normed = (forward_scaled * forward_state_gain).astype(jnp.bfloat16)
            forward_full_normed, forward_full_state = (
                lax.all_gather(normed, "tensor", axis=1, tiled=True),
                lax.all_gather(state_normed, "tensor", axis=2, tiled=True),
            )
            forward_query = matmul(forward_full_normed, forward_full_query).astype(jnp.bfloat16)
            forward_key = matmul(forward_full_normed, forward_full_key).astype(jnp.bfloat16)
            forward_value = matmul(forward_full_normed, forward_full_value).astype(jnp.bfloat16)
            forward_state_query = matmul(forward_full_state, forward_full_state_query).astype(
                jnp.bfloat16
            )
            forward_state_key = matmul(forward_full_state, forward_full_state_key).astype(
                jnp.bfloat16
            )
            forward_state_value = matmul(forward_full_state, forward_full_state_value).astype(
                jnp.bfloat16
            )
            gate_pre = matmul(forward_full_state, forward_full_gate) + forward_bias_columns
            forward_allowed = token_mask(forward_labels, forward_block)
            forward_token_keys = jnp.concatenate(
                [forward_earlier_key, forward_key, forward_state_key], axis=1
            )
            forward_token_values = jnp.concatenate(
                [forward_earlier_value, forward_value, forward_state_value], axis=1
            )
            forward_token_mixed, forward_token_total = attend(
                forward_query, forward_token_keys, forward_token_values, forward_allowed
            )
            forward_cross_keys = jnp.concatenate([forward_key, forward_state_key], axis=1)
            forward_cross_values = jnp.concatenate([forward_value, forward_state_value], axis=1)
            forward_state_mixed, forward_state_total = attend(
                forward_state_query, forward_cross_keys, forward_cross_values, True
            )
            forward_row_part = matmul(forward_token_mixed, forward_full_out)
            forward_state_part = matmul(forward_state_mixed, forward_full_state_out)
            row_sum, forward_state_sum = (
                lax.psum_scatter(
                    forward_row_part.astype(jnp.bfloat16), "tensor", scatter_dimension=1, tiled=True
                ).astype(jnp.float32),
                lax.psum_scatter(
                    forward_state_part.astype(jnp.bfloat16),
                    "tensor",
                    scatter_dimension=2,
                    tiled=True,
                ).astype(jnp.float32),
            )
            forward_forget = jax.nn.sigmoid(gate_pre)
            forward_kept.append(
                (
                    forward_full_normed,
                    forward_full_state,
                    forward_query,
                    forward_key,
                    forward_value,
                    forward_state_query,
                    forward_state_key,
                    forward_state_value,
                    forward_token_mixed,
                    forward_state_mixed,
                    forward_token_total,
                    forward_state_total,
                    forward_state,
                    forward_scaled,
                    forward_inverse,
                    forward_forget,
                    forward_state_sum,
                    forward_earlier_key,
                    forward_earlier_value,
                )
            )
            middle_block = forward_rows + row_sum
            middles.append(middle_block)
            forward_state = (
                forward_forget * forward_state + (1.0 - forward_forget) * forward_state_sum
            )
            forward_earlier_key, forward_earlier_value = (forward_key, forward_value)
        forward_middle = jnp.stack(middles, axis=1)
        mlp_in = normed_rows(forward_middle, forward_mlp_gain).astype(jnp.bfloat16)
        forward_full_mlp_in = lax.all_gather(mlp_in, "tensor", axis=2, tiled=True)
        forward_hidden, forward_active, mlp_partial = mlp_local(
            forward_full_mlp_in, forward_full_up, forward_full_down
        )
        mlp_sum = lax.psum_scatter(
            mlp_partial.astype(jnp.bfloat16), "tensor", scatter_dimension=2, tiled=True
        ).astype(jnp.float32)
        output = (forward_middle + mlp_sum).astype(jnp.bfloat16)
        output, saved = (
            output,
            (
                forward_kept,
                forward_middle,
                forward_full_mlp_in,
                forward_hidden,
                forward_active,
                forward_labels,
            ),
        )
        outputs.append(output)
        backward_weights = collect()
        rows_in = tokens_in[micro]
        grad_rows_out = cotangent[micro]
        (
            full_query,
            full_key,
            full_value,
            full_state_query,
            full_state_key,
            full_state_value,
            full_gate,
            full_up,
            full_init,
            full_out,
            full_state_out,
            full_down,
        ) = backward_weights[:12]
        backward_token_gain, backward_mlp_gain, backward_state_gain, backward_bias_columns = (
            unpack_gains(backward_weights)
        )
        kept, middle, full_mlp_in, hidden, active, labels = saved
        batch = rows_in.shape[0]
        full_grad = lax.all_gather(grad_rows_out, "tensor", axis=2, tiled=True)
        grad_down_w, grad_up_w, mlp_part = mlp_back_local(
            full_grad, active, hidden, full_mlp_in, full_down, full_up
        )
        grad_mlp_in = lax.psum_scatter(
            mlp_part.astype(jnp.bfloat16), "tensor", scatter_dimension=2, tiled=True
        ).astype(jnp.float32)
        unused_norm, mlp_norm_back = jax.vjp(normed_rows, middle, backward_mlp_gain)
        grad_middle_norm, grad_mlp_gain = mlp_norm_back(grad_mlp_in)
        grad_middle = grad_rows_out.astype(jnp.float32) + grad_middle_norm
        grad_state = jnp.zeros((batch, S, width_local), jnp.float32)
        carry_key = jnp.zeros((batch, W, width_local), jnp.float32)
        carry_value = jnp.zeros((batch, W, width_local), jnp.float32)
        square_zero = jnp.zeros((D, width_local), jnp.float32)
        grad_query_w = square_zero
        grad_key_w = square_zero
        grad_value_w = square_zero
        grad_state_query_w = square_zero
        grad_state_key_w = square_zero
        grad_state_value_w = square_zero
        grad_gate_w = square_zero
        grad_out_w = jnp.zeros((width_local, D), jnp.float32)
        grad_state_out_w = jnp.zeros((width_local, D), jnp.float32)
        grad_token_gain = jnp.zeros((D,), jnp.float32)
        grad_state_gain = jnp.zeros((width_local,), jnp.float32)
        grad_bias = jnp.zeros((width_local,), jnp.float32)
        grad_rows = [None] * NB
        for block in reversed(range(NB)):
            (
                full_normed,
                full_state,
                query,
                key,
                value,
                state_query,
                state_key,
                state_value,
                token_mixed,
                state_mixed,
                token_total,
                state_total,
                state,
                scaled,
                inverse,
                forget,
                state_sum,
                earlier_key,
                earlier_value,
            ) = kept[block]
            grad_row_block = grad_middle[:, block]
            grad_branch_state = ((1.0 - forget) * grad_state).astype(jnp.bfloat16)
            grad_gate = (grad_state * (state - state_sum) * forget * (1.0 - forget)).astype(
                jnp.bfloat16
            )
            carried_state = grad_state * forget
            full_grad_rows, full_grad_state = (
                lax.all_gather(grad_row_block.astype(jnp.bfloat16), "tensor", axis=1, tiled=True),
                lax.all_gather(grad_branch_state, "tensor", axis=2, tiled=True),
            )
            grad_out_w = grad_out_w + jnp.einsum(
                "bwc,bwd->cd", token_mixed, full_grad_rows, preferred_element_type=jnp.float32
            )
            grad_state_out_w = grad_state_out_w + jnp.einsum(
                "bsc,bsd->cd", state_mixed, full_grad_state, preferred_element_type=jnp.float32
            )
            grad_token_mixed = jnp.einsum(
                "bwd,cd->bwc", full_grad_rows, full_out, preferred_element_type=jnp.float32
            ).astype(jnp.bfloat16)
            grad_state_mixed = jnp.einsum(
                "bsd,cd->bsc", full_grad_state, full_state_out, preferred_element_type=jnp.float32
            ).astype(jnp.bfloat16)
            allowed = token_mask(labels, block)
            token_keys = jnp.concatenate([earlier_key, key, state_key], axis=1)
            token_values = jnp.concatenate([earlier_value, value, state_value], axis=1)
            cross_keys = jnp.concatenate([key, state_key], axis=1)
            cross_values = jnp.concatenate([value, state_value], axis=1)
            token_grad_query, token_grad_keys, token_grad_values = attend_back(
                query, token_keys, token_values, allowed, token_total, grad_token_mixed
            )
            state_grad_query, cross_grad_keys, cross_grad_values = attend_back(
                state_query, cross_keys, cross_values, True, state_total, grad_state_mixed
            )
            grad_key = (token_grad_keys[:, W : 2 * W] + cross_grad_keys[:, :W] + carry_key).astype(
                jnp.bfloat16
            )
            grad_value = (
                token_grad_values[:, W : 2 * W] + cross_grad_values[:, :W] + carry_value
            ).astype(jnp.bfloat16)
            carry_key = token_grad_keys[:, :W]
            carry_value = token_grad_values[:, :W]
            grad_state_key = (token_grad_keys[:, 2 * W :] + cross_grad_keys[:, W:]).astype(
                jnp.bfloat16
            )
            grad_state_value = (token_grad_values[:, 2 * W :] + cross_grad_values[:, W:]).astype(
                jnp.bfloat16
            )
            grad_query = token_grad_query.astype(jnp.bfloat16)
            grad_state_query = state_grad_query.astype(jnp.bfloat16)
            grad_query_w = grad_query_w + jnp.einsum(
                "bwd,bwc->dc", full_normed, grad_query, preferred_element_type=jnp.float32
            )
            grad_key_w = grad_key_w + jnp.einsum(
                "bwd,bwc->dc", full_normed, grad_key, preferred_element_type=jnp.float32
            )
            grad_value_w = grad_value_w + jnp.einsum(
                "bwd,bwc->dc", full_normed, grad_value, preferred_element_type=jnp.float32
            )
            grad_state_query_w = grad_state_query_w + jnp.einsum(
                "bsd,bsc->dc", full_state, grad_state_query, preferred_element_type=jnp.float32
            )
            grad_state_key_w = grad_state_key_w + jnp.einsum(
                "bsd,bsc->dc", full_state, grad_state_key, preferred_element_type=jnp.float32
            )
            grad_state_value_w = grad_state_value_w + jnp.einsum(
                "bsd,bsc->dc", full_state, grad_state_value, preferred_element_type=jnp.float32
            )
            grad_gate_w = grad_gate_w + jnp.einsum(
                "bsd,bsc->dc", full_state, grad_gate, preferred_element_type=jnp.float32
            )
            grad_bias = grad_bias + jnp.sum(grad_gate.astype(jnp.float32), axis=(0, 1))
            row_part = jnp.einsum(
                "bwc,dc->bwd", grad_query, full_query, preferred_element_type=jnp.float32
            )
            row_part = row_part + jnp.einsum(
                "bwc,dc->bwd", grad_key, full_key, preferred_element_type=jnp.float32
            )
            row_part = row_part + jnp.einsum(
                "bwc,dc->bwd", grad_value, full_value, preferred_element_type=jnp.float32
            )
            state_part = jnp.einsum(
                "bsc,dc->bsd",
                grad_state_query,
                full_state_query,
                preferred_element_type=jnp.float32,
            )
            state_part = state_part + jnp.einsum(
                "bsc,dc->bsd", grad_state_key, full_state_key, preferred_element_type=jnp.float32
            )
            state_part = state_part + jnp.einsum(
                "bsc,dc->bsd",
                grad_state_value,
                full_state_value,
                preferred_element_type=jnp.float32,
            )
            state_part = state_part + jnp.einsum(
                "bsc,dc->bsd", grad_gate, full_gate, preferred_element_type=jnp.float32
            )
            grad_normed, grad_state_normed = (
                lax.psum_scatter(
                    row_part.astype(jnp.bfloat16), "tensor", scatter_dimension=1, tiled=True
                ).astype(jnp.float32),
                lax.psum_scatter(
                    state_part.astype(jnp.bfloat16), "tensor", scatter_dimension=2, tiled=True
                ).astype(jnp.float32),
            )
            rows = rows_in[:, block].astype(jnp.float32)
            unused_rows, token_norm_back = jax.vjp(normed_rows, rows, backward_token_gain)
            grad_rows_norm, grad_gain_part = token_norm_back(grad_normed)
            grad_token_gain = grad_token_gain + grad_gain_part
            grad_rows[block] = (grad_row_block + grad_rows_norm).astype(jnp.bfloat16)
            grad_scaled = grad_state_normed * backward_state_gain
            grad_state_gain = grad_state_gain + jnp.sum(grad_state_normed * scaled, axis=(0, 1))
            dot_sum = lax.psum(jnp.sum(grad_scaled * scaled, axis=-1), "tensor")
            grad_state = carried_state + inverse * (grad_scaled - scaled * (dot_sum / D)[..., None])
        grad_init = jnp.sum(grad_state, axis=0)
        state_gain_full = lax.dynamic_update_slice_in_dim(
            jnp.zeros((D,), jnp.float32), grad_state_gain, column_start, 0
        )
        bias_full = lax.dynamic_update_slice_in_dim(
            jnp.zeros((D,), jnp.float32), grad_bias, column_start, 0
        )
        grads = (
            grad_query_w,
            grad_key_w,
            grad_value_w,
            grad_state_query_w,
            grad_state_key_w,
            grad_state_value_w,
            grad_gate_w,
            grad_up_w,
            grad_init,
            grad_out_w,
            grad_state_out_w,
            grad_down_w,
            grad_token_gain,
            grad_mlp_gain,
            state_gain_full,
            bias_full,
        )
        grads, grad_in = (grads, jnp.stack(grad_rows, axis=1))
        input_grads.append(grad_in)
        if totals is None:
            totals = grads
        else:
            totals = tuple((first + second for first, second in zip(totals, grads)))
    reduced = (
        lax.psum_scatter(
            totals[0].astype(jnp.bfloat16), "dp", scatter_dimension=0, tiled=True
        ).astype(jnp.float32),
        lax.psum_scatter(
            totals[1].astype(jnp.bfloat16), "dp", scatter_dimension=0, tiled=True
        ).astype(jnp.float32),
        lax.psum_scatter(
            totals[2].astype(jnp.bfloat16), "dp", scatter_dimension=0, tiled=True
        ).astype(jnp.float32),
        lax.psum_scatter(
            totals[3].astype(jnp.bfloat16), "dp", scatter_dimension=0, tiled=True
        ).astype(jnp.float32),
        lax.psum_scatter(
            totals[4].astype(jnp.bfloat16), "dp", scatter_dimension=0, tiled=True
        ).astype(jnp.float32),
        lax.psum_scatter(
            totals[5].astype(jnp.bfloat16), "dp", scatter_dimension=0, tiled=True
        ).astype(jnp.float32),
        lax.psum_scatter(
            totals[6].astype(jnp.bfloat16), "dp", scatter_dimension=0, tiled=True
        ).astype(jnp.float32),
        lax.psum_scatter(
            totals[7].astype(jnp.bfloat16), "dp", scatter_dimension=0, tiled=True
        ).astype(jnp.float32),
        lax.psum_scatter(
            totals[8].astype(jnp.bfloat16), "dp", scatter_dimension=0, tiled=True
        ).astype(jnp.float32),
        lax.psum_scatter(
            totals[9].astype(jnp.bfloat16), "dp", scatter_dimension=1, tiled=True
        ).astype(jnp.float32),
        lax.psum_scatter(
            totals[10].astype(jnp.bfloat16), "dp", scatter_dimension=1, tiled=True
        ).astype(jnp.float32),
        lax.psum_scatter(
            totals[11].astype(jnp.bfloat16), "dp", scatter_dimension=1, tiled=True
        ).astype(jnp.float32),
        lax.psum_scatter(
            totals[12].astype(jnp.bfloat16), "dp", scatter_dimension=0, tiled=True
        ).astype(jnp.float32),
        lax.psum_scatter(
            totals[13].astype(jnp.bfloat16), "dp", scatter_dimension=0, tiled=True
        ).astype(jnp.float32),
        lax.psum_scatter(
            totals[14].astype(jnp.bfloat16), "dp", scatter_dimension=0, tiled=True
        ).astype(jnp.float32),
        lax.psum_scatter(
            totals[15].astype(jnp.bfloat16), "dp", scatter_dimension=0, tiled=True
        ).astype(jnp.float32),
    )
    gain_totals = lax.psum((reduced[12], reduced[13], reduced[14], reduced[15]), "tensor")
    return (
        jnp.stack(outputs, axis=0),
        jnp.stack(input_grads, axis=0),
        gain_totals[0],
        gain_totals[1],
        gain_totals[2],
        gain_totals[3],
        reduced[0],
        reduced[1],
        reduced[2],
        reduced[9],
        reduced[3],
        reduced[4],
        reduced[5],
        reduced[10],
        reduced[6],
        reduced[7],
        reduced[11],
        reduced[8],
    )


def solution(mesh):
    return jax.shard_map(
        body,
        mesh=mesh,
        in_specs=(
            P(None, "dp", None, "tensor", None),
            P(None, "dp", None),
            P(None, "dp", None, "tensor", None),
            P("dp"),
            P("dp"),
            P("dp"),
            P("dp"),
            P("dp", "tensor"),
            P("dp", "tensor"),
            P("dp", "tensor"),
            P("tensor", "dp"),
            P("dp", "tensor"),
            P("dp", "tensor"),
            P("dp", "tensor"),
            P("tensor", "dp"),
            P("dp", "tensor"),
            P("dp", "tensor"),
            P("tensor", "dp"),
            P("dp", "tensor"),
        ),
        out_specs=(
            P(None, "dp", None, "tensor", None),
            P(None, "dp", None, "tensor", None),
            P("dp"),
            P("dp"),
            P("dp"),
            P("dp"),
            P("dp", "tensor"),
            P("dp", "tensor"),
            P("dp", "tensor"),
            P("tensor", "dp"),
            P("dp", "tensor"),
            P("dp", "tensor"),
            P("dp", "tensor"),
            P("tensor", "dp"),
            P("dp", "tensor"),
            P("dp", "tensor"),
            P("tensor", "dp"),
            P("dp", "tensor"),
        ),
        check_vma=False,
    )
```

profile of v0, /device:TPU:0, one launch (start us, length us, event | category | flops | bytes accessed | tf_op | source)
XLA Modules:
  0.0 3409.9 jit_solution(1056702553702722839)
XLA Ops:
  7.2 24.8 all_gather.201
  42.5 30.6 all-reduce.16
  92.9 40.1 %all-gather.62.cloned.1.call-done = bf16[1024,512]{1,0:T(8,128)(2,1)} async-done(((bf16[64,512]{1,0:T(8,128)(2,1)}), bf16[1024,512]{1,0:T(8,128)(2,1)}) %all-gather.62.cloned.1.call-update) | async-done | bytes 1048592 | tf_op jit(solution)/shard_map/all_gather | solution.py:161
  155.4 40.0 %all-gather.60.cloned.1.call-done = bf16[1024,512]{1,0:T(8,128)(2,1)} async-done(((bf16[64,512]{1,0:T(8,128)(2,1)}), bf16[1024,512]{1,0:T(8,128)(2,1)}) %all-gather.60.cloned.1.call-update) | async-done | bytes 1048592 | tf_op jit(solution)/shard_map/all_gather | solution.py:158
  220.6 37.0 %all-gather.70.cloned.1.call-done = bf16[1024,512]{1,0:T(8,128)(2,1)} async-done(((bf16[64,512]{1,0:T(8,128)(2,1)}), bf16[1024,512]{1,0:T(8,128)(2,1)}) %all-gather.70.cloned.1.call-update) | async-done | bytes 1048592 | tf_op jit(solution)/shard_map/all_gather | solution.py:160
  265.7 31.0 all-gather.56.cloned.1.call-done
  299.4 36.3 %all-gather.54.cloned.1.call-done = bf16[1024,512]{1,0:T(8,128)(2,1)} async-done(((bf16[64,512]{1,0:T(8,128)(2,1)}), bf16[1024,512]{1,0:T(8,128)(2,1)}) %all-gather.54.cloned.1.call-update) | async-done | bytes 1048592 | tf_op jit(solution)/shard_map/all_gather | solution.py:159
  344.9 29.9 all-gather.72.cloned.1.call-done
  390.9 22.8 all-gather.68.cloned.1.call-done
  435.8 23.1 reduce-scatter.67.cloned.1.call-done
  944.9 23.3 reduce-scatter.61.cloned.1.call-done
  1076.5 47.3 %all-gather.84.cloned.1.call-done = bf16[1,4,512,1024]{3,2,1,0:T(8,128)(2,1)} async-done(((bf16[1,4,256,1024]{3,2,1,0:T(8,128)(2,1)}), bf16[1,4,512,1024]{3,2,1,0:T(8,128)(2,1)}) %all-gather.84.cloned.1.call-update) | async-done | bytes 4194320 | tf_op jit(solution)/shard_map/all_gather | solution.py:303
  1139.0 37.5 %all-gather.88.cloned.1.call-done = bf16[2048,1024]{0,1:T(8,128)(2,1)} async-done(((bf16[2048,64]{0,1:T(8,128)(2,1)}), bf16[2048,1024]{0,1:T(8,128)(2,1)}) %all-gather.88.cloned.1.call-update) | async-done | bytes 4194320 | tf_op jit(solution)/shard_map/all_gather | solution.py:168
  1193.0 40.2 %all-gather.136.cloned.1.call-done = bf16[1,1,4,512,1024]{4,3,2,1,0:T(8,128)(2,1)} async-done(((bf16[1,1,4,256,1024]{4,3,2,1,0:T(8,128)(2,1)}), bf16[1,1,4,512,1024]{4,3,2,1,0:T(8,128)(2,1)}) %all-gather.136.cloned.1.call-update) | async-done | bytes 4194320 | tf_op jit(solution)/shard_map/all_gather | solution.py:345
  1233.2 22.7 fusion.6
  1278.4 22.6 reduce-scatter.73.cloned.1.call-done
  1301.0 22.7 reduce-scatter.77.cloned.1.call-done
  1327.7 53.0 %reduce-scatter.63.cloned.1.call-done = bf16[1,4,256,1024]{3,2,1,0:T(8,128)(2,1)} async-done(((bf16[1,4,512,1024]{3,2,1,0:T(8,128)(2,1)}), bf16[1,4,256,1024]{3,2,1,0:T(8,128)(2,1)}) %reduce-scatter.63.cloned.1.call-update) | async-done | bytes 2097168 | tf_op jit(solution)/shard_map/reduce_scatter | solution.py:307
  1380.7 57.3 %reduce-scatter.81.cloned.1.call-done = bf16[1,4,256,1024]{3,2,1,0:T(8,128)(2,1)} async-done(((bf16[1,4,512,1024]{3,2,1,0:T(8,128)(2,1)}), bf16[1,4,256,1024]{3,2,1,0:T(8,128)(2,1)}) %reduce-scatter.81.cloned.1.call-update) | async-done | bytes 2097168 | tf_op jit(solution)/shard_map/reduce_scatter | solution.py:349
  1451.9 49.9 %all-gather.104.cloned.1.call-done = bf16[1,4,512,1024]{3,2,1,0:T(8,128)(2,1)} async-done(((bf16[1,4,256,1024]{3,2,1,0:T(8,128)(2,1)}), bf16[1,4,512,1024]{3,2,1,0:T(8,128)(2,1)}) %all-gather.104.cloned.1.call-update) | async-done | bytes 4194320 | tf_op jit(solution)/shard_map/all_gather | solution.py:303
  1517.0 43.0 %all-gather.140.cloned.1.call-done = bf16[1,1,4,512,1024]{4,3,2,1,0:T(8,128)(2,1)} async-done(((bf16[1,1,4,256,1024]{4,3,2,1,0:T(8,128)(2,1)}), bf16[1,1,4,512,1024]{4,3,2,1,0:T(8,128)(2,1)}) %all-gather.140.cloned.1.call-update) | async-done | bytes 4194320 | tf_op jit(solution)/shard_map/all_gather | solution.py:345
  1559.9 26.2 fusion.13
  1687.2 32.6 reduce-scatter.79.cloned.1.call-done
  2269.1 23.3 reduce-scatter.89.cloned.1.call-done
  2777.9 58.5 %reduce-scatter.133.cloned.1.call-done = bf16[64,512]{1,0:T(8,128)(2,1)} async-done(((bf16[1024,512]{1,0:T(8,128)(2,1)}), bf16[64,512]{1,0:T(8,128)(2,1)}) %reduce-scatter.133.cloned.1.call-update) | async-done | bytes 65552 | tf_op jit(solution)/shard_map/reduce_scatter | solution.py:556
  2838.0 59.1 %reduce-scatter.125.cloned.1.call-done = bf16[64,512]{1,0:T(8,128)(2,1)} async-done(((bf16[1024,512]{1,0:T(8,128)(2,1)}), bf16[64,512]{1,0:T(8,128)(2,1)}) %reduce-scatter.125.cloned.1.call-update) | async-done | bytes 65552 | tf_op jit(solution)/shard_map/reduce_scatter | solution.py:547
  2898.6 58.6 %reduce-scatter.129.cloned.1.call-done = bf16[64,512]{1,0:T(8,128)(2,1)} async-done(((bf16[1024,512]{1,0:T(8,128)(2,1)}), bf16[64,512]{1,0:T(8,128)(2,1)}) %reduce-scatter.129.cloned.1.call-update) | async-done | bytes 65552 | tf_op jit(solution)/shard_map/reduce_scatter | solution.py:550
  2958.6 58.9 %reduce-scatter.123.cloned.1.call-done = bf16[64,512]{1,0:T(8,128)(2,1)} async-done(((bf16[1024,512]{1,0:T(8,128)(2,1)}), bf16[64,512]{1,0:T(8,128)(2,1)}) %reduce-scatter.123.cloned.1.call-update) | async-done | bytes 65552 | tf_op jit(solution)/shard_map/reduce_scatter | solution.py:544
  3019.0 58.5 %reduce-scatter.131.cloned.1.call-done = bf16[64,512]{1,0:T(8,128)(2,1)} async-done(((bf16[1024,512]{1,0:T(8,128)(2,1)}), bf16[64,512]{1,0:T(8,128)(2,1)}) %reduce-scatter.131.cloned.1.call-update) | async-done | bytes 65552 | tf_op jit(solution)/shard_map/reduce_scatter | solution.py:553
  3099.1 22.6 reduce-scatter.117.cloned.1.call-done
  3306.1 33.7 all-reduce.15
  3359.6 41.8 %reduce-scatter.143.cloned.1.call-done = bf16[32,512]{1,0:T(8,128)(2,1)} async-done(((bf16[512,512]{1,0:T(8,128)(2,1)}), bf16[32,512]{1,0:T(8,128)(2,1)}) %reduce-scatter.143.cloned.1.call-update) | async-done | bytes 32784 | tf_op jit(solution)/shard_map/reduce_scatter | solution.py:565
  (2181 shorter events, 2176.4 us)
Async XLA Ops:
  84.7 251.0 %all-gather.54.cloned.1.call-start = ((), (), s32[]{:S(2)}) async-start(), calls=%async_computation.49 | async-start | bytes 1114112 | tf_op jit(solution)/shard_map/all_gather | solution.py:159
  85.5 289.3 %all-gather.72.cloned.1.call-start = ((), (), s32[]{:S(2)}) async-start(), calls=%async_computation.59 | async-start | bytes 1114112 | tf_op jit(solution)/shard_map/all_gather | solution.py:167
  86.2 327.5 %all-gather.68.cloned.1.call-start = ((), (), s32[]{:S(2)}) async-start(), calls=%async_computation.57 | async-start | bytes 1114112 | tf_op jit(solution)/shard_map/all_gather | solution.py:163
  86.8 349.0 %reduce-scatter.51.cloned.1.call-start = ((), (), s32[]{:S(2)}) async-start(), calls=%async_computation.60 | async-start | bytes 1572864 | tf_op jit(solution)/shard_map/reduce_scatter | solution.py:264
  975.4 257.9 %all-gather.136.cloned.1.call-start = ((), (), s32[]{:S(2)}) async-start(), calls=%async_computation.138 | async-start | bytes 6291456 | tf_op jit(solution)/shard_map/all_gather | solution.py:345
  980.4 289.6 %reduce-scatter.65.cloned.1.call-start = ((), (), s32[]{:S(2)}) async-start(), calls=%async_computation.76 | async-start | bytes 1572864 | tf_op jit(solution)/shard_map/reduce_scatter | solution.py:261
  1016.0 262.4 %reduce-scatter.69.cloned.1.call-start = ((), (), s32[]{:S(2)}) async-start(), calls=%async_computation.80 | async-start | bytes 1572864 | tf_op jit(solution)/shard_map/reduce_scatter | solution.py:261
  1040.5 260.5 %reduce-scatter.73.cloned.1.call-start = ((), (), s32[]{:S(2)}) async-start(), calls=%async_computation.84 | async-start | bytes 1572864 | tf_op jit(solution)/shard_map/reduce_scatter | solution.py:261
  1056.8 266.9 %reduce-scatter.77.cloned.1.call-start = ((), (), s32[]{:S(2)}) async-start(), calls=%async_computation.88 | async-start | bytes 1572864 | tf_op jit(solution)/shard_map/reduce_scatter | solution.py:261
  1076.2 304.5 %reduce-scatter.63.cloned.1.call-start = ((), (), s32[]{:S(2)}) async-start(), calls=%async_computation.74 | async-start | bytes 6291456 | tf_op jit(solution)/shard_map/reduce_scatter | solution.py:307
  2263.7 322.5 %all-gather.132.cloned.1.call-start = ((), (), s32[]{:S(2)}) async-start(), calls=%async_computation.118 | async-start | bytes 1572864 | tf_op jit(solution)/shard_map/all_gather | solution.py:402
  2306.9 288.8 %all-gather.118.cloned.1.call-start = ((), (), s32[]{:S(2)}) async-start(), calls=%async_computation.102 | async-start | bytes 1572864 | tf_op jit(solution)/shard_map/all_gather | solution.py:402
  2323.2 424.6 %reduce-scatter.141.cloned.1.call-start = ((), (), s32[]{:S(2)}) async-start(), calls=%async_computation.135 | async-start | bytes 4456448 | tf_op jit(solution)/shard_map/reduce_scatter | solution.py:574
  2340.8 408.8 %reduce-scatter.139.cloned.1.call-start = ((), (), s32[]{:S(2)}) async-start(), calls=%async_computation.134 | async-start | bytes 4456448 | tf_op jit(solution)/shard_map/reduce_scatter | solution.py:562
  2378.6 382.4 %reduce-scatter.127.cloned.1.call-start = ((), (), s32[]{:S(2)}) async-start(), calls=%async_computation.128 | async-start | bytes 1114112 | tf_op jit(solution)/shard_map/reduce_scatter | solution.py:568
  2483.3 279.2 %reduce-scatter.121.cloned.1.call-start = ((), (), s32[]{:S(2)}) async-start(), calls=%async_computation.125 | async-start | bytes 1114112 | tf_op jit(solution)/shard_map/reduce_scatter | solution.py:541
  2513.8 250.4 %reduce-scatter.137.cloned.1.call-start = ((), (), s32[]{:S(2)}) async-start(), calls=%async_computation.133 | async-start | bytes 1114112 | tf_op jit(solution)/shard_map/reduce_scatter | solution.py:559
  2640.7 256.4 %reduce-scatter.125.cloned.1.call-start = ((), (), s32[]{:S(2)}) async-start(), calls=%async_computation.127 | async-start | bytes 1114112 | tf_op jit(solution)/shard_map/reduce_scatter | solution.py:547
  2655.1 302.0 %reduce-scatter.129.cloned.1.call-start = ((), (), s32[]{:S(2)}) async-start(), calls=%async_computation.129 | async-start | bytes 1114112 | tf_op jit(solution)/shard_map/reduce_scatter | solution.py:550
  2673.9 343.6 %reduce-scatter.123.cloned.1.call-start = ((), (), s32[]{:S(2)}) async-start(), calls=%async_computation.126 | async-start | bytes 1114112 | tf_op jit(solution)/shard_map/reduce_scatter | solution.py:544
  2687.1 390.4 %reduce-scatter.131.cloned.1.call-start = ((), (), s32[]{:S(2)}) async-start(), calls=%async_computation.130 | async-start | bytes 1114112 | tf_op jit(solution)/shard_map/reduce_scatter | solution.py:553
  2694.7 404.3 %reduce-scatter.119.cloned.1.call-start = ((), (), s32[]{:S(2)}) async-start(), calls=%async_computation.124 | async-start | bytes 1572864 | tf_op jit(solution)/shard_map/reduce_scatter | solution.py:496
  2701.3 420.4 %reduce-scatter.117.cloned.1.call-start = ((), (), s32[]{:S(2)}) async-start(), calls=%async_computation.123 | async-start | bytes 1572864 | tf_op jit(solution)/shard_map/reduce_scatter | solution.py:496
  2707.8 436.5 %reduce-scatter.115.cloned.1.call-start = ((), (), s32[]{:S(2)}) async-start(), calls=%async_computation.122 | async-start | bytes 1572864 | tf_op jit(solution)/shard_map/reduce_scatter | solution.py:493
  2713.4 453.2 %reduce-scatter.113.cloned.1.call-start = ((), (), s32[]{:S(2)}) async-start(), calls=%async_computation.121 | async-start | bytes 1572864 | tf_op jit(solution)/shard_map/reduce_scatter | solution.py:493
  2719.1 470.1 %reduce-scatter.111.cloned.1.call-start = ((), (), s32[]{:S(2)}) async-start(), calls=%async_computation.120 | async-start | bytes 1572864 | tf_op jit(solution)/shard_map/reduce_scatter | solution.py:493
  2724.6 487.1 %reduce-scatter.109.cloned.1.call-start = ((), (), s32[]{:S(2)}) async-start(), calls=%async_computation.119 | async-start | bytes 1572864 | tf_op jit(solution)/shard_map/reduce_scatter | solution.py:493
  2730.1 504.4 %reduce-scatter.97.cloned.1.call-start = ((), (), s32[]{:S(2)}) async-start(), calls=%async_computation.106 | async-start | bytes 1572864 | tf_op jit(solution)/shard_map/reduce_scatter | solution.py:493
  2735.6 521.4 %reduce-scatter.95.cloned.1.call-start = ((), (), s32[]{:S(2)}) async-start(), calls=%async_computation.105 | async-start | bytes 1572864 | tf_op jit(solution)/shard_map/reduce_scatter | solution.py:493
  2741.2 538.5 %reduce-scatter.93.cloned.1.call-start = ((), (), s32[]{:S(2)}) async-start(), calls=%async_computation.104 | async-start | bytes 1572864 | tf_op jit(solution)/shard_map/reduce_scatter | solution.py:493
  2747.1 555.0 %reduce-scatter.91.cloned.1.call-start = ((), (), s32[]{:S(2)}) async-start(), calls=%async_computation.103 | async-start | bytes 1572864 | tf_op jit(solution)/shard_map/reduce_scatter | solution.py:493
  2755.8 645.6 %reduce-scatter.143.cloned.1.call-start = ((), (), s32[]{:S(2)}) async-start(), calls=%async_computation.136 | async-start | bytes 557056 | tf_op jit(solution)/shard_map/reduce_scatter | solution.py:565
  (731 other events, 25951.8 us)
Sparse Core Ops, SparseCore 0:
  95.1 37.9 all-gather.61
  157.4 37.9 all-gather.59
  219.6 37.9 all-gather.69
  259.8 36.8 all-gather.55
  298.8 36.8 all-gather.53
  337.9 36.8 all-gather.71
  376.8 36.8 all-gather.67
  707.7 37.9 all-gather.57
  816.2 37.9 all-gather.63
  1016.0 50.5 all-gather.85
  1068.5 55.2 all-gather.83
  1125.8 50.5 all-gather.87
  1178.0 55.2 all-gather.135
  1326.4 54.2 reduce-scatter.62
  1383.7 54.3 reduce-scatter.80
  1445.0 56.7 all-gather.103
  1503.2 56.7 all-gather.139
  1608.1 54.2 reduce-scatter.98
  1665.4 54.3 reduce-scatter.78
  2013.9 21.5 all-gather.109
  2387.3 72.3 reduce-scatter.140
  2463.9 71.4 reduce-scatter.138
  2539.0 56.3 reduce-scatter.126
  2599.4 56.4 reduce-scatter.120
  2659.5 56.3 reduce-scatter.136
  2720.0 56.4 reduce-scatter.134
  2780.1 56.3 reduce-scatter.132
  2840.5 56.4 reduce-scatter.124
  2900.7 56.3 reduce-scatter.128
  2961.0 56.4 reduce-scatter.122
  3021.1 56.3 reduce-scatter.130
  3349.4 52.0 reduce-scatter.142
  (62 shorter events, 1276.7 us)
where the time goes:
time: 3420 us; the launch traced here: 3410 us
  waiting for transfers between devices  1630 us (48%)
  matrix products  1120 us (33%)
  other arithmetic  337 us (10%)
  local copies, waits for them, and re-layouts  153 us (4%)
  blocking collectives  129 us (4%)
    dot_general x72, matrix products, matmul(): return jnp.dot(left, right, preferred_element_type=jnp.float32)  225 us
    reduce_scatter x8, waiting for transfers between devices, body(): lax.psum_scatter(row_part.astype(jnp.bfloat16), 'tensor', scatter_dimensi...  174 us
    dot_general x16, matrix products, attend_back(): jnp.einsum('brhe,bkhe->bhrk', grad_heads, split_heads(values), preferred_...  156 us
    dot_general x16, matrix products, attend_back(): jnp.einsum('bhrk,brhe->bkhe', weights.astype(jnp.bfloat16), grad_heads, p...  121 us
    convert_element_type x16, other arithmetic, attend_back(): grad_scores = (weights * (grad_weights - jnp.sum(weights * grad_weights,...  115 us
    all_gather x8, waiting for transfers between devices, body(): lax.all_gather(normed, 'tensor', axis=1, tiled=True)  109 us
    reduce_scatter x8, waiting for transfers between devices, body(): lax.psum_scatter(forward_state_part.astype(jnp.bfloat16), 'tensor', scatt...  102 us
    all_gather x2, waiting for transfers between devices, body(): forward_full_mlp_in = lax.all_gather(mlp_in, 'tensor', axis=2, tiled=True)  97.2 us
  transfers between devices with their start and end apart: 94, of which 66 were waited for; matrix products, arithmetic and copies ran while one was open for 41% of the time, Pallas kernels for 0%

commit v1 on v0

--- a/solution.py
+++ b/solution.py
@@ -3,6 +3,8 @@
 import jax
 import jax.numpy as jnp
 from jax import lax
+from jax.experimental import pallas as pl
+from jax.experimental.pallas import tpu as pltpu
 from jax.sharding import PartitionSpec as P
 
 D = 1024
@@ -128,7 +130,7 @@
     )
 
 
-def body(
+def generic_body(
     tokens_in,
     piece_starts,
     cotangent,
@@ -610,9 +612,935 @@
     )
 
 
+BF = jnp.bfloat16
+F32 = jnp.float32
+HALF = 256
+VMEM_BYTES = 60 * 1024 * 1024
+EXP2_SCALE = math.log2(math.e) / math.sqrt(HEAD)
+SCORE_SCALE = 1.0 / math.sqrt(HEAD)
+
+
+def nn(left, right):
+    return lax.dot_general(left, right, (((1,), (0,)), ((), ())), preferred_element_type=F32)
+
+
+def nt(left, right):
+    return lax.dot_general(left, right, (((1,), (1,)), ((), ())), preferred_element_type=F32)
+
+
+def tn(left, right):
+    return lax.dot_general(left, right, (((0,), (0,)), ((), ())), preferred_element_type=F32)
+
+
+def inverse_rms(values):
+    return lax.rsqrt(jnp.mean(values * values, axis=-1, keepdims=True) + epsilon)
+
+
+def rms_back(scaled, inverse, grad):
+    return (grad - scaled * jnp.mean(grad * scaled, axis=-1, keepdims=True)) * inverse
+
+
+def params(semantics=("arbitrary",)):
+    return pltpu.CompilerParams(dimension_semantics=semantics, vmem_limit_bytes=VMEM_BYTES)
+
+
+def cost(flops, moved, transcendentals=0):
+    return pl.CostEstimate(
+        flops=int(flops), bytes_accessed=int(moved), transcendentals=int(transcendentals)
+    )
+
+
+def once(shape, index):
+    return pl.BlockSpec(shape, index, pipeline_mode=pl.Buffered(1))
+
+
+def project_kernel(rows, gain, w0, w1, normed, query, key, value):
+    width = w0.shape[1] // 3
+    wide = rows[...].astype(F32)
+    normed[...] = (wide * inverse_rms(wide) * gain[...]).astype(BF)
+    for half, weight in enumerate((w0, w1)):
+        for which, out in enumerate((query, key, value)):
+            out[:, half * width : (half + 1) * width] = nn(
+                normed[...], weight[:, which * width : (which + 1) * width]
+            ).astype(BF)
+
+
+def project(rows, gain, weights):
+    tokens = rows.shape[0]
+    width = weights.shape[1]
+    out = jax.ShapeDtypeStruct((tokens, D), BF)
+    block = pl.BlockSpec((W, D), lambda b: (b, 0))
+    return pl.pallas_call(
+        project_kernel,
+        grid=(tokens // W,),
+        in_specs=[
+            block,
+            once((1, D), lambda b: (0, 0)),
+            once((D, width), lambda b: (0, 0)),
+            once((D, width), lambda b: (1, 0)),
+        ],
+        out_specs=[block] * 4,
+        out_shape=[out] * 4,
+        compiler_params=params(),
+        cost_estimate=cost(2 * tokens * D * 3 * D, 2 * (5 * tokens * D + 3 * D * D)),
+        name="project",
+    )(rows, gain, weights, weights)
+
+
+def softmax_parts(parts):
+    top = parts[0][0].max(axis=1, keepdims=True)
+    for scores, unused in parts[1:]:
+        top = jnp.maximum(top, scores.max(axis=1, keepdims=True))
+    total = None
+    mixed = None
+    for scores, values in parts:
+        weights = jnp.exp2((scores - top) * EXP2_SCALE)
+        part_total = weights.sum(axis=1, keepdims=True)
+        part_mixed = nn(weights.astype(BF), values)
+        total = part_total if total is None else total + part_total
+        mixed = part_mixed if mixed is None else mixed + part_mixed
+    return (mixed / total).astype(BF), top * EXP2_SCALE + jnp.log2(total)
+
+
+def allowed_in_half(flag):
+    row = lax.broadcasted_iota(jnp.int32, (HALF, HALF), 0)
+    column = lax.broadcasted_iota(jnp.int32, (HALF, HALF), 1)
+    return row, column
+
+
+def forward_kernel(
+    flags,
+    query,
+    key,
+    value,
+    key_before,
+    value_before,
+    init,
+    gain,
+    bias,
+    wst0,
+    wst1,
+    wso0,
+    wso1,
+    token_mixed,
+    state_mixed,
+    state_normed,
+    state_query,
+    state_key,
+    state_value,
+    state_in,
+    forget,
+    apart,
+    totals,
+    state,
+    token_totals,
+    state_totals,
+):
+    block = pl.program_id(0)
+    width = wso0.shape[1]
+
+    @pl.when(block == 0)
+    def start():
+        state[...] = init[...].astype(F32)
+
+    now = state[...]
+    state_in[...] = now
+    state_normed[...] = (now * inverse_rms(now) * gain[...]).astype(BF)
+    for half, weight in enumerate((wst0, wst1)):
+        columns = slice(half * width, (half + 1) * width)
+        for which, out in enumerate((state_query, state_key, state_value)):
+            out[:, columns] = nn(
+                state_normed[...], weight[:, which * width : (which + 1) * width]
+            ).astype(BF)
+        gate = nn(state_normed[...], weight[:, 3 * width :]) + bias[:, columns]
+        forget[:, columns] = jax.nn.sigmoid(gate)
+
+    def heads(with_before):
+        def head(index, carry):
+            columns = pl.ds(pl.multiple_of(index * HEAD, HEAD), HEAD)
+            lane = lax.broadcasted_iota(jnp.int32, (HALF, HEAD), 1) == index
+            for half in range(2):
+                rows = slice(half * HALF, (half + 1) * HALF)
+                own = query[rows, columns]
+                parts = []
+                if with_before:
+                    parts.append((nt(own, key_before[:, columns]), value_before[:, columns]))
+                if half == 1:
+                    parts.append((nt(own, key[:HALF, columns]), value[:HALF, columns]))
+                row = lax.broadcasted_iota(jnp.int32, (HALF, HALF), 0)
+                column = lax.broadcasted_iota(jnp.int32, (HALF, HALF), 1)
+                reach = row + flags[2 * block + half] * HALF
+                near = jnp.where(column <= reach, nt(own, key[rows, columns]), masked_score)
+                parts.append((near, value[rows, columns]))
+                parts.append((nt(own, state_key[:, columns]), state_value[:, columns]))
+                mixed, total = softmax_parts(parts)
+                token_mixed[rows, columns] = mixed
+                token_totals[rows, :] = jnp.where(lane, total, token_totals[rows, :])
+                own = state_query[rows, columns]
+                mixed, total = softmax_parts(
+                    [
+                        (nt(own, key[:, columns]), value[:, columns]),
+                        (nt(own, state_key[:, columns]), state_value[:, columns]),
+                    ]
+                )
+                state_mixed[rows, columns] = mixed
+                state_totals[rows, :] = jnp.where(lane, total, state_totals[rows, :])
+            return carry
+
+        lax.fori_loop(0, D // HEAD, head, 0)
+
+    @pl.when(block == 0)
+    def first():
+        heads(False)
+
+    @pl.when(block > 0)
+    def later():
+        heads(True)
+
+    count = D // HEAD
+    totals[0, :count, :] = token_totals[...].T[:count]
+    totals[0, count:, :] = state_totals[...].T[:count]
+    new = nt(state_mixed[:, :width], wso0[...]) + nt(state_mixed[:, width:], wso1[...])
+    apart[...] = (now - new).astype(BF)
+    state[...] = new + forget[...] * (now - new)
+
+
+def forward(flags, query, key, value, init, gain, bias, weights, out_weights):
+    blocks = query.shape[0] // W
+    heads = D // HEAD
+    width = weights.shape[1]
+    own = pl.BlockSpec((W, D), lambda b, s: (b, 0))
+    before = pl.BlockSpec((W, D), lambda b, s: (jnp.maximum(b - 1, 0), 0))
+    low = jax.ShapeDtypeStruct((blocks * W, D), BF)
+    wide = jax.ShapeDtypeStruct((blocks * W, D), F32)
+    return pl.pallas_call(
+        forward_kernel,
+        grid_spec=pltpu.PrefetchScalarGridSpec(
+            num_scalar_prefetch=1,
+            grid=(blocks,),
+            in_specs=[
+                own,
+                own,
+                own,
+                before,
+                before,
+                once((S, D), lambda b, s: (0, 0)),
+                once((1, D), lambda b, s: (0, 0)),
+                once((1, D), lambda b, s: (0, 0)),
+                once((D, width), lambda b, s: (0, 0)),
+                once((D, width), lambda b, s: (1, 0)),
+                once((D, width // 4), lambda b, s: (0, 0)),
+                once((D, width // 4), lambda b, s: (1, 0)),
+            ],
+            out_specs=[own] * 9 + [pl.BlockSpec((1, 2 * heads, W), lambda b, s: (b, 0, 0))],
+            scratch_shapes=[
+                pltpu.VMEM((S, D), F32),
+                pltpu.VMEM((W, HEAD), F32),
+                pltpu.VMEM((S, HEAD), F32),
+            ],
+        ),
+        out_shape=[low] * 6 + [wide, wide, low, jax.ShapeDtypeStruct((blocks, 2 * heads, W), F32)],
+        compiler_params=params(),
+        cost_estimate=cost(42e9, 100e6, 40e6),
+        name="forward",
+    )(
+        flags,
+        query,
+        key,
+        value,
+        key,
+        value,
+        init,
+        gain,
+        bias,
+        weights,
+        weights,
+        out_weights,
+        out_weights,
+    )
+
+
+def middle_kernel(rows, mixed, w0, w1, gain, cotangent, middle, mlp_in, mlp_turned, cot_turned):
+    width = w0.shape[1]
+    here = (
+        rows[...].astype(F32) + nt(mixed[:, :width], w0[...]) + nt(mixed[:, width:], w1[...])
+    )
+    middle[...] = here
+    low = (here * inverse_rms(here) * gain[...]).astype(BF)
+    mlp_in[...] = low
+    mlp_turned[...] = low.T
+    cot_turned[...] = cotangent[...].T
+
+
+def middle_rows(rows, mixed, weights, gain, cotangent):
+    tokens = rows.shape[0]
+    width = weights.shape[1]
+    block = pl.BlockSpec((W, D), lambda b: (b, 0))
+    turned = pl.BlockSpec((D, W), lambda b: (0, b))
+    low = jax.ShapeDtypeStruct((tokens, D), BF)
+    return pl.pallas_call(
+        middle_kernel,
+        grid=(tokens // W,),
+        in_specs=[
+            block,
+            block,
+            once((D, width), lambda b: (0, 0)),
+            once((D, width), lambda b: (1, 0)),
+            once((1, D), lambda b: (0, 0)),
+            block,
+        ],
+        out_specs=[block, block, turned, turned],
+        out_shape=[
+            jax.ShapeDtypeStruct((tokens, D), F32),
+            low,
+            jax.ShapeDtypeStruct((D, tokens), BF),
+            jax.ShapeDtypeStruct((D, tokens), BF),
+        ],
+        compiler_params=params(),
+        cost_estimate=cost(2 * tokens * D * D, 2 * 8 * tokens * D),
+        name="middle",
+    )(rows, mixed, weights, weights, gain, cotangent)
+
+
+def mlp_kernel(
+    mlp_in, mlp_turned, cot, cot_turned, weights, out, grad_in, grads, out_sum, grad_sum, act, gh
+):
+    step = pl.program_id(0)
+    units = weights.shape[1] // 2
+    tokens = mlp_in.shape[0]
+
+    @pl.when(step == 0)
+    def start():
+        out_sum[...] = jnp.zeros_like(out_sum)
+        grad_sum[...] = jnp.zeros_like(grad_sum)
+
+    slope = math.sqrt(2.0 / math.pi)
+
+    def chunk(index, carry):
+        rows = pl.ds(pl.multiple_of(index * W, W), W)
+        hidden = nn(mlp_in[rows, :], weights[:, :units])
+        back = nn(cot[rows, :], weights[:, units:])
+        square = hidden * hidden
+        bent = jnp.tanh(slope * hidden * (1.0 + 0.044715 * square))
+        open_part = 0.5 * (1.0 + bent)
+        active = (hidden * open_part).astype(BF)
+        steep = open_part + (0.5 * slope) * hidden * (1.0 - bent * bent) * (
+            1.0 + (3 * 0.044715) * square
+        )
+        grad = (steep * back).astype(BF)
+        act[rows, :] = active
+        gh[rows, :] = grad
+        out_sum[rows, :] += nt(active, weights[:, units:])
+        grad_sum[rows, :] += nt(grad, weights[:, :units])
+        return carry
+
+    lax.fori_loop(0, tokens // W, chunk, 0)
+    grads[:, :units] = nn(mlp_turned[...], gh[...]).astype(BF)
+    grads[:, units:] = nn(cot_turned[...], act[...]).astype(BF)
+
+    @pl.when(step == pl.num_programs(0) - 1)
+    def end():
+        out[...] = out_sum[...].astype(BF)
+        grad_in[...] = grad_sum[...].astype(BF)
+
+
+def mlp(mlp_in, mlp_turned, cot, cot_turned, weights):
+    tokens = mlp_in.shape[0]
+    units = 512
+    across = weights.shape[1] // (2 * units)
+    low = jax.ShapeDtypeStruct((tokens, D), BF)
+    rows = once((tokens, D), lambda f: (0, 0))
+    turned = once((D, tokens), lambda f: (0, 0))
+    tile = pl.BlockSpec((D, 2 * units), lambda f: (f // across, f % across))
+    return pl.pallas_call(
+        mlp_kernel,
+        grid=(2 * across,),
+        in_specs=[rows, turned, rows, turned, tile],
+        out_specs=[rows, rows, tile],
+        out_shape=[low, low, jax.ShapeDtypeStruct(weights.shape, BF)],
+        scratch_shapes=[
+            pltpu.VMEM((tokens, D), F32),
+            pltpu.VMEM((tokens, D), F32),
+            pltpu.VMEM((tokens, units), BF),
+            pltpu.VMEM((tokens, units), BF),
+        ],
+        compiler_params=params(),
+        cost_estimate=cost(103e9, 60e6, 8e6),
+        name="mlp",
+    )(mlp_in, mlp_turned, cot, cot_turned, weights)
+
+
+def after_mlp_kernel(
+    middle, mlp_out, grad_in, cot, gain, w0, w1, output, grad_middle, grad_mixed, grad_gain
+):
+    width = w0.shape[1]
+    here = middle[...]
+    inverse = inverse_rms(here)
+    scaled = here * inverse
+    grad = grad_in[...].astype(F32)
+    output[...] = (here + mlp_out[...].astype(F32)).astype(BF)
+    low = (cot[...].astype(F32) + rms_back(scaled, inverse, gain[...] * grad)).astype(BF)
+    grad_middle[...] = low
+    grad_mixed[:, :width] = nn(low, w0[...]).astype(BF)
+    grad_mixed[:, width:] = nn(low, w1[...]).astype(BF)
+    part = jnp.sum(grad * scaled, axis=0, keepdims=True)
+
+    @pl.when(pl.program_id(0) == 0)
+    def first():
+        grad_gain[...] = part
+
+    @pl.when(pl.program_id(0) > 0)
+    def later():
+        grad_gain[...] += part
+
+
+def after_mlp(middle, mlp_out, grad_in, cot, gain, weights):
+    tokens = middle.shape[0]
+    width = weights.shape[1]
+    block = pl.BlockSpec((W, D), lambda b: (b, 0))
+    low = jax.ShapeDtypeStruct((tokens, D), BF)
+    return pl.pallas_call(
+        after_mlp_kernel,
+        grid=(tokens // W,),
+        in_specs=[
+            block,
+            block,
+            block,
+            block,
+            once((1, D), lambda b: (0, 0)),
+            once((D, width), lambda b: (0, 0)),
+            once((D, width), lambda b: (1, 0)),
+        ],
+        out_specs=[block, block, block, pl.BlockSpec((1, D), lambda b: (0, 0))],
+        out_shape=[low, low, low, jax.ShapeDtypeStruct((1, D), F32)],
+        compiler_params=params(),
+        cost_estimate=cost(2 * tokens * D * D, 2 * 8 * tokens * D),
+        name="after_mlp",
+    )(middle, mlp_out, grad_in, cot, gain, weights, weights)
+
+
+def backward_kernel(
+    flags,
+    query,
+    key,
+    value,
+    key_before,
+    value_before,
+    state_query,
+    state_key,
+    state_value,
+    token_mixed,
+    state_mixed,
+    grad_mixed,
+    totals,
+    forget,
+    state_in,
+    apart,
+    gain,
+    weight,
+    wso0,
+    wso1,
+    grad_tokens,
+    grad_states,
+    branch,
+    grad_init,
+    grad_gain,
+    grad_bias,
+    grad_state,
+    grad_state_mixed,
+    grad_normed,
+    gate_part,
+    carry_key,
+    carry_value,
+    grad_query_sum,
+    deltas,
+    queries,
+    grads_out,
+):
+    step = pl.program_id(0)
+    half = pl.program_id(1)
+    block = pl.num_programs(0) - 1 - step
+    width = wso0.shape[1]
+    local = width // HEAD
+    count = D // HEAD
+
+    @pl.when((step == 0) & (half == 0))
+    def start():
+        grad_state[...] = jnp.zeros_like(grad_state)
+        carry_key[...] = jnp.zeros_like(carry_key)
+        carry_value[...] = jnp.zeros_like(carry_value)
+        grad_gain[...] = jnp.zeros_like(grad_gain)
+        grad_bias[...] = jnp.zeros_like(grad_bias)
+
+    @pl.when(half == 0)
+    def begin():
+        coming = grad_state[...]
+        keep = forget[...]
+        low = ((1.0 - keep) * coming).astype(BF)
+        branch[...] = low
+        gate = (coming * apart[...].astype(F32) * keep * (1.0 - keep)).astype(BF)
+        gate_part[0] = gate[:, :width]
+        gate_part[1] = gate[:, width:]
+        grad_bias[...] += jnp.sum(gate.astype(F32), axis=0, keepdims=True)
+        grad_state_mixed[0] = nn(low, wso0[...]).astype(BF)
+        grad_state_mixed[1] = nn(low, wso1[...]).astype(BF)
+        grad_normed[...] = jnp.zeros_like(grad_normed)
+
+    grad_states[3] = gate_part[half]
+
+    def head(index, carry):
+        columns = pl.ds(pl.multiple_of(index * HEAD, HEAD), HEAD)
+        at = half * local + index
+        queries[:W] = query[:, columns]
+        queries[W:] = state_query[:, columns]
+        grads_out[:W] = grad_mixed[:, columns]
+        grads_out[W:] = grad_state_mixed[half, :, columns]
+        for first, mixed in ((0, token_mixed), (W, state_mixed)):
+            product = grads_out[first : first + W].astype(F32) * mixed[:, columns].astype(F32)
+            deltas[:, first : first + W] = jnp.sum(product.T, axis=0, keepdims=True)
+        token_total = totals[0, pl.ds(at, 1), :]
+        state_total = totals[0, pl.ds(count + at, 1), :]
+        total = jnp.concatenate([token_total, state_total], axis=1)
+
+        def chunk(keys, values, first, last, mask, fresh):
+            some = queries[first:last]
+            some_grads = grads_out[first:last]
+            scores = nt(keys, some)
+            if mask is not None:
+                size = mask.shape[1]
+                scores = jnp.concatenate(
+                    [jnp.where(mask, scores[:, :size], masked_score), scores[:, size:]], axis=1
+                )
+            weights = jnp.exp2(scores * EXP2_SCALE - total[:, first:last])
+            back = nt(values, some_grads) - deltas[:, first:last]
+            grad_scores = (weights * back).astype(BF)
+            grad_values = nn(weights.astype(BF), some_grads)
+            grad_keys = nn(grad_scores, some)
+            turned = tn(keys, grad_scores)
+            if fresh:
+                grad_query_sum[:, first:last] = turned
+            else:
+                grad_query_sum[:, first:last] += turned
+            return grad_keys * SCORE_SCALE, grad_values
+
+        for part in range(2):
+            rows = slice(part * HALF, (part + 1) * HALF)
+            grad_keys, grad_values = chunk(
+                state_key[rows, columns], state_value[rows, columns], 0, W + S, None, part == 0
+            )
+            grad_states[1, rows, columns] = grad_keys.astype(BF)
+            grad_states[2, rows, columns] = grad_values.astype(BF)
+        for part in range(2):
+            rows = slice(part * HALF, (part + 1) * HALF)
+            row = lax.broadcasted_iota(jnp.int32, (HALF, HALF), 0)
+            column = lax.broadcasted_iota(jnp.int32, (HALF, HALF), 1)
+            mask = row <= column + flags[2 * block + part] * HALF
+            grad_keys, grad_values = chunk(
+                key[rows, columns], value[rows, columns], part * HALF, W + S, mask, False
+            )
+            grad_tokens[1, rows, columns] = (grad_keys + carry_key[half, rows, columns]).astype(BF)
+            grad_tokens[2, rows, columns] = (
+                grad_values + carry_value[half, rows, columns]
+            ).astype(BF)
+
+        @pl.when(block > 0)
+        def before():
+            for part in range(2):
+                rows = slice(part * HALF, (part + 1) * HALF)
+                grad_keys, grad_values = chunk(
+                    key_before[rows, columns], value_before[rows, columns], 0, W, None, False
+                )
+                carry_key[half, rows, columns] = grad_keys
+                carry_value[half, rows, columns] = grad_values
+
+        grad_query = (grad_query_sum[...] * SCORE_SCALE).T
+        grad_tokens[0, :, columns] = grad_query[:W].astype(BF)
+        grad_states[0, :, columns] = grad_query[W:].astype(BF)
+        return carry
+
+    lax.fori_loop(0, local, head, 0)
+    for which in range(4):
+        grad_normed[...] += nt(
+            grad_states[which], weight[:, which * width : (which + 1) * width]
+        )
+
+    @pl.when(half == 1)
+    def finish():
+        here = state_in[...]
+        inverse = inverse_rms(here)
+        scaled = here * inverse
+        grad = grad_normed[...]
+        grad_gain[...] += jnp.sum(grad * scaled, axis=0, keepdims=True)
+        grad_state[...] = forget[...] * grad_state[...] + rms_back(
+            scaled, inverse, gain[...] * grad
+        )
+
+    @pl.when((half == 1) & (block == 0))
+    def end():
+        grad_init[...] = grad_state[...].astype(BF)
+
+
+def backward(
+    flags,
+    query,
+    key,
+    value,
+    state_query,
+    state_key,
+    state_value,
+    token_mixed,
+    state_mixed,
+    grad_mixed,
+    totals,
+    forget,
+    state_in,
+    apart,
+    gain,
+    weights,
+    out_weights,
+):
+    blocks = query.shape[0] // W
+    heads = D // HEAD
+    width = weights.shape[1]
+    half_width = width // 4
+
+    def rev(b):
+        return blocks - 1 - b
+
+    own = pl.BlockSpec((W, half_width), lambda b, t, s: (rev(b), t))
+    before = pl.BlockSpec((W, half_width), lambda b, t, s: (jnp.maximum(rev(b) - 1, 0), t))
+    whole = pl.BlockSpec((S, D), lambda b, t, s: (rev(b), 0))
+    fixed_row = pl.BlockSpec((1, D), lambda b, t, s: (0, 0))
+    return pl.pallas_call(
+        backward_kernel,
+        grid_spec=pltpu.PrefetchScalarGridSpec(
+            num_scalar_prefetch=1,
+            grid=(blocks, 2),
+            in_specs=[own, own, own, before, before]
+            + [own] * 6
+            + [pl.BlockSpec((1, 2 * heads, W), lambda b, t, s: (rev(b), 0, 0))]
+            + [whole] * 3
+            + [
+                once((1, D), lambda b, t, s: (0, 0)),
+                pl.BlockSpec((D, width), lambda b, t, s: (t, 0)),
+                once((D, half_width), lambda b, t, s: (0, 0)),
+                once((D, half_width), lambda b, t, s: (1, 0)),
+            ],
+            out_specs=[
+                pl.BlockSpec((3, W, half_width), lambda b, t, s: (0, rev(b), t)),
+                pl.BlockSpec((4, S, half_width), lambda b, t, s: (0, rev(b), t)),
+                whole,
+                pl.BlockSpec((S, D), lambda b, t, s: (0, 0)),
+                fixed_row,
+                fixed_row,
+            ],
+            scratch_shapes=[
+                pltpu.VMEM((S, D), F32),
+                pltpu.VMEM((2, S, half_width), BF),
+                pltpu.VMEM((S, D), F32),
+                pltpu.VMEM((2, S, half_width), BF),
+                pltpu.VMEM((2, W, half_width), F32),
+                pltpu.VMEM((2, W, half_width), F32),
+                pltpu.VMEM((HEAD, W + S), F32),
+                pltpu.VMEM((1, W + S), F32),
+                pltpu.VMEM((W + S, HEAD), BF),
+                pltpu.VMEM((W + S, HEAD), BF),
+            ],
+        ),
+        out_shape=[
+            jax.ShapeDtypeStruct((3, blocks * W, D), BF),
+            jax.ShapeDtypeStruct((4, blocks * W, D), BF),
+            jax.ShapeDtypeStruct((blocks * W, D), BF),
+            jax.ShapeDtypeStruct((S, D), BF),
+            jax.ShapeDtypeStruct((1, D), F32),
+            jax.ShapeDtypeStruct((1, D), F32),
+        ],
+        compiler_params=params(("arbitrary", "arbitrary")),
+        cost_estimate=cost(70e9, 100e6, 40e6),
+        name="backward",
+    )(
+        flags,
+        query,
+        key,
+        value,
+        key,
+        value,
+        state_query,
+        state_key,
+        state_value,
+        token_mixed,
+        state_mixed,
+        grad_mixed,
+        totals,
+        forget,
+        state_in,
+        apart,
+        gain,
+        weights,
+        out_weights,
+        out_weights,
+    )
+
+
+def weight_grad_kernel(left, right, out, turned):
+    @pl.when(pl.program_id(0) == 0)
+    def start():
+        turned[...] = left[...].T
+
+    out[...] = nn(turned[...], right[0]).astype(BF)
+
+
+def weight_grads(left, rights):
+    many, tokens, unused = rights.shape
+    width = D // 2
+    return pl.pallas_call(
+        weight_grad_kernel,
+        grid=(2 * many,),
+        in_specs=[
+            once((tokens, D), lambda g: (0, 0)),
+            pl.BlockSpec((1, tokens, width), lambda g: (g // 2, 0, g % 2)),
+        ],
+        out_specs=pl.BlockSpec((D, width), lambda g: (g % 2, g // 2)),
+        out_shape=jax.ShapeDtypeStruct((2 * D, many * width), BF),
+        scratch_shapes=[pltpu.VMEM((D, tokens), BF)],
+        compiler_params=params(),
+        cost_estimate=cost(2 * tokens * D * D * many, 2 * (tokens * D + 2 * many * D * D)),
+        name="weight_grads",
+    )(left, rights)
+
+
+def token_grad_kernel(grads, w0, w1, rows, grad_middle, gain, out, grad_gain):
+    width = w0.shape[1] // 3
+    total = None
+    for which in range(3):
+        for half, weight in enumerate((w0, w1)):
+            part = nt(
+                grads[which, :, half * width : (half + 1) * width],
+                weight[:, which * width : (which + 1) * width],
+            )
+            total = part if total is None else total + part
+    here = rows[...].astype(F32)
+    inverse = inverse_rms(here)
+    scaled = here * inverse
+    out[...] = (
+        grad_middle[...].astype(F32) + rms_back(scaled, inverse, gain[...] * total)
+    ).astype(BF)
+    part = jnp.sum(total * scaled, axis=0, keepdims=True)
+
+    @pl.when(pl.program_id(0) == 0)
+    def first():
+        grad_gain[...] = part
+
+    @pl.when(pl.program_id(0) > 0)
+    def later():
+        grad_gain[...] += part
+
+
+def token_grad(grads, weights, rows, grad_middle, gain):
+    tokens = rows.shape[0]
+    width = weights.shape[1]
+    block = pl.BlockSpec((W, D), lambda b: (b, 0))
+    return pl.pallas_call(
+        token_grad_kernel,
+        grid=(tokens // W,),
+        in_specs=[
+            pl.BlockSpec((3, W, D), lambda b: (0, b, 0)),
+            once((D, width), lambda b: (0, 0)),
+            once((D, width), lambda b: (1, 0)),
+            block,
+            block,
+            once((1, D), lambda b: (0, 0)),
+        ],
+        out_specs=[block, pl.BlockSpec((1, D), lambda b: (0, 0))],
+        out_shape=[jax.ShapeDtypeStruct((tokens, D), BF), jax.ShapeDtypeStruct((1, D), F32)],
+        compiler_params=params(),
+        cost_estimate=cost(2 * tokens * 3 * D * D, 2 * 6 * tokens * D),
+        name="token_grad",
+    )(grads, weights, weights, rows, grad_middle, gain)
+
+
+def gather(local):
+    return lax.all_gather(local, ("tensor", "dp"), axis=0, tiled=True)
+
+
+def scatter(total):
+    return lax.psum_scatter(total, ("tensor", "dp"), scatter_dimension=0, tiled=True)
+
+
+def whole_sequence_body(
+    tokens_in,
+    piece_starts,
+    cotangent,
+    gain_tokens,
+    gain_mlp,
+    gain_state,
+    gate_bias,
+    w_query,
+    w_key,
+    w_value,
+    w_out,
+    w_state_query,
+    w_state_key,
+    w_state_value,
+    w_state_out,
+    w_gate,
+    w_up,
+    w_down,
+    state_init,
+):
+    mine = lax.axis_index("tensor")
+    first = mine == 0
+    local_rows = w_query.shape[0]
+    dp = D // local_rows
+    width = w_query.shape[1]
+    units = 512
+    across = w_up.shape[1] // units
+    swap = [(0, 1), (1, 0)]
+
+    def bring(pair):
+        keep = jnp.where(first, pair[0, 0], pair[1, 0])
+        send = jnp.where(first, pair[1, 0], pair[0, 0])
+        come = lax.ppermute(send, "tensor", swap)
+        top = jnp.where(first, keep, come)
+        low = jnp.where(first, come, keep)
+        return jnp.concatenate([top, low], axis=1).reshape(NB * W, D)
+
+    def give(rows):
+        halves = rows.reshape(NB, 2, HALF, D)
+        keep = jnp.where(first, halves[:, 0], halves[:, 1])
+        send = jnp.where(first, halves[:, 1], halves[:, 0])
+        come = lax.ppermute(send, "tensor", swap)
+        return jnp.stack([jnp.where(first, keep, come), jnp.where(first, come, keep)])[:, None]
+
+    def split_init(values):
+        side = values.shape[1] // 2
+        return jnp.concatenate([values[:, :side], values[:, side:]], axis=0)
+
+    gains = jnp.stack([gain_tokens, gain_mlp, gain_state, gate_bias])
+    small = jnp.concatenate(
+        [split_init(state_init), jnp.pad(gains, ((0, local_rows - 4), (0, 128 - local_rows)))],
+        axis=1,
+    )
+    full_qkv = gather(jnp.concatenate([w_query, w_key, w_value, small], axis=1))
+    full_small = full_qkv[:, 3 * width :]
+    full_state = gather(
+        jnp.concatenate([w_state_query, w_state_key, w_state_value, w_gate], axis=1)
+    )
+    full_outs = gather(jnp.concatenate([w_state_out.T, w_out.T], axis=1))
+    up_parts = w_up.reshape(local_rows, across, 1, units)
+    down_parts = w_down.T.reshape(local_rows, across, 1, units)
+    full_mlp = gather(
+        jnp.concatenate([up_parts, down_parts], axis=2).reshape(local_rows, 2 * across * units)
+    )
+    side = width // 2
+    init = full_small[:, :side].reshape(2, dp, 2, local_rows // 2, side)
+    init = jnp.transpose(init, (1, 3, 0, 2, 4)).reshape(S, D)
+    gains = full_small[:D, side:].reshape(dp, local_rows, 128)[:, :4, :local_rows]
+    gains = jnp.transpose(gains, (1, 0, 2)).reshape(4, 1, D).astype(F32)
+
+    rows = bring(tokens_in)
+    cot = bring(cotangent)
+    starts = jnp.where(first, piece_starts[0, 0], piece_starts[1, 0])
+    flags = jnp.any(
+        starts[:, None] == PIECE * jnp.arange(NB * W // PIECE, dtype=jnp.int32)[None], axis=0
+    ).astype(jnp.int32)
+
+    weights_qkv = full_qkv[:, : 3 * width]
+    weights_so = full_outs[:, :width]
+    weights_out = full_outs[:, width:]
+    normed, query, key, value = project(rows, gains[0], weights_qkv)
+    (
+        token_mixed,
+        state_mixed,
+        state_normed,
+        state_query,
+        state_key,
+        state_value,
+        state_in,
+        forget,
+        apart,
+        totals,
+    ) = forward(flags, query, key, value, init, gains[2], gains[3], full_state, weights_so)
+    middle, mlp_in, mlp_turned, cot_turned = middle_rows(
+        rows, token_mixed, weights_out, gains[1], cot
+    )
+    mlp_out, grad_mlp_in, grad_mlp_w = mlp(mlp_in, mlp_turned, cot, cot_turned, full_mlp)
+    output, grad_middle, grad_mixed, grad_gain_mlp = after_mlp(
+        middle, mlp_out, grad_mlp_in, cot, gains[1], weights_out
+    )
+    part_mlp = scatter(grad_mlp_w)
+    grad_tok, grad_sta, branch, grad_init, grad_gain_state, grad_bias = backward(
+        flags,
+        query,
+        key,
+        value,
+        state_query,
+        state_key,
+        state_value,
+        token_mixed,
+        state_mixed,
+        grad_mixed,
+        totals,
+        forget,
+        state_in,
+        apart,
+        gains[2],
+        full_state,
+        weights_so,
+    )
+    part_out = scatter(weight_grads(grad_middle, token_mixed[None]))
+    part_so = scatter(weight_grads(branch, state_mixed[None]))
+    part_state = scatter(weight_grads(state_normed, grad_sta))
+    part_qkv = scatter(weight_grads(normed, grad_tok))
+    grad_in, grad_gain_tokens = token_grad(grad_tok, weights_qkv, rows, grad_middle, gains[0])
+
+    init_parts = jnp.transpose(
+        grad_init.reshape(dp, local_rows // 2, 2, 2, side), (2, 0, 3, 1, 4)
+    ).reshape(2 * D, side)
+    gain_parts = jnp.stack(
+        [grad_gain_tokens[0], grad_gain_mlp[0], grad_gain_state[0], grad_bias[0]]
+    ).reshape(4, dp, local_rows)
+    gain_parts = jnp.pad(
+        jnp.transpose(gain_parts, (1, 0, 2)),
+        ((0, 0), (0, local_rows - 4), (0, 128 - local_rows)),
+    ).reshape(D, 128)
+    gain_parts = jnp.concatenate([gain_parts, gain_parts], axis=0).astype(BF)
+    part_small = scatter(jnp.concatenate([init_parts, gain_parts], axis=1)).astype(F32)
+
+    part_init = part_small[:, :side]
+    part_init = jnp.concatenate(
+        [part_init[: local_rows // 2], part_init[local_rows // 2 :]], axis=1
+    )
+    part_gains = part_small[:4, side : side + local_rows]
+    part_mlp = part_mlp.astype(F32).reshape(local_rows, across, 2, units)
+    part_qkv = part_qkv.astype(F32)
+    part_state = part_state.astype(F32)
+    return (
+        give(output),
+        give(grad_in),
+        part_gains[0],
+        part_gains[1],
+        part_gains[2],
+        part_gains[3],
+        part_qkv[:, :width],
+        part_qkv[:, width : 2 * width],
+        part_qkv[:, 2 * width :],
+        part_out.astype(F32).T,
+        part_state[:, :width],
+        part_state[:, width : 2 * width],
+        part_state[:, 2 * width : 3 * width],
+        part_so.astype(F32).T,
+        part_state[:, 3 * width :],
+        part_mlp[:, :, 0].reshape(local_rows, across * units),
+        part_mlp[:, :, 1].reshape(local_rows, across * units).T,
+        part_init,
+    )
+
+
 def solution(mesh):
+    one_each = mesh.shape["tensor"] == MICRO
     return jax.shard_map(
-        body,
+        whole_sequence_body if one_each else generic_body,
         mesh=mesh,
         in_specs=(
             P(None, "dp", None, "tensor", None),

time: 3420 us -> 1540 us (0.45)
  matrix products: 1120 us -> 0 us
  waiting for transfers between devices: 1630 us -> 913 us
  Pallas kernels: 0 us -> 528 us
  other arithmetic: 337 us -> 35 us
  blocking collectives: 129 us -> 0 us
  local copies, waits for them, and re-layouts: 153 us -> 38.4 us
    dot_general x320 -> x0, matrix products: 1120 us -> none  [the longest x72 225 us: matmul(): return jnp.dot(left, right, preferred_element_type=jnp.float32)]
    all_gather x46 -> x4, waiting for transfers between devices: 684 us -> 77 us  [gather(): return lax.all_gather(local, ('tensor', 'dp'), axis=0, tiled=True)]
    pallas_call x0 -> x11, Pallas kernels: none -> 528 us  [the longest x1 152 us: backward(): pl.pallas_call(backward_kernel, grid_spec=pltpu.PrefetchScalarGridSpec(nu...]
    reduce_scatter x48 -> x6, waiting for transfers between devices: 932 us -> 673 us  [scatter(): lax.psum_scatter(total, ('tensor', 'dp'), scatter_dimension=0, tiled=True)]
    ppermute x0 -> x4, waiting for transfers between devices: none -> 163 us  [the longest x2 106 us: bring(): come = lax.ppermute(send, 'tensor', swap)]
    convert_element_type x50 -> x3, other arithmetic: 156 us -> 1.33 us  [the longest x1 0.81 us: whole_sequence_body(): scatter(jnp.concatenate([init_parts, gain_parts], axis=1)).astype(F32)]
    reduce_sum x35 -> x0, other arithmetic: 101 us -> none  [the longest x16 44.3 us: attend(): jnp.sum(jnp.exp(scores - top), axis=-1, keepdims=True)]
    unnamed x1347 -> x23, local copies, waits for them, and re-layouts: 86.5 us -> 5.18 us
  transfers between devices with their start and end apart: 94 -> 14, of which waited for: 66 -> 12; matrix products, arithmetic and copies ran while one was open for 41% -> 4% of each run, Pallas kernels for 0% -> 14%
where the time goes in v1:
time: 1540 us
  waiting for transfers between devices  913 us (59%)
  Pallas kernels  528 us (34%)
  local copies, waits for them, and re-layouts  38.4 us (2%)
  other arithmetic  35 us (2%)
    reduce_scatter x6, waiting for transfers between devices, scatter(): lax.psum_scatter(total, ('tensor', 'dp'), scatter_dimension=0, tiled=True)  673 us
    pallas_call x1, Pallas kernels, backward(): pl.pallas_call(backward_kernel, grid_spec=pltpu.PrefetchScalarGridSpec(nu...  152 us
    pallas_call x1, Pallas kernels, mlp(): pl.pallas_call(mlp_kernel, grid=(2 * across,), in_specs=[rows, turned, ro...  128 us
    pallas_call x1, Pallas kernels, forward(): pl.pallas_call(forward_kernel, grid_spec=pltpu.PrefetchScalarGridSpec(num...  114 us
    ppermute x2, waiting for transfers between devices, bring(): come = lax.ppermute(send, 'tensor', swap)  106 us
    all_gather x4, waiting for transfers between devices, gather(): return lax.all_gather(local, ('tensor', 'dp'), axis=0, tiled=True)  77 us
    pallas_call x4, Pallas kernels, weight_grads(): pl.pallas_call(weight_grad_kernel, grid=(2 * many,), in_specs=[once((toke...  63 us
    ppermute x2, waiting for transfers between devices, give(): come = lax.ppermute(send, 'tensor', swap)  57.3 us
  transfers between devices with their start and end apart: 14, of which 12 were waited for; matrix products, arithmetic and copies ran while one was open for 4% of the time, Pallas kernels for 14%

profile of v1, /device:TPU:0, one launch (start us, length us, event | category | flops | bytes accessed | tf_op | source)
XLA Modules:
  0.0 1536.8 jit_solution(1482256144990836945)
XLA Ops:
  20.5 2.7 select_bitcast_fusion.2
  23.2 3.0 collective-permute-start.1
  27.9 56.0 %collective-permute-done.1 = bf16[4,256,1024]{2,1,0:T(8,128)(2,1)S(1)} collective-permute-done((bf16[4,256,1024]{2,1,0:T(8,128)(2,1)S(1)}, bf16[4,256,1024]{2,1,0:T(8,128)(2,1)S(1)}, u32[]{:S(2)}, u32[]{:S(2)}) %collective-permute-start.1) | collective-permute-done | bytes 2097184 | tf_op jit(solution)/shard_map/ppermute | solution.py:1403
  86.7 50.1 %collective-permute-done = bf16[4,256,1024]{2,1,0:T(8,128)(2,1)S(1)} collective-permute-done((bf16[4,256,1024]{2,1,0:T(8,128)(2,1)S(1)}, bf16[4,256,1024]{2,1,0:T(8,128)(2,1)S(1)}, u32[]{:S(2)}, u32[]{:S(2)}) %collective-permute-start) | collective-permute-done | bytes 2097184 | tf_op jit(solution)/shard_map/ppermute | solution.py:1403
  137.2 2.5 pad_maximum_fusion
  139.6 4.6 fusion.18
  144.2 28.2 %all-gather.5.cloned.1.call-done = bf16[2048,1920]{1,0:T(8,128)(2,1)} async-done(((bf16[64,1920]{1,0:T(8,128)(2,1)}), bf16[2048,1920]{1,0:T(8,128)(2,1)}) %all-gather.5.cloned.1.call-update) | async-done | bytes 7864336 | tf_op jit(solution)/shard_map/all_gather | solution.py:1363
  178.8 5.8 slice.177.w0.w1
  184.7 18.6 %project.1 = (bf16[2048,1024]{1,0:T(8,128)(2,1)}, bf16[2048,1024]{1,0:T(8,128)(2,1)}, bf16[2048,1024]{1,0:T(8,128)(2,1)}, bf16[2048,1024]{1,0:T(8,128)(2,1)}) custom-call(bf16[2048,1024]{1,0:T(8,128)(2,1)} %bitcast.126, f32[1,1024]{1,0:T(1,128)} %squeeze.16.gain, bf16[2048,1536]{1,0:T(8,128)(2,1)} %slice.177.w0.w1, bf16[2048,1536]{1,0:T(8,128)(2,1)} %slice.177.w0.w1), custom_call_target="tpu_custom_call" | custom-call | flops 12884901888 | bytes 27262976 | tf_op jit(solution)/shard_map/project/pallas_call | solution.py:673
  203.3 48.8 %all-gather.7.cloned.1.call-done.wst0.wst1.weight = bf16[2048,2048]{1,0:T(8,128)(2,1)} async-done(((bf16[64,2048]{1,0:T(8,128)(2,1)}), bf16[2048,2048]{1,0:T(8,128)(2,1)}) %all-gather.7.cloned.1.call-update) | async-done | bytes 8388624 | tf_op jit(solution)/shard_map/all_gather | solution.py:1363
  252.1 114.2 %forward.1 = (bf16[2048,1024]{1,0:T(8,128)(2,1)}, bf16[2048,1024]{1,0:T(8,128)(2,1)}, bf16[2048,1024]{1,0:T(8,128)(2,1)}, bf16[2048,1024]{1,0:T(8,128)(2,1)}, bf...) custom-call(s32[8]{0:T(128)} %convert_element_type.35.flags, ...), custom_call_target="tpu_custom_call" | custom-call | flops 41999998976 | bytes 100000000 | tf_op jit(solution)/shard_map/forward/pallas_call | solution.py:816
  366.2 14.2 middle.1
  380.5 127.6 %mlp.1 = (bf16[2048,1024]{1,0:T(8,128)(2,1)}, bf16[2048,1024]{1,0:T(8,128)(2,1)}, bf16[2048,4096]{1,0:T(8,128)(2,1)}) custom-call(bf16[2048,1024]{1,0:T(8,128)(2,1)} %get-tuple-element.56.mlp_in, bf16[1024,2048]{1,0:T(8,128)(2,1)} %get-tuple-element.57.mlp_turned, bf16[2048,1024]{1,0:T(8,128)(2,1)} %bitcast.124, ...), custom_call_target="tpu_custom_call" | custom-call | flops 102999998464 | bytes 60000000 | tf_op jit(solution)/shard_map/mlp/pallas_call | solution.py:955
  508.1 16.5 %after_mlp.1 = (bf16[2048,1024]{1,0:T(8,128)(2,1)}, bf16[2048,1024]{1,0:T(8,128)(2,1)}, bf16[2048,1024]{1,0:T(8,128)(2,1)}, f32[1,1024]{1,0:T(1,128)}) custom-call(f32[2048,1024]{1,0:T(8,128)} %get-tuple-element.55.middle, bf16[2048,1024]{1,0:T(8,128)(2,1)} %get-tuple-element.59.mlp_out, bf16[2048,1024]{1,0:T(8,128)(2,1)} %get-tuple-element.60.grad_in, ...), custom_call_target="tpu_custom_call" | custom-call | flops 4294967296 | bytes 33554432 | tf_op jit(solution)/shard_map/after_mlp/pallas_call | solution.py:1002
  524.6 152.4 %backward.1 = (bf16[3,2048,1024]{2,1,0:T(8,128)(2,1)}, bf16[4,2048,1024]{2,1,0:T(8,128)(2,1)}, bf16[2048,1024]{1,0:T(8,128)(2,1)}, bf16[512,1024]{1,0:T(8,128)(2...) custom-call(s32[8]{0:T(128)} %convert_element_type.35.flags, bf16[2048,1024]{1,0:T(8,128)(2,1)} %get-tuple-element.51.query, ...), custom_call_target="tpu_custom_call" | custom-call | flops 70000001024 | bytes 100000000 | tf_op jit(solution)/shard_map/backward/pallas_call | solution.py:1214
  679.1 21.9 %token_grad.1 = (bf16[2048,1024]{1,0:T(8,128)(2,1)}, f32[1,1024]{1,0:T(1,128)}) custom-call(bf16[3,2048,1024]{2,1,0:T(8,128)(2,1)} %get-tuple-element.71.grads.right, bf16[2048,1536]{1,0:T(8,128)(2,1)} %slice.177.w0.w1, bf16[2048,1536]{1,0:T(8,128)(2,1)} %slice.177.w0.w1, bf16[2048,1024]{1,0:T(8,128)(2,1)} %bitcast.128, ...), custom_call_target="tpu_custom_call" | custom-call | flops 12884901888 | bytes 25165824 | tf_op jit(solution)/shard_map/token_grad/pallas_call | solution.py:1343
  703.3 9.8 weight_grads.5
  713.2 9.8 weight_grads.7
  723.1 19.3 %weight_grads.4 = bf16[2048,1536]{1,0:T(8,128)(2,1)} custom-call(bf16[2048,1024]{1,0:T(8,128)(2,1)} %get-tuple-element.79.left, bf16[3,2048,1024]{2,1,0:T(8,128)(2,1)} %get-tuple-element.71.grads.right), custom_call_target="tpu_custom_call" | custom-call | flops 12884901888 | bytes 16777216 | tf_op jit(solution)/shard_map/weight_grads/pallas_call | solution.py:1296
  742.4 24.0 %weight_grads.6 = bf16[2048,2048]{1,0:T(8,128)(2,1)} custom-call(bf16[2048,1024]{1,0:T(8,128)(2,1)} %get-tuple-element.80.left, bf16[4,2048,1024]{2,1,0:T(8,128)(2,1)} %get-tuple-element.81.right), custom_call_target="tpu_custom_call" | custom-call | flops 17179869184 | bytes 20971520 | tf_op jit(solution)/shard_map/weight_grads/pallas_call | solution.py:1296
  767.1 4.0 select_bitcast_fusion.1
  773.4 25.6 %reduce-scatter.7.cloned.1.call-done = bf16[64,384]{1,0:T(8,128)(2,1)} async-done(((bf16[2048,384]{1,0:T(8,128)(2,1)}), bf16[64,384]{1,0:T(8,128)(2,1)}) %reduce-scatter.7.cloned.1.call-update) | async-done | bytes 49168 | tf_op jit(solution)/shard_map/reduce_scatter | solution.py:1367
  801.2 19.1 %collective-permute-done.2 = bf16[4,256,1024]{2,1,0:T(8,128)(2,1)} collective-permute-done((bf16[4,256,1024]{2,1,0:T(8,128)(2,1)}, bf16[4,256,1024]{2,1,0:T(8,128)(2,1)}, u32[]{:S(2)}, u32[]{:S(2)}) %collective-permute-start.2) | collective-permute-done | bytes 2097184 | tf_op jit(solution)/shard_map/ppermute | solution.py:1412
  820.3 3.3 fusion.2
  823.5 2.5 maximum_bitcast_fusion
  826.0 38.2 %collective-permute-done.3 = bf16[4,256,1024]{2,1,0:T(8,128)(2,1)} collective-permute-done((bf16[4,256,1024]{2,1,0:T(8,128)(2,1)S(1)}, bf16[4,256,1024]{2,1,0:T(8,128)(2,1)}, u32[]{:S(2)}, u32[]{:S(2)}) %collective-permute-start.3) | collective-permute-done | bytes 2097184 | tf_op jit(solution)/shard_map/ppermute | solution.py:1412
  869.2 69.1 %reduce-scatter.11.cloned.1.call-done = bf16[64,512]{1,0:T(8,128)(2,1)} async-done(((bf16[2048,512]{1,0:T(8,128)(2,1)}), bf16[64,512]{1,0:T(8,128)(2,1)}) %reduce-scatter.11.cloned.1.call-update) | async-done | bytes 65552 | tf_op jit(solution)/shard_map/reduce_scatter | solution.py:1367
  939.7 133.9 %reduce-scatter.15.cloned.1.call-done = bf16[64,512]{1,0:T(8,128)(2,1)} async-done(((bf16[2048,512]{1,0:T(8,128)(2,1)}), bf16[64,512]{1,0:T(8,128)(2,1)}) %reduce-scatter.15.cloned.1.call-update) | async-done | bytes 65552 | tf_op jit(solution)/shard_map/reduce_scatter | solution.py:1367
  1075.1 114.9 %reduce-scatter.9.cloned.1.call-done = bf16[64,1536]{1,0:T(8,128)(2,1)} async-done(((bf16[2048,1536]{1,0:T(8,128)(2,1)}), bf16[64,1536]{1,0:T(8,128)(2,1)}) %reduce-scatter.9.cloned.1.call-update) | async-done | bytes 196624 | tf_op jit(solution)/shard_map/reduce_scatter | solution.py:1367
  1191.7 148.5 %reduce-scatter.13.cloned.1.call-done = bf16[64,2048]{1,0:T(8,128)(2,1)} async-done(((bf16[2048,2048]{1,0:T(8,128)(2,1)}), bf16[64,2048]{1,0:T(8,128)(2,1)}) %reduce-scatter.13.cloned.1.call-update) | async-done | bytes 262160 | tf_op jit(solution)/shard_map/reduce_scatter | solution.py:1367
  1341.9 180.6 %reduce-scatter.17.cloned.1.call-done = bf16[64,4096]{1,0:T(8,128)(2,1)} async-done(((bf16[2048,4096]{1,0:T(8,128)(2,1)}), bf16[64,4096]{1,0:T(8,128)(2,1)}) %reduce-scatter.17.cloned.1.call-update) | async-done | bytes 524304 | tf_op jit(solution)/shard_map/reduce_scatter | solution.py:1367
  1524.6 3.0 slice_reduce_fusion
  (96 shorter events, 49.3 us)
Async XLA Ops:
  7.2 132.5 %all-gather.9.cloned.1.call-start = ((), (), s32[]{:S(2)}) async-start(), calls=%async_computation.8 | async-start | bytes 4325376 | tf_op jit(solution)/shard_map/all_gather | solution.py:1363
  8.8 163.6 %all-gather.5.cloned.1.call-start = ((), (), s32[]{:S(2)}) async-start(), calls=%async_computation.6 | async-start | bytes 8110080 | tf_op jit(solution)/shard_map/all_gather | solution.py:1363
  12.9 0.7 copy-start.4
  13.6 238.5 %all-gather.7.cloned.1.call-start = ((), (), s32[]{:S(2)}) async-start(), calls=%async_computation.7 | async-start | bytes 8650752 | tf_op jit(solution)/shard_map/all_gather | solution.py:1363
  15.3 365.2 %all-gather.11.cloned.1.call-start = ((), (), s32[]{:S(2)}) async-start(), calls=%async_computation.9 | async-start | bytes 17301504 | tf_op jit(solution)/shard_map/all_gather | solution.py:1363
  20.5 778.5 %reduce-scatter.7.cloned.1.call-start = ((), (), s32[]{:S(2)}) async-start(), calls=%async_computation.10 | async-start | bytes 1622016 | tf_op jit(solution)/shard_map/reduce_scatter | solution.py:1367
  20.5 5.7 copy-start.1
  23.2 4.1 copy-start.8
  23.2 60.7 %copy-start = (bf16[2,1,4,256,1024]{4,3,2,1,0:T(8,128)(2,1)S(1)}, bf16[2,1,4,256,1024]{4,3,2,1,0:T(8,128)(2,1)}, u32[]{:S(2)}) copy-start(bf16[2,1,4,256,1024]{4,3,2,1,0:T(8,128)(2,1)} %param.21) | copy-start | bytes 12582916
  23.2 60.7 %collective-permute-start.1 = (bf16[4,256,1024]{2,1,0:T(8,128)(2,1)S(1)}, bf16[4,256,1024]{2,1,0:T(8,128)(2,1)S(1)}, u32[]{:S(2)}, u32[]{:S(2)}) collective-permute-start(bf16[4,256,1024]{2,1,0:T(8,128)(2,1)S(1)} %select_bitcast_fusion.2), channel_id=1, source_target_pairs={{0,1},{1,0},{2,3},{3,2},{4,5},{5,4},{6,7},{7,6},{8,9},{9,8},{10,11... | collective-permute-start | bytes 6291464 | tf_op jit(solution)/shard_map/ppermute | solution.py:1403
  26.5 110.4 %collective-permute-start = (bf16[4,256,1024]{2,1,0:T(8,128)(2,1)S(1)}, bf16[4,256,1024]{2,1,0:T(8,128)(2,1)S(1)}, u32[]{:S(2)}, u32[]{:S(2)}) collective-permute-start(bf16[4,256,1024]{2,1,0:T(8,128)(2,1)S(1)} %select_bitcast_fusion.3), channel_id=1, source_target_pairs={{0,1},{1,0},{2,3},{3,2},{4,5},{5,4},{6,7},{7,6},{8,9},{9,8},{10,11... | collective-permute-start | bytes 6291464 | tf_op jit(solution)/shard_map/ppermute | solution.py:1403
  172.4 3.8 slice-start
  679.1 21.9 %copy-start.5 = (f32[1,1024]{1,0:T(1,128)S(1)}, f32[1,1024]{1,0:T(1,128)}, u32[]{:S(2)}) copy-start(f32[1,1024]{1,0:T(1,128)} %get-tuple-element.76) | copy-start | bytes 12292
  679.1 21.9 %copy-start.6 = (f32[1,1024]{1,0:T(1,128)S(1)}, f32[1,1024]{1,0:T(1,128)}, u32[]{:S(2)}) copy-start(f32[1,1024]{1,0:T(1,128)} %get-tuple-element.77) | copy-start | bytes 12292
  679.1 21.9 %copy-start.7 = (f32[1,1024]{1,0:T(1,128)S(1)}, f32[1,1024]{1,0:T(1,128)}, u32[]{:S(2)}) copy-start(f32[1,1024]{1,0:T(1,128)} %get-tuple-element.78) | copy-start | bytes 12292
  703.3 235.0 %reduce-scatter.11.cloned.1.call-start = ((), (), s32[]{:S(2)}) async-start(), calls=%async_computation.12 | async-start | bytes 2162688 | tf_op jit(solution)/shard_map/reduce_scatter | solution.py:1367
  713.1 360.5 %reduce-scatter.15.cloned.1.call-start = ((), (), s32[]{:S(2)}) async-start(), calls=%async_computation.14 | async-start | bytes 2162688 | tf_op jit(solution)/shard_map/reduce_scatter | solution.py:1367
  723.0 467.0 %reduce-scatter.9.cloned.1.call-start = ((), (), s32[]{:S(2)}) async-start(), calls=%async_computation.11 | async-start | bytes 6488064 | tf_op jit(solution)/shard_map/reduce_scatter | solution.py:1367
  742.4 597.8 %reduce-scatter.13.cloned.1.call-start = ((), (), s32[]{:S(2)}) async-start(), calls=%async_computation.13 | async-start | bytes 8650752 | tf_op jit(solution)/shard_map/reduce_scatter | solution.py:1367
  766.5 756.0 %reduce-scatter.17.cloned.1.call-start = ((), (), s32[]{:S(2)}) async-start(), calls=%async_computation.15 | async-start | bytes 17301504 | tf_op jit(solution)/shard_map/reduce_scatter | solution.py:1367
  767.1 5.5 copy-start.2
  771.1 49.2 %collective-permute-start.2 = (bf16[4,256,1024]{2,1,0:T(8,128)(2,1)}, bf16[4,256,1024]{2,1,0:T(8,128)(2,1)}, u32[]{:S(2)}, u32[]{:S(2)}) collective-permute-start(bf16[4,256,1024]{2,1,0:T(8,128)(2,1)} %select_bitcast_fusion.1), channel_id=1, source_target_pairs={{0,1},{1,0},{2,3},{3,2},{4,5},{5,4},{6,7},{7,6},{8,9},{9,8},{10,11... | collective-permute-start | bytes 6291464 | tf_op jit(solution)/shard_map/ppermute | solution.py:1412
  772.8 91.5 %collective-permute-start.3 = (bf16[4,256,1024]{2,1,0:T(8,128)(2,1)S(1)}, bf16[4,256,1024]{2,1,0:T(8,128)(2,1)}, u32[]{:S(2)}, u32[]{:S(2)}) collective-permute-start(bf16[4,256,1024]{2,1,0:T(8,128)(2,1)S(1)} %select_bitcast_fusion), channel_id=1, source_target_pairs={{0,1},{1,0},{2,3},{3,2},{4,5},{5,4},{6,7},{7,6},{8,9},{9,8},{10,11... | collective-permute-start | bytes 6291464 | tf_op jit(solution)/shard_map/ppermute | solution.py:1412
  823.5 40.7 %copy-start.3 = (bf16[2048,1024]{1,0:T(8,128)(2,1)S(1)}, bf16[2048,1024]{1,0:T(8,128)(2,1)}, u32[]{:S(2)}) copy-start(bf16[2048,1024]{1,0:T(8,128)(2,1)} %get-tuple-element.73) | copy-start | bytes 12582916
Sparse Core Ops, SparseCore 0:
  11.5 74.8 all-gather.8
  89.8 82.5 all-gather.4
  175.9 76.1 all-gather.6
  255.4 113.4 all-gather.10
  703.4 95.5 reduce-scatter.6
  801.1 137.0 reduce-scatter.10
  940.6 133.0 reduce-scatter.14
  1079.3 110.7 reduce-scatter.8
  1192.5 147.6 reduce-scatter.12
  1342.4 180.0 reduce-scatter.16

commit v2 on v1

--- a/solution.py
+++ b/solution.py
@@ -1,3 +1,4 @@
+import functools
 import math
 
 import jax
@@ -654,20 +655,21 @@
     return pl.BlockSpec(shape, index, pipeline_mode=pl.Buffered(1))
 
 
-def project_kernel(rows, gain, w0, w1, normed, query, key, value):
+def project_kernel(rows, gain, w0, w1, turned, query, key, value):
     width = w0.shape[1] // 3
     wide = rows[...].astype(F32)
-    normed[...] = (wide * inverse_rms(wide) * gain[...]).astype(BF)
+    normed = (wide * inverse_rms(wide) * gain[...]).astype(BF)
+    turned[...] = normed.T
     for half, weight in enumerate((w0, w1)):
         for which, out in enumerate((query, key, value)):
             out[:, half * width : (half + 1) * width] = nn(
-                normed[...], weight[:, which * width : (which + 1) * width]
+                normed, weight[:, which * width : (which + 1) * width]
             ).astype(BF)
 
 
 def project(rows, gain, weights):
     tokens = rows.shape[0]
-    width = weights.shape[1]
+    width = 3 * D // 2
     out = jax.ShapeDtypeStruct((tokens, D), BF)
     block = pl.BlockSpec((W, D), lambda b: (b, 0))
     return pl.pallas_call(
@@ -679,8 +681,8 @@
             once((D, width), lambda b: (0, 0)),
             once((D, width), lambda b: (1, 0)),
         ],
-        out_specs=[block] * 4,
-        out_shape=[out] * 4,
+        out_specs=[pl.BlockSpec((D, W), lambda b: (0, b))] + [block] * 3,
+        out_shape=[jax.ShapeDtypeStruct((D, tokens), BF)] + [out] * 3,
         compiler_params=params(),
         cost_estimate=cost(2 * tokens * D * 3 * D, 2 * (5 * tokens * D + 3 * D * D)),
         name="project",
@@ -702,12 +704,6 @@
     return (mixed / total).astype(BF), top * EXP2_SCALE + jnp.log2(total)
 
 
-def allowed_in_half(flag):
-    row = lax.broadcasted_iota(jnp.int32, (HALF, HALF), 0)
-    column = lax.broadcasted_iota(jnp.int32, (HALF, HALF), 1)
-    return row, column
-
-
 def forward_kernel(
     flags,
     query,
@@ -718,13 +714,15 @@
     init,
     gain,
     bias,
-    wst0,
-    wst1,
-    wso0,
-    wso1,
+    query0,
+    query1,
+    key0,
+    key1,
+    second0,
+    second1,
     token_mixed,
     state_mixed,
-    state_normed,
+    turned,
     state_query,
     state_key,
     state_value,
@@ -737,7 +735,7 @@
     state_totals,
 ):
     block = pl.program_id(0)
-    width = wso0.shape[1]
+    width = query0.shape[1]
 
     @pl.when(block == 0)
     def start():
@@ -745,14 +743,14 @@
 
     now = state[...]
     state_in[...] = now
-    state_normed[...] = (now * inverse_rms(now) * gain[...]).astype(BF)
-    for half, weight in enumerate((wst0, wst1)):
+    state_normed = (now * inverse_rms(now) * gain[...]).astype(BF)
+    turned[...] = state_normed.T
+    for half, (one, other, two) in enumerate(((query0, key0, second0), (query1, key1, second1))):
         columns = slice(half * width, (half + 1) * width)
-        for which, out in enumerate((state_query, state_key, state_value)):
-            out[:, columns] = nn(
-                state_normed[...], weight[:, which * width : (which + 1) * width]
-            ).astype(BF)
-        gate = nn(state_normed[...], weight[:, 3 * width :]) + bias[:, columns]
+        state_query[:, columns] = nn(state_normed, one[...]).astype(BF)
+        state_key[:, columns] = nn(state_normed, other[...]).astype(BF)
+        state_value[:, columns] = nn(state_normed, two[:, :width]).astype(BF)
+        gate = nn(state_normed, two[:, width : 2 * width]) + bias[:, columns]
         forget[:, columns] = jax.nn.sigmoid(gate)
 
     def heads(with_before):
@@ -800,15 +798,16 @@
     count = D // HEAD
     totals[0, :count, :] = token_totals[...].T[:count]
     totals[0, count:, :] = state_totals[...].T[:count]
-    new = nt(state_mixed[:, :width], wso0[...]) + nt(state_mixed[:, width:], wso1[...])
+    new = nt(state_mixed[:, :width], second0[:, 2 * width :]) + nt(
+        state_mixed[:, width:], second1[:, 2 * width :]
+    )
     apart[...] = (now - new).astype(BF)
     state[...] = new + forget[...] * (now - new)
 
 
-def forward(flags, query, key, value, init, gain, bias, weights, out_weights):
+def forward(flags, query, key, value, init, gain, bias, weights, more_weights):
     blocks = query.shape[0] // W
     heads = D // HEAD
-    width = weights.shape[1]
     own = pl.BlockSpec((W, D), lambda b, s: (b, 0))
     before = pl.BlockSpec((W, D), lambda b, s: (jnp.maximum(b - 1, 0), 0))
     low = jax.ShapeDtypeStruct((blocks * W, D), BF)
@@ -827,19 +826,27 @@
                 once((S, D), lambda b, s: (0, 0)),
                 once((1, D), lambda b, s: (0, 0)),
                 once((1, D), lambda b, s: (0, 0)),
-                once((D, width), lambda b, s: (0, 0)),
-                once((D, width), lambda b, s: (1, 0)),
-                once((D, width // 4), lambda b, s: (0, 0)),
-                once((D, width // 4), lambda b, s: (1, 0)),
+                once((D, D // 2), lambda b, s: (0, 3)),
+                once((D, D // 2), lambda b, s: (1, 3)),
+                once((D, D // 2), lambda b, s: (0, 4)),
+                once((D, D // 2), lambda b, s: (1, 4)),
+                once((D, more_weights.shape[1]), lambda b, s: (0, 0)),
+                once((D, more_weights.shape[1]), lambda b, s: (1, 0)),
             ],
-            out_specs=[own] * 9 + [pl.BlockSpec((1, 2 * heads, W), lambda b, s: (b, 0, 0))],
+            out_specs=[own] * 2
+            + [pl.BlockSpec((D, S), lambda b, s: (0, b))]
+            + [own] * 6
+            + [pl.BlockSpec((1, 2 * heads, W), lambda b, s: (b, 0, 0))],
             scratch_shapes=[
                 pltpu.VMEM((S, D), F32),
                 pltpu.VMEM((W, HEAD), F32),
                 pltpu.VMEM((S, HEAD), F32),
             ],
         ),
-        out_shape=[low] * 6 + [wide, wide, low, jax.ShapeDtypeStruct((blocks, 2 * heads, W), F32)],
+        out_shape=[low] * 2
+        + [jax.ShapeDtypeStruct((D, blocks * S), BF)]
+        + [low] * 3
+        + [wide, wide, low, jax.ShapeDtypeStruct((blocks, 2 * heads, W), F32)],
         compiler_params=params(),
         cost_estimate=cost(42e9, 100e6, 40e6),
         name="forward",
@@ -855,8 +862,10 @@
         bias,
         weights,
         weights,
-        out_weights,
-        out_weights,
+        weights,
+        weights,
+        more_weights,
+        more_weights,
     )
 
 
@@ -874,7 +883,8 @@
 
 def middle_rows(rows, mixed, weights, gain, cotangent):
     tokens = rows.shape[0]
-    width = weights.shape[1]
+    width = D // 2
+    last = weights.shape[1] // width - 1
     block = pl.BlockSpec((W, D), lambda b: (b, 0))
     turned = pl.BlockSpec((D, W), lambda b: (0, b))
     low = jax.ShapeDtypeStruct((tokens, D), BF)
@@ -884,8 +894,8 @@
         in_specs=[
             block,
             block,
-            once((D, width), lambda b: (0, 0)),
-            once((D, width), lambda b: (1, 0)),
+            once((D, width), lambda b: (0, last)),
+            once((D, width), lambda b: (1, last)),
             once((1, D), lambda b: (0, 0)),
             block,
         ],
@@ -947,7 +957,7 @@
 def mlp(mlp_in, mlp_turned, cot, cot_turned, weights):
     tokens = mlp_in.shape[0]
     units = 512
-    across = weights.shape[1] // (2 * units)
+    across = (weights.shape[1] - D // 2) // (2 * units)
     low = jax.ShapeDtypeStruct((tokens, D), BF)
     rows = once((tokens, D), lambda f: (0, 0))
     turned = once((D, tokens), lambda f: (0, 0))
@@ -971,7 +981,7 @@
 
 
 def after_mlp_kernel(
-    middle, mlp_out, grad_in, cot, gain, w0, w1, output, grad_middle, grad_mixed, grad_gain
+    middle, mlp_out, grad_in, cot, gain, w0, w1, output, grad_middle, turned, grad_mixed, grad_gain
 ):
     width = w0.shape[1]
     here = middle[...]
@@ -981,6 +991,7 @@
     output[...] = (here + mlp_out[...].astype(F32)).astype(BF)
     low = (cot[...].astype(F32) + rms_back(scaled, inverse, gain[...] * grad)).astype(BF)
     grad_middle[...] = low
+    turned[...] = low.T
     grad_mixed[:, :width] = nn(low, w0[...]).astype(BF)
     grad_mixed[:, width:] = nn(low, w1[...]).astype(BF)
     part = jnp.sum(grad * scaled, axis=0, keepdims=True)
@@ -996,7 +1007,8 @@
 
 def after_mlp(middle, mlp_out, grad_in, cot, gain, weights):
     tokens = middle.shape[0]
-    width = weights.shape[1]
+    width = D // 2
+    last = weights.shape[1] // width - 1
     block = pl.BlockSpec((W, D), lambda b: (b, 0))
     low = jax.ShapeDtypeStruct((tokens, D), BF)
     return pl.pallas_call(
@@ -1008,11 +1020,23 @@
             block,
             block,
             once((1, D), lambda b: (0, 0)),
-            once((D, width), lambda b: (0, 0)),
-            once((D, width), lambda b: (1, 0)),
+            once((D, width), lambda b: (0, last)),
+            once((D, width), lambda b: (1, last)),
         ],
-        out_specs=[block, block, block, pl.BlockSpec((1, D), lambda b: (0, 0))],
-        out_shape=[low, low, low, jax.ShapeDtypeStruct((1, D), F32)],
+        out_specs=[
+            block,
+            block,
+            pl.BlockSpec((D, W), lambda b: (0, b)),
+            block,
+            pl.BlockSpec((1, D), lambda b: (0, 0)),
+        ],
+        out_shape=[
+            low,
+            low,
+            jax.ShapeDtypeStruct((D, tokens), BF),
+            low,
+            jax.ShapeDtypeStruct((1, D), F32),
+        ],
         compiler_params=params(),
         cost_estimate=cost(2 * tokens * D * D, 2 * 8 * tokens * D),
         name="after_mlp",
@@ -1037,7 +1061,9 @@
     state_in,
     apart,
     gain,
-    weight,
+    weight_query,
+    weight_key,
+    more_weight,
     wso0,
     wso1,
     grad_tokens,
@@ -1077,7 +1103,7 @@
         coming = grad_state[...]
         keep = forget[...]
         low = ((1.0 - keep) * coming).astype(BF)
-        branch[...] = low
+        branch[...] = low.T
         gate = (coming * apart[...].astype(F32) * keep * (1.0 - keep)).astype(BF)
         gate_part[0] = gate[:, :width]
         gate_part[1] = gate[:, width:]
@@ -1159,10 +1185,12 @@
         return carry
 
     lax.fori_loop(0, local, head, 0)
-    for which in range(4):
-        grad_normed[...] += nt(
-            grad_states[which], weight[:, which * width : (which + 1) * width]
-        )
+    grad_normed[...] += (
+        nt(grad_states[0], weight_query[...])
+        + nt(grad_states[1], weight_key[...])
+        + nt(grad_states[2], more_weight[:, :width])
+        + nt(grad_states[3], more_weight[:, width:])
+    )
 
     @pl.when(half == 1)
     def finish():
@@ -1197,12 +1225,11 @@
     apart,
     gain,
     weights,
-    out_weights,
+    more_weights,
 ):
     blocks = query.shape[0] // W
     heads = D // HEAD
-    width = weights.shape[1]
-    half_width = width // 4
+    half_width = D // 2
 
     def rev(b):
         return blocks - 1 - b
@@ -1222,14 +1249,16 @@
             + [whole] * 3
             + [
                 once((1, D), lambda b, t, s: (0, 0)),
-                pl.BlockSpec((D, width), lambda b, t, s: (t, 0)),
-                once((D, half_width), lambda b, t, s: (0, 0)),
-                once((D, half_width), lambda b, t, s: (1, 0)),
+                pl.BlockSpec((D, half_width), lambda b, t, s: (t, 3)),
+                pl.BlockSpec((D, half_width), lambda b, t, s: (t, 4)),
+                pl.BlockSpec((D, 2 * half_width), lambda b, t, s: (t, 0)),
+                once((D, half_width), lambda b, t, s: (0, 2)),
+                once((D, half_width), lambda b, t, s: (1, 2)),
             ],
             out_specs=[
                 pl.BlockSpec((3, W, half_width), lambda b, t, s: (0, rev(b), t)),
                 pl.BlockSpec((4, S, half_width), lambda b, t, s: (0, rev(b), t)),
-                whole,
+                pl.BlockSpec((D, S), lambda b, t, s: (0, rev(b))),
                 pl.BlockSpec((S, D), lambda b, t, s: (0, 0)),
                 fixed_row,
                 fixed_row,
@@ -1250,7 +1279,7 @@
         out_shape=[
             jax.ShapeDtypeStruct((3, blocks * W, D), BF),
             jax.ShapeDtypeStruct((4, blocks * W, D), BF),
-            jax.ShapeDtypeStruct((blocks * W, D), BF),
+            jax.ShapeDtypeStruct((D, blocks * W), BF),
             jax.ShapeDtypeStruct((S, D), BF),
             jax.ShapeDtypeStruct((1, D), F32),
             jax.ShapeDtypeStruct((1, D), F32),
@@ -1277,36 +1306,76 @@
         apart,
         gain,
         weights,
-        out_weights,
-        out_weights,
-    )
-
-
-def weight_grad_kernel(left, right, out, turned):
-    @pl.when(pl.program_id(0) == 0)
-    def start():
-        turned[...] = left[...].T
-
-    out[...] = nn(turned[...], right[0]).astype(BF)
-
-
-def weight_grads(left, rights):
-    many, tokens, unused = rights.shape
+        weights,
+        more_weights,
+        more_weights,
+        more_weights,
+    )
+
+
+def whole_grad_kernel(turned, right, into, out):
+    out[...] = nn(turned[...], right[...]).astype(BF)
+
+
+def whole_weight_grad(turned, right, into):
+    tokens = right.shape[0]
     width = D // 2
+    last = into.shape[1] // width - 1
     return pl.pallas_call(
-        weight_grad_kernel,
-        grid=(2 * many,),
+        whole_grad_kernel,
+        grid=(2,),
         in_specs=[
-            once((tokens, D), lambda g: (0, 0)),
-            pl.BlockSpec((1, tokens, width), lambda g: (g // 2, 0, g % 2)),
+            once((D, tokens), lambda g: (0, 0)),
+            pl.BlockSpec((tokens, width), lambda g: (0, g)),
+            pl.BlockSpec(memory_space=pl.ANY),
         ],
-        out_specs=pl.BlockSpec((D, width), lambda g: (g % 2, g // 2)),
-        out_shape=jax.ShapeDtypeStruct((2 * D, many * width), BF),
-        scratch_shapes=[pltpu.VMEM((D, tokens), BF)],
+        out_specs=pl.BlockSpec((D, width), lambda g: (g, last)),
+        out_shape=jax.ShapeDtypeStruct(into.shape, BF),
+        input_output_aliases={2: 0},
+        compiler_params=params(),
+        cost_estimate=cost(2 * tokens * D * D, 2 * (tokens * D + 2 * D * D)),
+        name="whole_weight_grad",
+    )(turned, right, into)
+
+
+def weight_grad_kernel(groups, core, turned, right, *rest):
+    keep, send = rest[-2:]
+    grads = nn(turned[...], right[0]).astype(BF)
+    group = turned.shape[0] // groups
+    grads = grads.reshape(groups // 2, 2, group, grads.shape[1])
+    shape = keep.shape
+    low = grads[:, 0].reshape(shape)
+    high = grads[:, 1].reshape(shape)
+    mine = core[0] == 0
+    keep[...] = jnp.where(mine, low, high)
+    send[...] = jnp.where(mine, high, low)
+
+
+def weight_grads(dp, core, turned, rights, first=0, many=1, across=0, at=0, into=None):
+    tokens = rights.shape[1]
+    width = D // 2
+    across = across or many
+    out = jax.ShapeDtypeStruct((D, across * width), BF)
+    tile = pl.BlockSpec((D // 2, width), lambda g, s: (g % 2, at + g // 2))
+    into = into or ()
+    return pl.pallas_call(
+        functools.partial(weight_grad_kernel, dp),
+        grid_spec=pltpu.PrefetchScalarGridSpec(
+            num_scalar_prefetch=1,
+            grid=(2 * many,),
+            in_specs=[
+                once((D, tokens), lambda g, s: (0, 0)),
+                pl.BlockSpec((1, tokens, width), lambda g, s: (first + g // 2, 0, g % 2)),
+            ]
+            + [pl.BlockSpec(memory_space=pl.ANY)] * len(into),
+            out_specs=[tile, tile],
+        ),
+        out_shape=[out, out],
+        input_output_aliases={3 + i: i for i in range(len(into))},
         compiler_params=params(),
         cost_estimate=cost(2 * tokens * D * D * many, 2 * (tokens * D + 2 * many * D * D)),
         name="weight_grads",
-    )(left, rights)
+    )(core, turned, rights, *into)
 
 
 def token_grad_kernel(grads, w0, w1, rows, grad_middle, gain, out, grad_gain):
@@ -1338,7 +1407,7 @@
 
 def token_grad(grads, weights, rows, grad_middle, gain):
     tokens = rows.shape[0]
-    width = weights.shape[1]
+    width = 3 * D // 2
     block = pl.BlockSpec((W, D), lambda b: (b, 0))
     return pl.pallas_call(
         token_grad_kernel,
@@ -1365,6 +1434,102 @@
 
 def scatter(total):
     return lax.psum_scatter(total, ("tensor", "dp"), scatter_dimension=0, tiled=True)
+
+
+def axes_of(dp):
+    return ["tensor"] + list(reversed(range(dp.bit_length() - 1)))
+
+
+def side_of(axis):
+    if axis == "tensor":
+        return lax.axis_index("tensor")
+    return (lax.axis_index("dp") >> axis) & 1
+
+
+def trade(values, axis, dp):
+    if axis == "tensor":
+        return lax.ppermute(values, "tensor", [(0, 1), (1, 0)])
+    return lax.ppermute(values, "dp", [(i, i ^ (1 << axis)) for i in range(dp)])
+
+
+def order_of(dp, turn):
+    bits = dp.bit_length() - 1
+    middle = ["tensor"] + ([1] if bits > 1 else [])
+    if turn:
+        middle = middle[::-1]
+    return ([0] if bits else []) + middle + list(reversed(range(2, bits)))
+
+
+class Halving:
+    def __init__(self, keep, send, dp, turn):
+        self.dp = dp
+        self.axes = axes_of(dp)
+        self.left = order_of(dp, turn)
+        self.rest = 2 * keep.shape[0] >> len(self.axes)
+        self.keep = keep
+        self.sent = send
+
+    def send(self):
+        axis = self.left[0]
+        where = self.axes.index(axis)
+        columns = self.part.shape[1]
+        many = len(self.axes) - where - 1
+        pairs = self.part.reshape(1 << where, 2, self.rest << many, columns)
+        side = side_of(axis)
+        self.sent = lax.dynamic_index_in_dim(pairs, 1 - side, 1, keepdims=False)
+        self.keep = lax.dynamic_index_in_dim(pairs, side, 1, keepdims=False)
+        return self.sent
+
+    def go(self):
+        self.come = trade(self.sent, self.left[0], self.dp)
+
+    def add(self, earlier=None):
+        come = self.come if earlier is None else after(self.come, earlier)
+        total = (self.keep.astype(F32) + come.astype(F32)).astype(BF)
+        self.part = total.reshape(-1, total.shape[-1])
+        self.axes.remove(self.left.pop(0))
+        if self.left:
+            self.send()
+
+
+def finish(many):
+    while any(one.left for one in many):
+        active = [one for one in many if one.left]
+        for one in active:
+            one.go()
+        for one, come in zip(active, lax.optimization_barrier([one.come for one in active])):
+            one.come = come
+            one.add()
+    return [one.part for one in many]
+
+
+def split_core(total, dp):
+    groups = total.reshape(dp, 2, total.shape[0] // (2 * dp), total.shape[1])
+    side = side_of(0)
+    keep = lax.dynamic_index_in_dim(groups, side, 1, keepdims=False)
+    send = lax.dynamic_index_in_dim(groups, 1 - side, 1, keepdims=False)
+    return [one.reshape(total.shape[0] // 2, total.shape[1]) for one in (keep, send)]
+
+
+def gather_steps(local, dp, turn, earlier):
+    axes = axes_of(dp)
+    done = []
+    part = local
+    for axis in reversed(order_of(dp, turn)):
+        if axis == "tensor":
+            part = after(part, earlier)
+        come = trade(part, axis, dp)
+        low = side_of(axis) == 0
+        done = [one for one in axes if one == axis or one in done]
+        lead = 1 << done.index(axis)
+        pair = [jnp.where(low, part, come), jnp.where(low, come, part)]
+        pair = [one.reshape(lead, part.shape[0] // lead, part.shape[1]) for one in pair]
+        part = jnp.stack(pair, axis=1).reshape(2 * part.shape[0], part.shape[1])
+    return part
+
+
+def after(values, earlier):
+    return lax.optimization_barrier((values, earlier))[0]
 
 
 def whole_sequence_body(
@@ -1397,19 +1562,22 @@
     across = w_up.shape[1] // units
     swap = [(0, 1), (1, 0)]
 
-    def bring(pair):
+    def other_half(pair):
+        return lax.ppermute(jnp.where(first, pair[1, 0], pair[0, 0]), "tensor", swap)
+
+    def bring(pair, come):
         keep = jnp.where(first, pair[0, 0], pair[1, 0])
-        send = jnp.where(first, pair[1, 0], pair[0, 0])
-        come = lax.ppermute(send, "tensor", swap)
         top = jnp.where(first, keep, come)
         low = jnp.where(first, come, keep)
         return jnp.concatenate([top, low], axis=1).reshape(NB * W, D)
 
-    def give(rows):
+    def give(rows, later=None):
         halves = rows.reshape(NB, 2, HALF, D)
         keep = jnp.where(first, halves[:, 0], halves[:, 1])
         send = jnp.where(first, halves[:, 1], halves[:, 0])
         come = lax.ppermute(send, "tensor", swap)
+        if later is not None:
+            come = after(come, later)
         return jnp.stack([jnp.where(first, keep, come), jnp.where(first, come, keep)])[:, None]
 
     def split_init(values):
@@ -1421,38 +1589,37 @@
         [split_init(state_init), jnp.pad(gains, ((0, local_rows - 4), (0, 128 - local_rows)))],
         axis=1,
     )
-    full_qkv = gather(jnp.concatenate([w_query, w_key, w_value, small], axis=1))
-    full_small = full_qkv[:, 3 * width :]
-    full_state = gather(
-        jnp.concatenate([w_state_query, w_state_key, w_state_value, w_gate], axis=1)
-    )
-    full_outs = gather(jnp.concatenate([w_state_out.T, w_out.T], axis=1))
-    up_parts = w_up.reshape(local_rows, across, 1, units)
-    down_parts = w_down.T.reshape(local_rows, across, 1, units)
-    full_mlp = gather(
-        jnp.concatenate([up_parts, down_parts], axis=2).reshape(local_rows, 2 * across * units)
-    )
+    full_qkv = gather(
+        jnp.concatenate([w_query, w_key, w_value, w_state_query, w_state_key, small], axis=1)
+    )
+    full_small = full_qkv[:, 5 * width :]
+    turned_down = w_down.T
+    late = []
+    for unit in range(0, across * units, units):
+        late += [w_up[:, unit : unit + units], turned_down[:, unit : unit + units]]
+    late = jnp.concatenate(late + [w_out.T], axis=1)
+    rows = bring(tokens_in, other_half(tokens_in))
+    full_state1 = gather_steps(
+        jnp.concatenate([w_state_value, w_gate, w_state_out.T], axis=1), dp, False, (rows, late)
+    )
+    full_late = gather(after(late, (full_qkv, full_state1)))
     side = width // 2
     init = full_small[:, :side].reshape(2, dp, 2, local_rows // 2, side)
     init = jnp.transpose(init, (1, 3, 0, 2, 4)).reshape(S, D)
     gains = full_small[:D, side:].reshape(dp, local_rows, 128)[:, :4, :local_rows]
     gains = jnp.transpose(gains, (1, 0, 2)).reshape(4, 1, D).astype(F32)
 
-    rows = bring(tokens_in)
-    cot = bring(cotangent)
+    cot_half = other_half(after(cotangent, rows))
     starts = jnp.where(first, piece_starts[0, 0], piece_starts[1, 0])
     flags = jnp.any(
         starts[:, None] == PIECE * jnp.arange(NB * W // PIECE, dtype=jnp.int32)[None], axis=0
     ).astype(jnp.int32)
 
-    weights_qkv = full_qkv[:, : 3 * width]
-    weights_so = full_outs[:, :width]
-    weights_out = full_outs[:, width:]
-    normed, query, key, value = project(rows, gains[0], weights_qkv)
+    turned, query, key, value = project(rows, gains[0], full_qkv)
     (
         token_mixed,
         state_mixed,
-        state_normed,
+        state_turned,
         state_query,
         state_key,
         state_value,
@@ -1460,15 +1627,18 @@
         forget,
         apart,
         totals,
-    ) = forward(flags, query, key, value, init, gains[2], gains[3], full_state, weights_so)
+    ) = forward(flags, query, key, value, init, gains[2], gains[3], full_qkv, full_state1)
+    cot = bring(cotangent, after(cot_half, token_mixed))
     middle, mlp_in, mlp_turned, cot_turned = middle_rows(
-        rows, token_mixed, weights_out, gains[1], cot
-    )
-    mlp_out, grad_mlp_in, grad_mlp_w = mlp(mlp_in, mlp_turned, cot, cot_turned, full_mlp)
-    output, grad_middle, grad_mixed, grad_gain_mlp = after_mlp(
-        middle, mlp_out, grad_mlp_in, cot, gains[1], weights_out
-    )
-    part_mlp = scatter(grad_mlp_w)
+        rows, token_mixed, full_late, gains[1], cot
+    )
+    mlp_out, grad_mlp_in, grad_mlp_w = mlp(mlp_in, mlp_turned, cot, cot_turned, full_late)
+    output, grad_middle, middle_turned, grad_mixed, grad_gain_mlp = after_mlp(
+        middle, mlp_out, grad_mlp_in, cot, gains[1], full_late
+    )
+    grads_late = whole_weight_grad(middle_turned, token_mixed, grad_mlp_w)
+    part_late = scatter(grads_late)
+    core = (side_of(0) & 1).astype(jnp.int32).reshape(1)
     grad_tok, grad_sta, branch, grad_init, grad_gain_state, grad_bias = backward(
         flags,
         query,
@@ -1479,21 +1649,42 @@
         state_value,
         token_mixed,
         state_mixed,
-        grad_mixed,
+        after(grad_mixed, grads_late),
         totals,
         forget,
         state_in,
         apart,
         gains[2],
-        full_state,
-        weights_so,
-    )
-    part_out = scatter(weight_grads(grad_middle, token_mixed[None]))
-    part_so = scatter(weight_grads(branch, state_mixed[None]))
-    part_state = scatter(weight_grads(state_normed, grad_sta))
-    part_qkv = scatter(weight_grads(normed, grad_tok))
-    grad_in, grad_gain_tokens = token_grad(grad_tok, weights_qkv, rows, grad_middle, gains[0])
-
+        full_qkv,
+        full_state1,
+    )
+    given_output = give(output, grad_tok)
+
+    a = Halving(*weight_grads(dp, core, state_turned, after(grad_sta, given_output), 0, 2), dp, False)
+    a.go()
+    b = Halving(*weight_grads(dp, core, state_turned, after(grad_sta, a.sent), 2, 2), dp, True)
+    a.add(b.keep)
+    a.go()
+    b.go()
+    c = Halving(*weight_grads(dp, core, turned, after(grad_tok, (a.sent, b.sent)), 1, 2), dp, False)
+    b.add(c.keep)
+    b.go()
+    c.go()
+    grads_q = weight_grads(dp, core, turned, after(grad_tok, (b.sent, c.sent)), 0, 1, 2, 0)
+    c.add(grads_q)
+    c.go()
+    d = Halving(
+        *weight_grads(dp, core, after(branch, c.sent), state_mixed[None], 0, 1, 2, 1, grads_q),
+        dp,
+        True,
+    )
+    d.go()
+    grad_in, grad_gain_tokens = token_grad(
+        after(grad_tok, (d.sent, part_late)), full_qkv, rows, grad_middle, gains[0]
+    )
+    a.add(grad_in)
+    d.add(grad_in)
+    b.add(grad_in)
     init_parts = jnp.transpose(
         grad_init.reshape(dp, local_rows // 2, 2, 2, side), (2, 0, 3, 1, 4)
     ).reshape(2 * D, side)
@@ -1505,40 +1696,47 @@
         ((0, 0), (0, local_rows - 4), (0, 128 - local_rows)),
     ).reshape(D, 128)
     gain_parts = jnp.concatenate([gain_parts, gain_parts], axis=0).astype(BF)
-    part_small = scatter(jnp.concatenate([init_parts, gain_parts], axis=1)).astype(F32)
-
+    e = Halving(*split_core(jnp.concatenate([init_parts, gain_parts], axis=1), dp), dp, True)
+    given_grad = give(grad_in)
+    part_rest, part_kv, part_sqk, part_svg, part_small = [
+        one.astype(F32) for one in finish([d, c, a, b, e])
+    ]
+    part_so = part_rest[:, width:]
     part_init = part_small[:, :side]
     part_init = jnp.concatenate(
         [part_init[: local_rows // 2], part_init[local_rows // 2 :]], axis=1
     )
     part_gains = part_small[:4, side : side + local_rows]
-    part_mlp = part_mlp.astype(F32).reshape(local_rows, across, 2, units)
-    part_qkv = part_qkv.astype(F32)
-    part_state = part_state.astype(F32)
+    part_late = part_late.astype(F32)
+    part_up = [part_late[:, 2 * i * units : (2 * i + 1) * units] for i in range(across)]
+    part_down = [part_late[:, (2 * i + 1) * units : (2 * i + 2) * units] for i in range(across)]
+    part_sqk = part_sqk.astype(F32)
+    part_svg = part_svg.astype(F32)
     return (
-        give(output),
-        give(grad_in),
+        given_output,
+        given_grad,
         part_gains[0],
         part_gains[1],
         part_gains[2],
         part_gains[3],
-        part_qkv[:, :width],
-        part_qkv[:, width : 2 * width],
-        part_qkv[:, 2 * width :],
-        part_out.astype(F32).T,
-        part_state[:, :width],
-        part_state[:, width : 2 * width],
-        part_state[:, 2 * width : 3 * width],
-        part_so.astype(F32).T,
-        part_state[:, 3 * width :],
-        part_mlp[:, :, 0].reshape(local_rows, across * units),
-        part_mlp[:, :, 1].reshape(local_rows, across * units).T,
+        part_rest[:, :width],
+        part_kv[:, :width],
+        part_kv[:, width:],
+        part_late[:, 2 * across * units :].T,
+        part_sqk[:, :width],
+        part_sqk[:, width:],
+        part_svg[:, :width],
+        part_so.T,
+        part_svg[:, width:],
+        jnp.concatenate(part_up, axis=1),
+        jnp.concatenate([one.T for one in part_down], axis=0),
         part_init,
     )
 
 
 def solution(mesh):
-    one_each = mesh.shape["tensor"] == MICRO
+    dp = mesh.shape["dp"]
+    one_each = mesh.shape["tensor"] == MICRO and dp > 1 and dp & (dp - 1) == 0
     return jax.shard_map(
         whole_sequence_body if one_each else generic_body,
         mesh=mesh,

time: 1540 us -> 875 us (0.57)
  waiting for transfers between devices: 913 us -> 189 us
  starting transfers between devices: 6.6 us -> 39.1 us
  other arithmetic: 35 us -> 60.8 us
    reduce_scatter x6 -> x1, waiting for transfers between devices: 673 us -> 0.01 us  [scatter(): lax.psum_scatter(total, ('tensor', 'dp'), scatter_dimension=0, tiled=True)]
    all_gather x4 -> x2, waiting for transfers between devices: 77 us -> 0.01 us  [gather(): return lax.all_gather(local, ('tensor', 'dp'), axis=0, tiled=True)]
    ppermute x2 -> x32, waiting for transfers between devices: 106 us -> 177 us  [the longest x24 98.7 us: trade(): return lax.ppermute(values, 'dp', [(i, i ^ 1 << axis) for i in range(dp)])]
    ppermute x2, waiting for transfers between devices: 57.3 us -> 11.8 us  [give(): come = lax.ppermute(send, 'tensor', swap)]
    ppermute x2 -> x32, starting transfers between devices: 3.84 us -> 38.1 us  [the longest x24 25.1 us: trade(): return lax.ppermute(values, 'dp', [(i, i ^ 1 << axis) for i in range(dp)])]
    convert_element_type x1 -> x24, other arithmetic: 0.81 us -> 18 us  [the longest x20 17.8 us: add(): total = (self.keep.astype(F32) + come.astype(F32)).astype(BF)]
    pallas_call x4 -> x6, Pallas kernels: 63 us -> 66.3 us  [the longest x5 57.6 us: weight_grads(): pl.pallas_call(functools.partial(weight_grad_kernel, dp), grid_spec=pltpu...]
  transfers between devices with their start and end apart: 14 -> 37, of which waited for: 12 -> 20; matrix products, arithmetic and copies ran while one was open for 4% -> 9% of each run, Pallas kernels for 14% -> 42%
where the time goes in v2:
time: 875 us; the launch traced here: 869 us
  Pallas kernels  535 us (61%)
  waiting for transfers between devices  189 us (22%)
  other arithmetic  60.8 us (7%)
  starting transfers between devices  39.1 us (4%)
  local copies, waits for them, and re-layouts  29.9 us (3%)
  between operations  15 us (2%)
    pallas_call x1, Pallas kernels, backward(): pl.pallas_call(backward_kernel, grid_spec=pltpu.PrefetchScalarGridSpec(nu...  154 us
    pallas_call x1, Pallas kernels, mlp(): pl.pallas_call(mlp_kernel, grid=(2 * across,), in_specs=[rows, turned, ro...  128 us
    pallas_call x1, Pallas kernels, forward(): pl.pallas_call(forward_kernel, grid_spec=pltpu.PrefetchScalarGridSpec(num...  115 us
    ppermute x24, waiting for transfers between devices, trade(): return lax.ppermute(values, 'dp', [(i, i ^ 1 << axis) for i in range(dp)])  98.7 us
    ppermute x6, waiting for transfers between devices, trade(): return lax.ppermute(values, 'tensor', [(0, 1), (1, 0)])  75.2 us
    pallas_call x5, Pallas kernels, weight_grads(): pl.pallas_call(functools.partial(weight_grad_kernel, dp), grid_spec=pltpu...  57.6 us
    ppermute x24, starting transfers between devices, trade(): return lax.ppermute(values, 'dp', [(i, i ^ 1 << axis) for i in range(dp)])  25.1 us
    pallas_call x1, Pallas kernels, token_grad(): pl.pallas_call(token_grad_kernel, grid=(tokens // W,), in_specs=[pl.Block...  21.9 us
  transfers between devices with their start and end apart: 37, of which 20 were waited for; matrix products, arithmetic and copies ran while one was open for 9% of the time, Pallas kernels for 42%

profile of v2, /device:TPU:0, one launch (start us, length us, event | category | flops | bytes accessed | tf_op | source)
XLA Modules:
  0.0 869.1 jit_solution(731934617276459738)
XLA Ops:
  27.5 24.9 %collective-permute-done.2 = bf16[128,1536]{1,0:T(8,128)(2,1)S(1)} collective-permute-done((bf16[128,1536]{1,0:T(8,128)(2,1)S(1)}, bf16[128,1536]{1,0:T(8,128)(2,1)S(1)}, u32[]{:S(2)}, u32[]{:S(2)}) %collective-permute-start.2) | collective-permute-done | bytes 393248 | tf_op jit(solution)/shard_map/ppermute | solution.py:1452
  56.5 20.1 %collective-permute-done.3 = bf16[256,1536]{1,0:T(8,128)(2,1)} collective-permute-done((bf16[256,1536]{1,0:T(8,128)(2,1)S(1)}, bf16[256,1536]{1,0:T(8,128)(2,1)}, u32[]{:S(2)}, u32[]{:S(2)}) %collective-permute-start.3) | collective-permute-done | bytes 786464 | tf_op jit(solution)/shard_map/ppermute | solution.py:1452
  78.2 3.4 collective-permute-done
  87.5 55.0 %collective-permute-done.4 = bf16[512,1536]{1,0:T(8,128)(2,1)S(1)} collective-permute-done((bf16[512,1536]{1,0:T(8,128)(2,1)S(1)}, bf16[512,1536]{1,0:T(8,128)(2,1)S(1)}, u32[]{:S(2)}, u32[]{:S(2)}) %collective-permute-start.4) | collective-permute-done | bytes 1572896 | tf_op jit(solution)/shard_map/ppermute | solution.py:1451
  143.3 5.9 collective-permute-done.5
  151.7 3.2 pad_maximum_fusion
  155.6 3.9 select_bitcast_fusion.2
  168.2 19.0 %project.1 = (bf16[1024,2048]{1,0:T(8,128)(2,1)}, bf16[2048,1024]{1,0:T(8,128)(2,1)}, bf16[2048,1024]{1,0:T(8,128)(2,1)}, bf16[2048,1024]{1,0:T(8,128)(2,1)}) custom-call(bf16[2048,1024]{1,0:T(8,128)(2,1)} %bitcast.309, f32[1,1024]{1,0:T(1,128)} %squeeze.138.gain, ...), custom_call_target="tpu_custom_call" | custom-call | flops 12884901888 | bytes 27262976 | tf_op jit(solution)/shard_map/project/pallas_call | solution.py:675
  187.2 114.7 %forward.1 = (bf16[2048,1024]{1,0:T(8,128)(2,1)}, bf16[2048,1024]{1,0:T(8,128)(2,1)}, bf16[1024,2048]{1,0:T(8,128)(2,1)}, bf16[2048,1024]{1,0:T(8,128)(2,1)}, bf...) custom-call(s32[8]{0:T(128)} %convert_element_type.468.flags, ...), custom_call_target="tpu_custom_call" | custom-call | flops 41999998976 | bytes 100000000 | tf_op jit(solution)/shard_map/forward/pallas_call | solution.py:815
  302.6 3.2 bitcast_select_fusion.5
  308.2 14.3 %middle.1 = (f32[2048,1024]{1,0:T(8,128)}, bf16[2048,1024]{1,0:T(8,128)(2,1)}, bf16[1024,2048]{1,0:T(8,128)(2,1)}, bf16[1024,2048]{1,0:T(8,128)(2,1)}) custom-call(bf16[2048,1024]{1,0:T(8,128)(2,1)} %bitcast.310, bf16[2048,1024]{1,0:T(8,128)(2,1)} %get-tuple-element.102.mixed.right.token_mixed, ...), custom_call_target="tpu_custom_call" | custom-call | flops 4294967296 | bytes 33554432 | tf_op jit(solution)/shard_map/middle/pallas_call | solution.py:891
  322.6 127.5 %mlp.1 = (bf16[2048,1024]{1,0:T(8,128)(2,1)}, bf16[2048,1024]{1,0:T(8,128)(2,1)}, bf16[2048,4608]{1,0:T(8,128)(2,1)}) custom-call(bf16[2048,1024]{1,0:T(8,128)(2,1)} %get-tuple-element.107.mlp_in, bf16[1024,2048]{1,0:T(8,128)(2,1)} %get-tuple-element.108.mlp_turned, bf16[2048,1024]{1,0:T(8,128)(2,1)} %bitcast.307, ...), custom_call_target="tpu_custom_call" | custom-call | flops 102999998464 | bytes 60000000 | tf_op jit(solution)/shard_map/mlp/pallas_call | solution.py:965
  450.1 18.0 %after_mlp.1 = (bf16[2048,1024]{1,0:T(8,128)(2,1)}, bf16[2048,1024]{1,0:T(8,128)(2,1)}, bf16[1024,2048]{1,0:T(8,128)(2,1)}, bf16[2048,1024]{1,0:T(8,128)(2,1)}, f32[1,1024]{1,0:T(1,128)}) custom-call(f32[2048,1024]{1,0:T(8,128)} %get-tuple-element.106.middle, bf16[2048,1024]{1,0:T(8,128)(2,1)} %get-tuple-element.110.mlp_out, ...), custom_call_target="tpu_custom_call" | custom-call | flops 4294967296 | bytes 33554432 | tf_op jit(solution)/shard_map/after_mlp/pallas_call | solution.py:1014
  468.1 8.7 whole_weight_grad.1
  479.4 153.5 %backward.1 = (bf16[3,2048,1024]{2,1,0:T(8,128)(2,1)}, bf16[4,2048,1024]{2,1,0:T(8,128)(2,1)}, bf16[1024,2048]{1,0:T(8,128)(2,1)}, bf16[512,1024]{1,0:T(8,128)(2...) custom-call(s32[8]{0:T(128)} %convert_element_type.468.flags, bf16[2048,1024]{1,0:T(8,128)(2,1)} %get-tuple-element.98.query, ...), custom_call_target="tpu_custom_call" | custom-call | flops 70000001024 | bytes 100000000 | tf_op jit(solution)/shard_map/backward/pallas_call | solution.py:1241
  632.9 3.3 fusion.6
  638.6 13.4 %weight_grads.5 = (bf16[1024,1024]{1,0:T(8,128)(2,1)}, bf16[1024,1024]{1,0:T(8,128)(2,1)}) custom-call(s32[1]{0:T(128)} %bitcast.39.core, bf16[1024,2048]{1,0:T(8,128)(2,1)} %get-tuple-element.129.turned, bf16[4,2048,1024]{2,1,0:T(8,128)(2,1)} %get-tuple-element.134.right), custom_call_target="tpu_custom_call" | custom-call | flops 8589934592 | bytes 12582912 | tf_op jit(solution)/shard_map/weight_grads/pallas_call | solution.py:1361
  652.0 13.7 %weight_grads.6 = (bf16[1024,1024]{1,0:T(8,128)(2,1)}, bf16[1024,1024]{1,0:T(8,128)(2,1)}) custom-call(s32[1]{0:T(128)} %bitcast.39.core, bf16[1024,2048]{1,0:T(8,128)(2,1)} %get-tuple-element.129.turned, bf16[4,2048,1024]{2,1,0:T(8,128)(2,1)} %get-tuple-element.134.right), custom_call_target="tpu_custom_call" | custom-call | flops 8589934592 | bytes 12582912 | tf_op jit(solution)/shard_map/weight_grads/pallas_call | solution.py:1361
  671.2 13.5 %weight_grads.7 = (bf16[1024,1024]{1,0:T(8,128)(2,1)}, bf16[1024,1024]{1,0:T(8,128)(2,1)}) custom-call(s32[1]{0:T(128)} %bitcast.39.core, bf16[1024,2048]{1,0:T(8,128)(2,1)} %get-tuple-element.128.turned, bf16[3,2048,1024]{2,1,0:T(8,128)(2,1)} %get-tuple-element.148.right.grads), custom_call_target="tpu_custom_call" | custom-call | flops 8589934592 | bytes 12582912 | tf_op jit(solution)/shard_map/weight_grads/pallas_call | solution.py:1361
  689.6 8.5 weight_grads.8
  702.5 8.6 weight_grads.9
  717.2 21.9 %token_grad.1 = (bf16[2048,1024]{1,0:T(8,128)(2,1)}, f32[1,1024]{1,0:T(1,128)}) custom-call(bf16[3,2048,1024]{2,1,0:T(8,128)(2,1)} %get-tuple-element.148.right.grads, bf16[2048,2944]{1,0:T(8,128)(2,1)} %all-gather.3.cloned.1.call-done.w0.w1.query0.query1.key0.key1.weight_query.weight_key, ...), custom_call_target="tpu_custom_call" | custom-call | flops 12884901888 | bytes 25165824 | tf_op jit(solution)/shard_map/token_grad/pallas_call | solution.py:1412
  753.9 10.1 %collective-permute-done.14 = bf16[1,512,1024]{2,1,0:T(8,128)(2,1)} collective-permute-done((bf16[1,512,1024]{2,1,0:T(8,128)(2,1)}, bf16[1,512,1024]{2,1,0:T(8,128)(2,1)}, u32[]{:S(2)}, u32[]{:S(2)}) %collective-permute-start.14) | collective-permute-done | bytes 1048608 | tf_op jit(solution)/shard_map/ppermute | solution.py:1451
  764.0 10.0 %collective-permute-done.18 = bf16[1,256,1024]{2,1,0:T(8,128)(2,1)S(1)} collective-permute-done((bf16[1,256,1024]{2,1,0:T(8,128)(2,1)S(1)}, bf16[1,256,1024]{2,1,0:T(8,128)(2,1)S(1)}, u32[]{:S(2)}, u32[]{:S(2)}) %collective-permute-start.18) | collective-permute-done | bytes 524320 | tf_op jit(solution)/shard_map/ppermute | solution.py:1451
  774.0 6.0 collective-permute-done.16
  791.0 8.6 collective-permute-done.23
  799.6 5.5 collective-permute-done.22
  807.0 3.2 collective-permute-start.26
  815.6 8.1 collective-permute-done.27
  823.7 4.8 collective-permute-done.26
  828.5 4.3 collective-permute-done.25
  847.6 11.8 %collective-permute-done.11 = bf16[4,256,1024]{2,1,0:T(8,128)(2,1)S(1)} collective-permute-done((bf16[4,256,1024]{2,1,0:T(8,128)(2,1)S(1)}, bf16[4,256,1024]{2,1,0:T(8,128)(2,1)S(1)}, u32[]{:S(2)}, u32[]{:S(2)}) %collective-permute-start.11) | collective-permute-done | bytes 2097184 | tf_op jit(solution)/shard_map/ppermute | solution.py:1578
  (224 shorter events, 123.5 us)
Async XLA Ops:
  7.2 147.7 %all-gather.3.cloned.1.call-start = ((), (), s32[]{:S(2)}) async-start(), calls=%async_computation.1 | async-start | bytes 12435456 | tf_op jit(solution)/shard_map/all_gather | solution.py:1432
  13.7 294.5 %all-gather.5.cloned.1.call-start = ((), (), s32[]{:S(2)}) async-start(), calls=%async_computation.2 | async-start | bytes 19464192 | tf_op jit(solution)/shard_map/all_gather | solution.py:1432
  15.3 8.2 collective-permute-start.1
  20.9 60.7 %collective-permute-start = (bf16[4,256,1024]{2,1,0:T(8,128)(2,1)S(1)}, bf16[4,256,1024]{2,1,0:T(8,128)(2,1)}, u32[]{:S(2)}, u32[]{:S(2)}) collective-permute-start(bf16[4,256,1024]{2,1,0:T(8,128)(2,1)S(1)} %select_bitcast_fusion.3), channel_id=1, source_target_pairs={{0,1},{1,0},{2,3},{3,2},{4,5},{5,4},{6,7},{7,6},{8,9},{9,8},{10,11... | collective-permute-start | bytes 6291464 | tf_op jit(solution)/shard_map/ppermute | solution.py:1566
  24.7 27.7 %collective-permute-start.2 = (bf16[128,1536]{1,0:T(8,128)(2,1)S(1)}, bf16[128,1536]{1,0:T(8,128)(2,1)S(1)}, u32[]{:S(2)}, u32[]{:S(2)}) collective-permute-start(bf16[128,1536]{1,0:T(8,128)(2,1)S(1)} %bitcast.358), channel_id=1, source_target_pairs={{0,16},{2,18},{4,20},{6,22},{8,24},{10,26},{12,28},{14,30},{16,0},... | collective-permute-start | bytes 1179656 | tf_op jit(solution)/shard_map/ppermute | solution.py:1452
  52.6 24.1 %collective-permute-start.3 = (bf16[256,1536]{1,0:T(8,128)(2,1)S(1)}, bf16[256,1536]{1,0:T(8,128)(2,1)}, u32[]{:S(2)}, u32[]{:S(2)}) collective-permute-start(bf16[256,1536]{1,0:T(8,128)(2,1)S(1)} %bitcast.346), channel_id=1, source_target_pairs={{0,4},{2,6},{4,0},{6,2},{8,12},{10,14},{12,8},{14,10},{16,20},{18,... | collective-permute-start | bytes 2359304 | tf_op jit(solution)/shard_map/ppermute | solution.py:1452
  86.0 56.5 %collective-permute-start.4 = (bf16[512,1536]{1,0:T(8,128)(2,1)S(1)}, bf16[512,1536]{1,0:T(8,128)(2,1)S(1)}, u32[]{:S(2)}, u32[]{:S(2)}) collective-permute-start(bf16[512,1536]{1,0:T(8,128)(2,1)S(1)} %bitcast.332), channel_id=1, source_target_pairs={{0,1},{1,0},{2,3},{3,2},{4,5},{5,4},{6,7},{7,6},{8,9},{9,8},{10,11... | collective-permute-start | bytes 4718600 | tf_op jit(solution)/shard_map/ppermute | solution.py:1451
  154.9 562.3 %reduce-scatter.2.cloned.1.call-start = ((), (), s32[]{:S(2)}) async-start(), calls=%async_computation.3 | async-start | bytes 19464192 | tf_op jit(solution)/shard_map/reduce_scatter | solution.py:1436
  159.5 142.4 %collective-permute-start.6 = (bf16[4,256,1024]{2,1,0:T(8,128)(2,1)}, bf16[4,256,1024]{2,1,0:T(8,128)(2,1)}, u32[]{:S(2)}, u32[]{:S(2)}) collective-permute-start(bf16[4,256,1024]{2,1,0:T(8,128)(2,1)} %select_bitcast_fusion.2), channel_id=1, source_target_pairs={{0,1},{1,0},{2,3},{3,2},{4,5},{5,4},{6,7},{7,6},{8,9},{9,8},{10,11... | collective-permute-start | bytes 6291464 | tf_op jit(solution)/shard_map/ppermute | solution.py:1566
  479.2 153.7 %collective-permute-start.7 = (bf16[4,256,1024]{2,1,0:T(8,128)(2,1)S(1)}, bf16[4,256,1024]{2,1,0:T(8,128)(2,1)}, u32[]{:S(2)}, u32[]{:S(2)}) collective-permute-start(bf16[4,256,1024]{2,1,0:T(8,128)(2,1)S(1)} %select_bitcast_fusion.1), channel_id=1, source_target_pairs={{0,1},{1,0},{2,3},{3,2},{4,5},{5,4},{6,7},{7,6},{8,9},{9,8},{10,11... | collective-permute-start | bytes 6291464 | tf_op jit(solution)/shard_map/ppermute | solution.py:1578
  652.0 14.2 %collective-permute-start.8 = (bf16[1024,1024]{1,0:T(8,128)(2,1)}, bf16[1024,1024]{1,0:T(8,128)(2,1)}, u32[]{:S(2)}, u32[]{:S(2)}) collective-permute-start(bf16[1024,1024]{1,0:T(8,128)(2,1)} %get-tuple-element.133), channel_id=1, source_target_pairs={{0,2},{2,0},{4,6},{6,4},{8,10},{10,8},{12,14},{14,12},{16,18},{18,... | collective-permute-start | bytes 6291464 | tf_op jit(solution)/shard_map/ppermute | solution.py:1452
  665.7 19.0 %collective-permute-start.10 = (bf16[1024,1024]{1,0:T(8,128)(2,1)}, bf16[1024,1024]{1,0:T(8,128)(2,1)}, u32[]{:S(2)}, u32[]{:S(2)}) collective-permute-start(bf16[1024,1024]{1,0:T(8,128)(2,1)} %get-tuple-element.137), channel_id=1, source_target_pairs={{0,2},{2,0},{4,6},{6,4},{8,10},{10,8},{12,14},{14,12},{16,18},{18,... | collective-permute-start | bytes 6291464 | tf_op jit(solution)/shard_map/ppermute | solution.py:1452
  684.6 13.5 %collective-permute-start.9 = (bf16[1024,1024]{1,0:T(8,128)(2,1)}, bf16[1024,1024]{1,0:T(8,128)(2,1)}, u32[]{:S(2)}, u32[]{:S(2)}) collective-permute-start(bf16[1024,1024]{1,0:T(8,128)(2,1)} %get-tuple-element.140), channel_id=1, source_target_pairs={{0,2},{2,0},{4,6},{6,4},{8,10},{10,8},{12,14},{14,12},{16,18},{18,... | collective-permute-start | bytes 6291464 | tf_op jit(solution)/shard_map/ppermute | solution.py:1452
  711.1 29.3 %collective-permute-start.12 = (bf16[1024,1024]{1,0:T(8,128)(2,1)}, bf16[1024,1024]{1,0:T(8,128)(2,1)}, u32[]{:S(2)}, u32[]{:S(2)}) collective-permute-start(bf16[1024,1024]{1,0:T(8,128)(2,1)} %get-tuple-element.147), channel_id=1, source_target_pairs={{0,2},{2,0},{4,6},{6,4},{8,10},{10,8},{12,14},{14,12},{16,18},{18,... | collective-permute-start | bytes 6291464 | tf_op jit(solution)/shard_map/ppermute | solution.py:1452
  714.6 25.8 %collective-permute-start.17 = (bf16[8,64,1024]{2,1,0:T(8,128)(2,1)}, bf16[8,64,1024]{2,1,0:T(8,128)(2,1)}, u32[]{:S(2)}, u32[]{:S(2)}) collective-permute-start(bf16[8,64,1024]{2,1,0:T(8,128)(2,1)} %dynamic-slice_bitcast_fusion.2), channel_id=1, source_target_pairs={{0,4},{2,6},{4,0},{6,2},{8,12},{10,14},{12,8},{14,10},{16,20},{18,... | collective-permute-start | bytes 3145736 | tf_op jit(solution)/shard_map/ppermute | solution.py:1452
  715.2 34.4 %collective-permute-start.15 = (bf16[1,512,1024]{2,1,0:T(8,128)(2,1)}, bf16[1,512,1024]{2,1,0:T(8,128)(2,1)}, u32[]{:S(2)}, u32[]{:S(2)}) collective-permute-start(bf16[1,512,1024]{2,1,0:T(8,128)(2,1)} %dynamic-slice_bitcast_fusion.3), channel_id=1, source_target_pairs={{0,1},{1,0},{2,3},{3,2},{4,5},{5,4},{6,7},{7,6},{8,9},{9,8},{10,11... | collective-permute-start | bytes 3145736 | tf_op jit(solution)/shard_map/ppermute | solution.py:1451
  717.0 47.0 %collective-permute-start.14 = (bf16[1,512,1024]{2,1,0:T(8,128)(2,1)}, bf16[1,512,1024]{2,1,0:T(8,128)(2,1)}, u32[]{:S(2)}, u32[]{:S(2)}) collective-permute-start(bf16[1,512,1024]{2,1,0:T(8,128)(2,1)} %dynamic-slice_bitcast_fusion.1), channel_id=1, source_target_pairs={{0,1},{1,0},{2,3},{3,2},{4,5},{5,4},{6,7},{7,6},{8,9},{9,8},{10,11... | collective-permute-start | bytes 3145736 | tf_op jit(solution)/shard_map/ppermute | solution.py:1451
  740.3 39.7 %collective-permute-start.19 = (bf16[1024,384]{1,0:T(8,128)(2,1)S(1)}, bf16[1024,384]{1,0:T(8,128)(2,1)S(1)}, u32[]{:S(2)}, u32[]{:S(2)}) collective-permute-start(bf16[1024,384]{1,0:T(8,128)(2,1)S(1)} %bitcast.370), channel_id=1, source_target_pairs={{0,2},{2,0},{4,6},{6,4},{8,10},{10,8},{12,14},{14,12},{16,18},{18,... | collective-permute-start | bytes 2359304 | tf_op jit(solution)/shard_map/ppermute | solution.py:1452
  744.3 35.7 %collective-permute-start.13 = (bf16[8,64,1024]{2,1,0:T(8,128)(2,1)S(1)}, bf16[8,64,1024]{2,1,0:T(8,128)(2,1)S(1)}, u32[]{:S(2)}, u32[]{:S(2)}) collective-permute-start(bf16[8,64,1024]{2,1,0:T(8,128)(2,1)S(1)} %dynamic-slice_bitcast_fusion), channel_id=1, source_target_pairs={{0,4},{2,6},{4,0},{6,2},{8,12},{10,14},{12,8},{14,10},{16,20},{18,... | collective-permute-start | bytes 3145736 | tf_op jit(solution)/shard_map/ppermute | solution.py:1452
  747.5 26.5 %collective-permute-start.18 = (bf16[1,256,1024]{2,1,0:T(8,128)(2,1)S(1)}, bf16[1,256,1024]{2,1,0:T(8,128)(2,1)S(1)}, u32[]{:S(2)}, u32[]{:S(2)}) collective-permute-start(bf16[1,256,1024]{2,1,0:T(8,128)(2,1)S(1)} %dynamic-slice_bitcast_fusion.6), channel_id=1, source_target_pairs={{0,1},{1,0},{2,3},{3,2},{4,5},{5,4},{6,7},{7,6},{8,9},{9,8},{10,11... | collective-permute-start | bytes 1572872 | tf_op jit(solution)/shard_map/ppermute | solution.py:1451
  751.4 28.6 %collective-permute-start.16 = (bf16[4,64,1024]{2,1,0:T(8,128)(2,1)S(1)}, bf16[4,64,1024]{2,1,0:T(8,128)(2,1)S(1)}, u32[]{:S(2)}, u32[]{:S(2)}) collective-permute-start(bf16[4,64,1024]{2,1,0:T(8,128)(2,1)S(1)} %dynamic-slice_bitcast_fusion.7), channel_id=1, source_target_pairs={{0,4},{2,6},{4,0},{6,2},{8,12},{10,14},{12,8},{14,10},{16,20},{18,... | collective-permute-start | bytes 1572872 | tf_op jit(solution)/shard_map/ppermute | solution.py:1452
  780.3 24.8 %collective-permute-start.24 = (bf16[8,64,384]{2,1,0:T(8,128)(2,1)S(1)}, bf16[8,64,384]{2,1,0:T(8,128)(2,1)S(1)}, u32[]{:S(2)}, u32[]{:S(2)}) collective-permute-start(bf16[8,64,384]{2,1,0:T(8,128)(2,1)S(1)} %dynamic-slice_bitcast_fusion.8), channel_id=1, source_target_pairs={{0,4},{2,6},{4,0},{6,2},{8,12},{10,14},{12,8},{14,10},{16,20},{18,... | collective-permute-start | bytes 1179656 | tf_op jit(solution)/shard_map/ppermute | solution.py:1452
  782.2 17.4 %collective-permute-start.23 = (bf16[1,128,1024]{2,1,0:T(8,128)(2,1)S(1)}, bf16[1,128,1024]{2,1,0:T(8,128)(2,1)S(1)}, u32[]{:S(2)}, u32[]{:S(2)}) collective-permute-start(bf16[1,128,1024]{2,1,0:T(8,128)(2,1)S(1)} %dynamic-slice_bitcast_fusion.11), channel_id=1, source_target_pairs={{0,16},{2,18},{4,20},{6,22},{8,24},{10,26},{12,28},{14,30},{16,0},... | collective-permute-start | bytes 786440 | tf_op jit(solution)/shard_map/ppermute | solution.py:1452
  786.0 19.1 %collective-permute-start.21 = (bf16[4,64,1024]{2,1,0:T(8,128)(2,1)S(1)}, bf16[4,64,1024]{2,1,0:T(8,128)(2,1)S(1)}, u32[]{:S(2)}, u32[]{:S(2)}) collective-permute-start(bf16[4,64,1024]{2,1,0:T(8,128)(2,1)S(1)} %dynamic-slice_bitcast_fusion.4), channel_id=1, source_target_pairs={{0,4},{2,6},{4,0},{6,2},{8,12},{10,14},{12,8},{14,10},{16,20},{18,... | collective-permute-start | bytes 1572872 | tf_op jit(solution)/shard_map/ppermute | solution.py:1452
  788.2 16.9 %collective-permute-start.20 = (bf16[1,256,1024]{2,1,0:T(8,128)(2,1)S(1)}, bf16[1,256,1024]{2,1,0:T(8,128)(2,1)S(1)}, u32[]{:S(2)}, u32[]{:S(2)}) collective-permute-start(bf16[1,256,1024]{2,1,0:T(8,128)(2,1)S(1)} %dynamic-slice_bitcast_fusion.5), channel_id=1, source_target_pairs={{0,1},{1,0},{2,3},{3,2},{4,5},{5,4},{6,7},{7,6},{8,9},{9,8},{10,11... | collective-permute-start | bytes 1572872 | tf_op jit(solution)/shard_map/ppermute | solution.py:1451
  790.0 15.1 %collective-permute-start.22 = (bf16[1,128,1024]{2,1,0:T(8,128)(2,1)S(1)}, bf16[1,128,1024]{2,1,0:T(8,128)(2,1)S(1)}, u32[]{:S(2)}, u32[]{:S(2)}) collective-permute-start(bf16[1,128,1024]{2,1,0:T(8,128)(2,1)S(1)} %dynamic-slice_bitcast_fusion.12), channel_id=1, source_target_pairs={{0,16},{2,18},{4,20},{6,22},{8,24},{10,26},{12,28},{14,30},{16,0},... | collective-permute-start | bytes 786440 | tf_op jit(solution)/shard_map/ppermute | solution.py:1452
  805.3 18.4 %collective-permute-start.29 = (bf16[1,256,384]{2,1,0:T(8,128)(2,1)S(1)}, bf16[1,256,384]{2,1,0:T(8,128)(2,1)S(1)}, u32[]{:S(2)}, u32[]{:S(2)}) collective-permute-start(bf16[1,256,384]{2,1,0:T(8,128)(2,1)S(1)} %dynamic-slice_bitcast_fusion.13), channel_id=1, source_target_pairs={{0,1},{1,0},{2,3},{3,2},{4,5},{5,4},{6,7},{7,6},{8,9},{9,8},{10,11... | collective-permute-start | bytes 589832 | tf_op jit(solution)/shard_map/ppermute | solution.py:1451
  806.6 8.2 collective-permute-start.28
  807.0 21.5 %collective-permute-start.26 = (bf16[1,128,1024]{2,1,0:T(8,128)(2,1)S(1)}, bf16[1,128,1024]{2,1,0:T(8,128)(2,1)S(1)}, u32[]{:S(2)}, u32[]{:S(2)}) collective-permute-start(bf16[1,128,1024]{2,1,0:T(8,128)(2,1)S(1)} %dynamic-slice_bitcast_fusion.9), channel_id=1, source_target_pairs={{0,16},{2,18},{4,20},{6,22},{8,24},{10,26},{12,28},{14,30},{16,0},... | collective-permute-start | bytes 786440 | tf_op jit(solution)/shard_map/ppermute | solution.py:1452
  810.5 22.3 %collective-permute-start.25 = (bf16[1,128,1024]{2,1,0:T(8,128)(2,1)S(1)}, bf16[1,128,1024]{2,1,0:T(8,128)(2,1)S(1)}, u32[]{:S(2)}, u32[]{:S(2)}) collective-permute-start(bf16[1,128,1024]{2,1,0:T(8,128)(2,1)S(1)} %dynamic-slice_bitcast_fusion.10), channel_id=1, source_target_pairs={{0,16},{2,18},{4,20},{6,22},{8,24},{10,26},{12,28},{14,30},{16,0},... | collective-permute-start | bytes 786440 | tf_op jit(solution)/shard_map/ppermute | solution.py:1452
  810.6 13.1 %collective-permute-start.27 = (bf16[1,64,1024]{2,1,0:T(8,128)(2,1)S(1)}, bf16[1,64,1024]{2,1,0:T(8,128)(2,1)S(1)}, u32[]{:S(2)}, u32[]{:S(2)}) collective-permute-start(bf16[1,64,1024]{2,1,0:T(8,128)(2,1)S(1)} %dynamic-slice_bitcast_fusion.17), channel_id=1, source_target_pairs={{0,8},{2,10},{4,12},{6,14},{8,0},{10,2},{12,4},{14,6},{16,24},{18,... | collective-permute-start | bytes 393224 | tf_op jit(solution)/shard_map/ppermute | solution.py:1452
  814.8 44.6 %collective-permute-start.11 = (bf16[4,256,1024]{2,1,0:T(8,128)(2,1)S(1)}, bf16[4,256,1024]{2,1,0:T(8,128)(2,1)S(1)}, u32[]{:S(2)}, u32[]{:S(2)}) collective-permute-start(bf16[4,256,1024]{2,1,0:T(8,128)(2,1)S(1)} %select_bitcast_fusion), channel_id=1, source_target_pairs={{0,1},{1,0},{2,3},{3,2},{4,5},{5,4},{6,7},{7,6},{8,9},{9,8},{10,11... | collective-permute-start | bytes 6291464 | tf_op jit(solution)/shard_map/ppermute | solution.py:1578
  (29 other events, 244.8 us)
Sparse Core Ops, SparseCore 0:
  13.8 140.0 all-gather.2
  156.8 143.5 all-gather.4
  476.9 203.7 reduce-scatter.1

commit v3 on v2

--- a/solution.py
+++ b/solution.py
@@ -693,15 +693,14 @@
     top = parts[0][0].max(axis=1, keepdims=True)
     for scores, unused in parts[1:]:
         top = jnp.maximum(top, scores.max(axis=1, keepdims=True))
-    total = None
     mixed = None
     for scores, values in parts:
         weights = jnp.exp2((scores - top) * EXP2_SCALE)
-        part_total = weights.sum(axis=1, keepdims=True)
-        part_mixed = nn(weights.astype(BF), values)
-        total = part_total if total is None else total + part_total
+        wide_values = jnp.concatenate([values, jnp.ones_like(values)], axis=1)
+        part_mixed = nn(weights.astype(BF), wide_values)
         mixed = part_mixed if mixed is None else mixed + part_mixed
-    return (mixed / total).astype(BF), top * EXP2_SCALE + jnp.log2(total)
+    total = mixed[:, HEAD:]
+    return (mixed[:, :HEAD] / total).astype(BF), top * EXP2_SCALE + jnp.log2(total)
 
 
 def forward_kernel(
@@ -756,36 +755,33 @@
     def heads(with_before):
         def head(index, carry):
             columns = pl.ds(pl.multiple_of(index * HEAD, HEAD), HEAD)
-            lane = lax.broadcasted_iota(jnp.int32, (HALF, HEAD), 1) == index
-            for half in range(2):
-                rows = slice(half * HALF, (half + 1) * HALF)
-                own = query[rows, columns]
-                parts = []
-                if with_before:
-                    parts.append((nt(own, key_before[:, columns]), value_before[:, columns]))
-                if half == 1:
-                    parts.append((nt(own, key[:HALF, columns]), value[:HALF, columns]))
-                row = lax.broadcasted_iota(jnp.int32, (HALF, HALF), 0)
-                column = lax.broadcasted_iota(jnp.int32, (HALF, HALF), 1)
-                reach = row + flags[2 * block + half] * HALF
-                near = jnp.where(column <= reach, nt(own, key[rows, columns]), masked_score)
-                parts.append((near, value[rows, columns]))
-                parts.append((nt(own, state_key[:, columns]), state_value[:, columns]))
-                mixed, total = softmax_parts(parts)
-                token_mixed[rows, columns] = mixed
-                token_totals[rows, :] = jnp.where(lane, total, token_totals[rows, :])
-                own = state_query[rows, columns]
-                mixed, total = softmax_parts(
-                    [
-                        (nt(own, key[:, columns]), value[:, columns]),
-                        (nt(own, state_key[:, columns]), state_value[:, columns]),
-                    ]
-                )
-                state_mixed[rows, columns] = mixed
-                state_totals[rows, :] = jnp.where(lane, total, state_totals[rows, :])
+            lane = lax.broadcasted_iota(jnp.int32, (W, HEAD), 1) == index
+            row = lax.broadcasted_iota(jnp.int32, (W, W), 0)
+            column = lax.broadcasted_iota(jnp.int32, (W, W), 1)
+            lead = jnp.where(row < HALF, flags[2 * block] * (HALF - 1 - row), flags[2 * block + 1] * (W - 1 - row))
+            reach = column <= row + lead
+            own = query[:, columns]
+            parts = []
+            if with_before:
+                parts.append((nt(own, key_before[:, columns]), value_before[:, columns]))
+            near = jnp.where(reach, nt(own, key[:, columns]), masked_score)
+            parts.append((near, value[:, columns]))
+            parts.append((nt(own, state_key[:, columns]), state_value[:, columns]))
+            mixed, total = softmax_parts(parts)
+            token_mixed[:, columns] = mixed
+            token_totals[...] = jnp.where(lane, total, token_totals[...])
+            own = state_query[:, columns]
+            mixed, total = softmax_parts(
+                [
+                    (nt(own, key[:, columns]), value[:, columns]),
+                    (nt(own, state_key[:, columns]), state_value[:, columns]),
+                ]
+            )
+            state_mixed[:, columns] = mixed
+            state_totals[...] = jnp.where(lane, total, state_totals[...])
             return carry
 
-        lax.fori_loop(0, D // HEAD, head, 0)
+        lax.fori_loop(0, D // HEAD, head, 0, unroll=2)
 
     @pl.when(block == 0)
     def first():
@@ -1078,10 +1074,6 @@
     gate_part,
     carry_key,
     carry_value,
-    grad_query_sum,
-    deltas,
-    queries,
-    grads_out,
 ):
     step = pl.program_id(0)
     half = pl.program_id(1)
@@ -1114,77 +1106,87 @@
 
     grad_states[3] = gate_part[half]
 
-    def head(index, carry):
-        columns = pl.ds(pl.multiple_of(index * HEAD, HEAD), HEAD)
-        at = half * local + index
-        queries[:W] = query[:, columns]
-        queries[W:] = state_query[:, columns]
-        grads_out[:W] = grad_mixed[:, columns]
-        grads_out[W:] = grad_state_mixed[half, :, columns]
-        for first, mixed in ((0, token_mixed), (W, state_mixed)):
-            product = grads_out[first : first + W].astype(F32) * mixed[:, columns].astype(F32)
-            deltas[:, first : first + W] = jnp.sum(product.T, axis=0, keepdims=True)
-        token_total = totals[0, pl.ds(at, 1), :]
-        state_total = totals[0, pl.ds(count + at, 1), :]
-        total = jnp.concatenate([token_total, state_total], axis=1)
-
-        def chunk(keys, values, first, last, mask, fresh):
-            some = queries[first:last]
-            some_grads = grads_out[first:last]
-            scores = nt(keys, some)
-            if mask is not None:
-                size = mask.shape[1]
-                scores = jnp.concatenate(
-                    [jnp.where(mask, scores[:, :size], masked_score), scores[:, size:]], axis=1
+    def heads(with_before):
+        def head(index, carry):
+            columns = pl.ds(pl.multiple_of(index * HEAD, HEAD), HEAD)
+            at = half * local + index
+            queries = jnp.concatenate([query[:, columns], state_query[:, columns]], axis=0)
+            grads_out = jnp.concatenate(
+                [grad_mixed[:, columns], grad_state_mixed[half, :, columns]], axis=0
+            )
+            mixed = jnp.concatenate([token_mixed[:, columns], state_mixed[:, columns]], axis=0)
+            product = grads_out.astype(F32) * mixed.astype(F32)
+            delta = jnp.sum(product.T, axis=0, keepdims=True)
+            token_total = totals[0, pl.ds(at, 1), :]
+            state_total = totals[0, pl.ds(count + at, 1), :]
+            total = jnp.concatenate([token_total, state_total], axis=1)
+
+            def chunk(keys, values, first, last, mask):
+                some = queries[first:last]
+                some_grads = grads_out[first:last]
+                scores = nt(keys, some)
+                if mask is not None:
+                    size = mask.shape[1]
+                    scores = jnp.concatenate(
+                        [jnp.where(mask, scores[:, :size], masked_score), scores[:, size:]], axis=1
+                    )
+                weights = jnp.exp2(scores * EXP2_SCALE - total[:, first:last])
+                back = nt(values, some_grads) - delta[:, first:last]
+                grad_scores = (weights * back).astype(BF)
+                grad_values = nn(weights.astype(BF), some_grads)
+                grad_keys = nn(grad_scores, some)
+                return grad_keys * SCORE_SCALE, grad_values, tn(keys, grad_scores)
+
+            turned = None
+            for first in range(0, S, HALF):
+                rows = slice(first, first + HALF)
+                grad_keys, grad_values, part = chunk(
+                    state_key[rows, columns], state_value[rows, columns], 0, W + S, None
                 )
-            weights = jnp.exp2(scores * EXP2_SCALE - total[:, first:last])
-            back = nt(values, some_grads) - deltas[:, first:last]
-            grad_scores = (weights * back).astype(BF)
-            grad_values = nn(weights.astype(BF), some_grads)
-            grad_keys = nn(grad_scores, some)
-            turned = tn(keys, grad_scores)
-            if fresh:
-                grad_query_sum[:, first:last] = turned
-            else:
-                grad_query_sum[:, first:last] += turned
-            return grad_keys * SCORE_SCALE, grad_values
-
-        for part in range(2):
-            rows = slice(part * HALF, (part + 1) * HALF)
-            grad_keys, grad_values = chunk(
-                state_key[rows, columns], state_value[rows, columns], 0, W + S, None, part == 0
-            )
-            grad_states[1, rows, columns] = grad_keys.astype(BF)
-            grad_states[2, rows, columns] = grad_values.astype(BF)
-        for part in range(2):
-            rows = slice(part * HALF, (part + 1) * HALF)
-            row = lax.broadcasted_iota(jnp.int32, (HALF, HALF), 0)
-            column = lax.broadcasted_iota(jnp.int32, (HALF, HALF), 1)
-            mask = row <= column + flags[2 * block + part] * HALF
-            grad_keys, grad_values = chunk(
-                key[rows, columns], value[rows, columns], part * HALF, W + S, mask, False
-            )
-            grad_tokens[1, rows, columns] = (grad_keys + carry_key[half, rows, columns]).astype(BF)
-            grad_tokens[2, rows, columns] = (
-                grad_values + carry_value[half, rows, columns]
-            ).astype(BF)
-
-        @pl.when(block > 0)
-        def before():
+                grad_states[1, rows, columns] = grad_keys.astype(BF)
+                grad_states[2, rows, columns] = grad_values.astype(BF)
+                turned = part if turned is None else turned + part
             for part in range(2):
                 rows = slice(part * HALF, (part + 1) * HALF)
-                grad_keys, grad_values = chunk(
-                    key_before[rows, columns], value_before[rows, columns], 0, W, None, False
+                row = lax.broadcasted_iota(jnp.int32, (HALF, HALF), 0)
+                column = lax.broadcasted_iota(jnp.int32, (HALF, HALF), 1)
+                mask = row <= column + flags[2 * block + part] * HALF
+                grad_keys, grad_values, more = chunk(
+                    key[rows, columns], value[rows, columns], part * HALF, W + S, mask
                 )
-                carry_key[half, rows, columns] = grad_keys
-                carry_value[half, rows, columns] = grad_values
-
-        grad_query = (grad_query_sum[...] * SCORE_SCALE).T
-        grad_tokens[0, :, columns] = grad_query[:W].astype(BF)
-        grad_states[0, :, columns] = grad_query[W:].astype(BF)
-        return carry
-
-    lax.fori_loop(0, local, head, 0)
+                grad_tokens[1, rows, columns] = (grad_keys + carry_key[half, rows, columns]).astype(
+                    BF
+                )
+                grad_tokens[2, rows, columns] = (
+                    grad_values + carry_value[half, rows, columns]
+                ).astype(BF)
+                if part:
+                    more = jnp.concatenate([jnp.zeros((HEAD, HALF), F32), more], axis=1)
+                turned = turned + more
+            turned_tokens = turned[:, :W]
+            if with_before:
+                for first in range(0, W, HALF):
+                    rows = slice(first, first + HALF)
+                    grad_keys, grad_values, part = chunk(
+                        key_before[rows, columns], value_before[rows, columns], 0, W, None
+                    )
+                    carry_key[half, rows, columns] = grad_keys
+                    carry_value[half, rows, columns] = grad_values
+                    turned_tokens = turned_tokens + part
+            grad_tokens[0, :, columns] = (turned_tokens * SCORE_SCALE).T.astype(BF)
+            grad_states[0, :, columns] = (turned[:, W:] * SCORE_SCALE).T.astype(BF)
+            return carry
+
+        lax.fori_loop(0, local, head, 0, unroll=2)
+
+    @pl.when(block > 0)
+    def later():
+        heads(True)
+
+    @pl.when(block == 0)
+    def first():
+        heads(False)
+
     grad_normed[...] += (
         nt(grad_states[0], weight_query[...])
         + nt(grad_states[1], weight_key[...])
@@ -1270,10 +1272,6 @@
                 pltpu.VMEM((2, S, half_width), BF),
                 pltpu.VMEM((2, W, half_width), F32),
                 pltpu.VMEM((2, W, half_width), F32),
-                pltpu.VMEM((HEAD, W + S), F32),
-                pltpu.VMEM((1, W + S), F32),
-                pltpu.VMEM((W + S, HEAD), BF),
-                pltpu.VMEM((W + S, HEAD), BF),
             ],
         ),
         out_shape=[

time: 875 us -> 859 us (0.982)
  Pallas kernels: 535 us -> 501 us
  waiting for transfers between devices: 189 us -> 207 us
    pallas_call x1, Pallas kernels: 115 us -> 90.9 us  [forward(): pl.pallas_call(forward_kernel, grid_spec=pltpu.PrefetchScalarGridSpec(num...]
    all_gather x2, waiting for transfers between devices: 0.01 us -> 16.1 us  [gather(): return lax.all_gather(local, ('tensor', 'dp'), axis=0, tiled=True)]
    pallas_call x1, Pallas kernels: 154 us -> 143 us  [backward(): pl.pallas_call(backward_kernel, grid_spec=pltpu.PrefetchScalarGridSpec(nu...]
  transfers between devices with their start and end apart: 37 -> 37, of which waited for: 20 -> 22; matrix products, arithmetic and copies ran while one was open for 9% -> 9% of each run, Pallas kernels for 42% -> 39%
where the time goes in v3:
time: 859 us; the launch traced here: 852 us
  Pallas kernels  501 us (58%)
  waiting for transfers between devices  207 us (24%)
  other arithmetic  60.8 us (7%)
  starting transfers between devices  38.9 us (5%)
  local copies, waits for them, and re-layouts  29.6 us (3%)
  between operations  14.7 us (2%)
    pallas_call x1, Pallas kernels, backward(): pl.pallas_call(backward_kernel, grid_spec=pltpu.PrefetchScalarGridSpec(nu...  143 us
    pallas_call x1, Pallas kernels, mlp(): pl.pallas_call(mlp_kernel, grid=(2 * across,), in_specs=[rows, turned, ro...  128 us
    ppermute x24, waiting for transfers between devices, trade(): return lax.ppermute(values, 'dp', [(i, i ^ 1 << axis) for i in range(dp)])  98.7 us
    pallas_call x1, Pallas kernels, forward(): pl.pallas_call(forward_kernel, grid_spec=pltpu.PrefetchScalarGridSpec(num...  90.9 us
    ppermute x6, waiting for transfers between devices, trade(): return lax.ppermute(values, 'tensor', [(0, 1), (1, 0)])  76.7 us
    pallas_call x5, Pallas kernels, weight_grads(): pl.pallas_call(functools.partial(weight_grad_kernel, dp), grid_spec=pltpu...  57.8 us
    ppermute x24, starting transfers between devices, trade(): return lax.ppermute(values, 'dp', [(i, i ^ 1 << axis) for i in range(dp)])  24.3 us
    pallas_call x1, Pallas kernels, token_grad(): pl.pallas_call(token_grad_kernel, grid=(tokens // W,), in_specs=[pl.Block...  21.8 us
  transfers between devices with their start and end apart: 37, of which 22 were waited for; matrix products, arithmetic and copies ran while one was open for 9% of the time, Pallas kernels for 39%

profile of v3, /device:TPU:0, one launch (start us, length us, event | category | flops | bytes accessed | tf_op | source)
XLA Modules:
  0.0 851.9 jit_solution(79354403308416059)
XLA Ops:
  27.5 24.9 %collective-permute-done.2 = bf16[128,1536]{1,0:T(8,128)(2,1)S(1)} collective-permute-done((bf16[128,1536]{1,0:T(8,128)(2,1)S(1)}, bf16[128,1536]{1,0:T(8,128)(2,1)S(1)}, u32[]{:S(2)}, u32[]{:S(2)}) %collective-permute-start.2) | collective-permute-done | bytes 393248 | tf_op jit(solution)/shard_map/ppermute | solution.py:1450
  56.5 20.1 %collective-permute-done.3 = bf16[256,1536]{1,0:T(8,128)(2,1)} collective-permute-done((bf16[256,1536]{1,0:T(8,128)(2,1)S(1)}, bf16[256,1536]{1,0:T(8,128)(2,1)}, u32[]{:S(2)}, u32[]{:S(2)}) %collective-permute-start.3) | collective-permute-done | bytes 786464 | tf_op jit(solution)/shard_map/ppermute | solution.py:1450
  78.2 3.4 collective-permute-done
  87.5 55.0 %collective-permute-done.4 = bf16[512,1536]{1,0:T(8,128)(2,1)S(1)} collective-permute-done((bf16[512,1536]{1,0:T(8,128)(2,1)S(1)}, bf16[512,1536]{1,0:T(8,128)(2,1)S(1)}, u32[]{:S(2)}, u32[]{:S(2)}) %collective-permute-start.4) | collective-permute-done | bytes 1572896 | tf_op jit(solution)/shard_map/ppermute | solution.py:1449
  143.3 5.9 collective-permute-done.5
  151.7 3.2 pad_maximum_fusion
  155.6 3.9 select_bitcast_fusion.2
  168.0 19.0 %project.1 = (bf16[1024,2048]{1,0:T(8,128)(2,1)}, bf16[2048,1024]{1,0:T(8,128)(2,1)}, bf16[2048,1024]{1,0:T(8,128)(2,1)}, bf16[2048,1024]{1,0:T(8,128)(2,1)}) custom-call(bf16[2048,1024]{1,0:T(8,128)(2,1)} %bitcast.309, f32[1,1024]{1,0:T(1,128)} %squeeze.138.gain, ...), custom_call_target="tpu_custom_call" | custom-call | flops 12884901888 | bytes 27262976 | tf_op jit(solution)/shard_map/project/pallas_call | solution.py:675
  187.0 90.9 %forward.1 = (bf16[2048,1024]{1,0:T(8,128)(2,1)}, bf16[2048,1024]{1,0:T(8,128)(2,1)}, bf16[1024,2048]{1,0:T(8,128)(2,1)}, bf16[2048,1024]{1,0:T(8,128)(2,1)}, bf...) custom-call(s32[8]{0:T(128)} %convert_element_type.468.flags, ...), custom_call_target="tpu_custom_call" | custom-call | flops 41999998976 | bytes 100000000 | tf_op jit(solution)/shard_map/forward/pallas_call | solution.py:811
  278.6 3.4 bitcast_select_fusion.5
  284.3 16.1 %all-gather.5.cloned.1.call-done.w0.w1.weights = bf16[2048,4608]{1,0:T(8,128)(2,1)} async-done(((bf16[64,4608]{1,0:T(8,128)(2,1)}), bf16[2048,4608]{1,0:T(8,128)(2,1)}) %all-gather.5.cloned.1.call-update) | async-done | bytes 18874384 | tf_op jit(solution)/shard_map/all_gather | solution.py:1430
  300.4 14.7 %middle.1 = (f32[2048,1024]{1,0:T(8,128)}, bf16[2048,1024]{1,0:T(8,128)(2,1)}, bf16[1024,2048]{1,0:T(8,128)(2,1)}, bf16[1024,2048]{1,0:T(8,128)(2,1)}) custom-call(bf16[2048,1024]{1,0:T(8,128)(2,1)} %bitcast.310, bf16[2048,1024]{1,0:T(8,128)(2,1)} %get-tuple-element.102.mixed.right.token_mixed, ...), custom_call_target="tpu_custom_call" | custom-call | flops 4294967296 | bytes 33554432 | tf_op jit(solution)/shard_map/middle/pallas_call | solution.py:887
  315.2 127.5 %mlp.1 = (bf16[2048,1024]{1,0:T(8,128)(2,1)}, bf16[2048,1024]{1,0:T(8,128)(2,1)}, bf16[2048,4608]{1,0:T(8,128)(2,1)}) custom-call(bf16[2048,1024]{1,0:T(8,128)(2,1)} %get-tuple-element.107.mlp_in, bf16[1024,2048]{1,0:T(8,128)(2,1)} %get-tuple-element.108.mlp_turned, bf16[2048,1024]{1,0:T(8,128)(2,1)} %bitcast.307, ...), custom_call_target="tpu_custom_call" | custom-call | flops 102999998464 | bytes 60000000 | tf_op jit(solution)/shard_map/mlp/pallas_call | solution.py:961
  442.7 18.0 %after_mlp.1 = (bf16[2048,1024]{1,0:T(8,128)(2,1)}, bf16[2048,1024]{1,0:T(8,128)(2,1)}, bf16[1024,2048]{1,0:T(8,128)(2,1)}, bf16[2048,1024]{1,0:T(8,128)(2,1)}, f32[1,1024]{1,0:T(1,128)}) custom-call(f32[2048,1024]{1,0:T(8,128)} %get-tuple-element.106.middle, bf16[2048,1024]{1,0:T(8,128)(2,1)} %get-tuple-element.110.mlp_out, ...), custom_call_target="tpu_custom_call" | custom-call | flops 4294967296 | bytes 33554432 | tf_op jit(solution)/shard_map/after_mlp/pallas_call | solution.py:1010
  460.6 8.5 %whole_weight_grad.1 = bf16[2048,4608]{1,0:T(8,128)(2,1)} custom-call(bf16[1024,2048]{1,0:T(8,128)(2,1)} %get-tuple-element.118.turned, bf16[2048,1024]{1,0:T(8,128)(2,1)} %get-tuple-element.102.mixed.right.token_mixed, bf16[2048,4608]{1,0:T(8,128)(2,1)} %get-tuple-element.119.into), custom_call_target="tpu_custom_call", output_to_operand_aliasing={{}: (2, {})} | custom-call | flops 4294967296 | bytes 8388608 | tf_op jit(solution)/shard_map/whole_weight_grad/pallas_call | solution.py:1322
  473.1 143.0 %backward.1 = (bf16[3,2048,1024]{2,1,0:T(8,128)(2,1)}, bf16[4,2048,1024]{2,1,0:T(8,128)(2,1)}, bf16[1024,2048]{1,0:T(8,128)(2,1)}, bf16[512,1024]{1,0:T(8,128)(2...) custom-call(s32[8]{0:T(128)} %convert_element_type.468.flags, bf16[2048,1024]{1,0:T(8,128)(2,1)} %get-tuple-element.98.query, ...), custom_call_target="tpu_custom_call" | custom-call | flops 70000001024 | bytes 100000000 | tf_op jit(solution)/shard_map/backward/pallas_call | solution.py:1243
  616.1 3.2 fusion.6
  621.7 13.3 %weight_grads.5 = (bf16[1024,1024]{1,0:T(8,128)(2,1)}, bf16[1024,1024]{1,0:T(8,128)(2,1)}) custom-call(s32[1]{0:T(128)} %bitcast.39.core, bf16[1024,2048]{1,0:T(8,128)(2,1)} %get-tuple-element.129.turned, bf16[4,2048,1024]{2,1,0:T(8,128)(2,1)} %get-tuple-element.134.right), custom_call_target="tpu_custom_call" | custom-call | flops 8589934592 | bytes 12582912 | tf_op jit(solution)/shard_map/weight_grads/pallas_call | solution.py:1359
  635.1 13.5 %weight_grads.6 = (bf16[1024,1024]{1,0:T(8,128)(2,1)}, bf16[1024,1024]{1,0:T(8,128)(2,1)}) custom-call(s32[1]{0:T(128)} %bitcast.39.core, bf16[1024,2048]{1,0:T(8,128)(2,1)} %get-tuple-element.129.turned, bf16[4,2048,1024]{2,1,0:T(8,128)(2,1)} %get-tuple-element.134.right), custom_call_target="tpu_custom_call" | custom-call | flops 8589934592 | bytes 12582912 | tf_op jit(solution)/shard_map/weight_grads/pallas_call | solution.py:1359
  654.0 13.8 %weight_grads.7 = (bf16[1024,1024]{1,0:T(8,128)(2,1)}, bf16[1024,1024]{1,0:T(8,128)(2,1)}) custom-call(s32[1]{0:T(128)} %bitcast.39.core, bf16[1024,2048]{1,0:T(8,128)(2,1)} %get-tuple-element.128.turned, bf16[3,2048,1024]{2,1,0:T(8,128)(2,1)} %get-tuple-element.148.right.grads), custom_call_target="tpu_custom_call" | custom-call | flops 8589934592 | bytes 12582912 | tf_op jit(solution)/shard_map/weight_grads/pallas_call | solution.py:1359
  672.9 8.5 %weight_grads.8 = (bf16[1024,1024]{1,0:T(8,128)(2,1)}, bf16[1024,1024]{1,0:T(8,128)(2,1)}) custom-call(s32[1]{0:T(128)} %bitcast.39.core, bf16[1024,2048]{1,0:T(8,128)(2,1)} %get-tuple-element.128.turned, bf16[3,2048,1024]{2,1,0:T(8,128)(2,1)} %get-tuple-element.148.right.grads), custom_call_target="tpu_custom_call" | custom-call | flops 4294967296 | bytes 8388608 | tf_op jit(solution)/shard_map/weight_grads/pallas_call | solution.py:1359
  685.8 8.6 %weight_grads.9 = (bf16[1024,1024]{1,0:T(8,128)(2,1)}, bf16[1024,1024]{1,0:T(8,128)(2,1)}) custom-call(s32[1]{0:T(128)} %bitcast.39.core, bf16[1024,2048]{1,0:T(8,128)(2,1)} %get-tuple-element.146.turned, bf16[1,2048,1024]{2,1,0:T(8,128)(2,1)} %bitcast.387, ...), custom_call_target="tpu_custom_call", output_to_operand_aliasing={{0}: (3, {}), {1}: (4, {})} | custom-call | flops 4294967296 | bytes 8388608 | tf_op jit(solution)/shard_map/weight_grads/pallas_call | solution.py:1359
  700.2 21.8 %token_grad.1 = (bf16[2048,1024]{1,0:T(8,128)(2,1)}, f32[1,1024]{1,0:T(1,128)}) custom-call(bf16[3,2048,1024]{2,1,0:T(8,128)(2,1)} %get-tuple-element.148.right.grads, bf16[2048,2944]{1,0:T(8,128)(2,1)} %all-gather.3.cloned.1.call-done.w0.w1.query0.query1.key0.key1.weight_query.weight_key, ...), custom_call_target="tpu_custom_call" | custom-call | flops 12884901888 | bytes 25165824 | tf_op jit(solution)/shard_map/token_grad/pallas_call | solution.py:1410
  735.4 11.6 %collective-permute-done.14 = bf16[1,512,1024]{2,1,0:T(8,128)(2,1)} collective-permute-done((bf16[1,512,1024]{2,1,0:T(8,128)(2,1)}, bf16[1,512,1024]{2,1,0:T(8,128)(2,1)}, u32[]{:S(2)}, u32[]{:S(2)}) %collective-permute-start.14) | collective-permute-done | bytes 1048608 | tf_op jit(solution)/shard_map/ppermute | solution.py:1449
  747.0 10.1 %collective-permute-done.18 = bf16[1,256,1024]{2,1,0:T(8,128)(2,1)S(1)} collective-permute-done((bf16[1,256,1024]{2,1,0:T(8,128)(2,1)S(1)}, bf16[1,256,1024]{2,1,0:T(8,128)(2,1)S(1)}, u32[]{:S(2)}, u32[]{:S(2)}) %collective-permute-start.18) | collective-permute-done | bytes 524320 | tf_op jit(solution)/shard_map/ppermute | solution.py:1449
  757.0 5.8 collective-permute-done.16
  773.5 9.4 %collective-permute-done.23 = bf16[1,128,1024]{2,1,0:T(8,128)(2,1)S(1)} collective-permute-done((bf16[1,128,1024]{2,1,0:T(8,128)(2,1)S(1)}, bf16[1,128,1024]{2,1,0:T(8,128)(2,1)S(1)}, u32[]{:S(2)}, u32[]{:S(2)}) %collective-permute-start.23) | collective-permute-done | bytes 262176 | tf_op jit(solution)/shard_map/ppermute | solution.py:1450
  782.9 5.5 collective-permute-done.22
  798.2 8.5 collective-permute-done.27
  806.7 4.7 collective-permute-done.26
  811.4 4.4 collective-permute-done.25
  830.8 11.6 %collective-permute-done.11 = bf16[4,256,1024]{2,1,0:T(8,128)(2,1)S(1)} collective-permute-done((bf16[4,256,1024]{2,1,0:T(8,128)(2,1)S(1)}, bf16[4,256,1024]{2,1,0:T(8,128)(2,1)S(1)}, u32[]{:S(2)}, u32[]{:S(2)}) %collective-permute-start.11) | collective-permute-done | bytes 2097184 | tf_op jit(solution)/shard_map/ppermute | solution.py:1576
  (224 shorter events, 125.2 us)
Async XLA Ops:
  7.2 147.7 %all-gather.3.cloned.1.call-start = ((), (), s32[]{:S(2)}) async-start(), calls=%async_computation.1 | async-start | bytes 12435456 | tf_op jit(solution)/shard_map/all_gather | solution.py:1430
  13.7 286.7 %all-gather.5.cloned.1.call-start = ((), (), s32[]{:S(2)}) async-start(), calls=%async_computation.2 | async-start | bytes 19464192 | tf_op jit(solution)/shard_map/all_gather | solution.py:1430
  15.3 8.2 collective-permute-start.1
  20.9 60.7 %collective-permute-start = (bf16[4,256,1024]{2,1,0:T(8,128)(2,1)S(1)}, bf16[4,256,1024]{2,1,0:T(8,128)(2,1)}, u32[]{:S(2)}, u32[]{:S(2)}) collective-permute-start(bf16[4,256,1024]{2,1,0:T(8,128)(2,1)S(1)} %select_bitcast_fusion.3), channel_id=1, source_target_pairs={{0,1},{1,0},{2,3},{3,2},{4,5},{5,4},{6,7},{7,6},{8,9},{9,8},{10,11... | collective-permute-start | bytes 6291464 | tf_op jit(solution)/shard_map/ppermute | solution.py:1564
  24.7 27.7 %collective-permute-start.2 = (bf16[128,1536]{1,0:T(8,128)(2,1)S(1)}, bf16[128,1536]{1,0:T(8,128)(2,1)S(1)}, u32[]{:S(2)}, u32[]{:S(2)}) collective-permute-start(bf16[128,1536]{1,0:T(8,128)(2,1)S(1)} %bitcast.358), channel_id=1, source_target_pairs={{0,16},{2,18},{4,20},{6,22},{8,24},{10,26},{12,28},{14,30},{16,0},... | collective-permute-start | bytes 1179656 | tf_op jit(solution)/shard_map/ppermute | solution.py:1450
  52.6 24.1 %collective-permute-start.3 = (bf16[256,1536]{1,0:T(8,128)(2,1)S(1)}, bf16[256,1536]{1,0:T(8,128)(2,1)}, u32[]{:S(2)}, u32[]{:S(2)}) collective-permute-start(bf16[256,1536]{1,0:T(8,128)(2,1)S(1)} %bitcast.346), channel_id=1, source_target_pairs={{0,4},{2,6},{4,0},{6,2},{8,12},{10,14},{12,8},{14,10},{16,20},{18,... | collective-permute-start | bytes 2359304 | tf_op jit(solution)/shard_map/ppermute | solution.py:1450
  86.0 56.5 %collective-permute-start.4 = (bf16[512,1536]{1,0:T(8,128)(2,1)S(1)}, bf16[512,1536]{1,0:T(8,128)(2,1)S(1)}, u32[]{:S(2)}, u32[]{:S(2)}) collective-permute-start(bf16[512,1536]{1,0:T(8,128)(2,1)S(1)} %bitcast.332), channel_id=1, source_target_pairs={{0,1},{1,0},{2,3},{3,2},{4,5},{5,4},{6,7},{7,6},{8,9},{9,8},{10,11... | collective-permute-start | bytes 4718600 | tf_op jit(solution)/shard_map/ppermute | solution.py:1449
  154.9 545.3 %reduce-scatter.2.cloned.1.call-start = ((), (), s32[]{:S(2)}) async-start(), calls=%async_computation.3 | async-start | bytes 19464192 | tf_op jit(solution)/shard_map/reduce_scatter | solution.py:1434
  159.5 118.4 %collective-permute-start.6 = (bf16[4,256,1024]{2,1,0:T(8,128)(2,1)}, bf16[4,256,1024]{2,1,0:T(8,128)(2,1)}, u32[]{:S(2)}, u32[]{:S(2)}) collective-permute-start(bf16[4,256,1024]{2,1,0:T(8,128)(2,1)} %select_bitcast_fusion.2), channel_id=1, source_target_pairs={{0,1},{1,0},{2,3},{3,2},{4,5},{5,4},{6,7},{7,6},{8,9},{9,8},{10,11... | collective-permute-start | bytes 6291464 | tf_op jit(solution)/shard_map/ppermute | solution.py:1564
  471.6 144.5 %collective-permute-start.7 = (bf16[4,256,1024]{2,1,0:T(8,128)(2,1)S(1)}, bf16[4,256,1024]{2,1,0:T(8,128)(2,1)}, u32[]{:S(2)}, u32[]{:S(2)}) collective-permute-start(bf16[4,256,1024]{2,1,0:T(8,128)(2,1)S(1)} %select_bitcast_fusion.1), channel_id=1, source_target_pairs={{0,1},{1,0},{2,3},{3,2},{4,5},{5,4},{6,7},{7,6},{8,9},{9,8},{10,11... | collective-permute-start | bytes 6291464 | tf_op jit(solution)/shard_map/ppermute | solution.py:1576
  635.1 14.0 %collective-permute-start.8 = (bf16[1024,1024]{1,0:T(8,128)(2,1)}, bf16[1024,1024]{1,0:T(8,128)(2,1)}, u32[]{:S(2)}, u32[]{:S(2)}) collective-permute-start(bf16[1024,1024]{1,0:T(8,128)(2,1)} %get-tuple-element.133), channel_id=1, source_target_pairs={{0,2},{2,0},{4,6},{6,4},{8,10},{10,8},{12,14},{14,12},{16,18},{18,... | collective-permute-start | bytes 6291464 | tf_op jit(solution)/shard_map/ppermute | solution.py:1450
  648.6 19.3 %collective-permute-start.10 = (bf16[1024,1024]{1,0:T(8,128)(2,1)}, bf16[1024,1024]{1,0:T(8,128)(2,1)}, u32[]{:S(2)}, u32[]{:S(2)}) collective-permute-start(bf16[1024,1024]{1,0:T(8,128)(2,1)} %get-tuple-element.137), channel_id=1, source_target_pairs={{0,2},{2,0},{4,6},{6,4},{8,10},{10,8},{12,14},{14,12},{16,18},{18,... | collective-permute-start | bytes 6291464 | tf_op jit(solution)/shard_map/ppermute | solution.py:1450
  667.8 13.6 %collective-permute-start.9 = (bf16[1024,1024]{1,0:T(8,128)(2,1)}, bf16[1024,1024]{1,0:T(8,128)(2,1)}, u32[]{:S(2)}, u32[]{:S(2)}) collective-permute-start(bf16[1024,1024]{1,0:T(8,128)(2,1)} %get-tuple-element.140), channel_id=1, source_target_pairs={{0,2},{2,0},{4,6},{6,4},{8,10},{10,8},{12,14},{14,12},{16,18},{18,... | collective-permute-start | bytes 6291464 | tf_op jit(solution)/shard_map/ppermute | solution.py:1450
  694.4 29.0 %collective-permute-start.12 = (bf16[1024,1024]{1,0:T(8,128)(2,1)}, bf16[1024,1024]{1,0:T(8,128)(2,1)}, u32[]{:S(2)}, u32[]{:S(2)}) collective-permute-start(bf16[1024,1024]{1,0:T(8,128)(2,1)} %get-tuple-element.147), channel_id=1, source_target_pairs={{0,2},{2,0},{4,6},{6,4},{8,10},{10,8},{12,14},{14,12},{16,18},{18,... | collective-permute-start | bytes 6291464 | tf_op jit(solution)/shard_map/ppermute | solution.py:1450
  697.8 25.5 %collective-permute-start.17 = (bf16[8,64,1024]{2,1,0:T(8,128)(2,1)}, bf16[8,64,1024]{2,1,0:T(8,128)(2,1)}, u32[]{:S(2)}, u32[]{:S(2)}) collective-permute-start(bf16[8,64,1024]{2,1,0:T(8,128)(2,1)} %dynamic-slice_bitcast_fusion.2), channel_id=1, source_target_pairs={{0,4},{2,6},{4,0},{6,2},{8,12},{10,14},{12,8},{14,10},{16,20},{18,... | collective-permute-start | bytes 3145736 | tf_op jit(solution)/shard_map/ppermute | solution.py:1450
  698.2 33.7 %collective-permute-start.15 = (bf16[1,512,1024]{2,1,0:T(8,128)(2,1)}, bf16[1,512,1024]{2,1,0:T(8,128)(2,1)}, u32[]{:S(2)}, u32[]{:S(2)}) collective-permute-start(bf16[1,512,1024]{2,1,0:T(8,128)(2,1)} %dynamic-slice_bitcast_fusion.3), channel_id=1, source_target_pairs={{0,1},{1,0},{2,3},{3,2},{4,5},{5,4},{6,7},{7,6},{8,9},{9,8},{10,11... | collective-permute-start | bytes 3145736 | tf_op jit(solution)/shard_map/ppermute | solution.py:1449
  699.7 47.3 %collective-permute-start.14 = (bf16[1,512,1024]{2,1,0:T(8,128)(2,1)}, bf16[1,512,1024]{2,1,0:T(8,128)(2,1)}, u32[]{:S(2)}, u32[]{:S(2)}) collective-permute-start(bf16[1,512,1024]{2,1,0:T(8,128)(2,1)} %dynamic-slice_bitcast_fusion.1), channel_id=1, source_target_pairs={{0,1},{1,0},{2,3},{3,2},{4,5},{5,4},{6,7},{7,6},{8,9},{9,8},{10,11... | collective-permute-start | bytes 3145736 | tf_op jit(solution)/shard_map/ppermute | solution.py:1449
  723.2 39.7 %collective-permute-start.19 = (bf16[1024,384]{1,0:T(8,128)(2,1)S(1)}, bf16[1024,384]{1,0:T(8,128)(2,1)S(1)}, u32[]{:S(2)}, u32[]{:S(2)}) collective-permute-start(bf16[1024,384]{1,0:T(8,128)(2,1)S(1)} %bitcast.370), channel_id=1, source_target_pairs={{0,2},{2,0},{4,6},{6,4},{8,10},{10,8},{12,14},{14,12},{16,18},{18,... | collective-permute-start | bytes 2359304 | tf_op jit(solution)/shard_map/ppermute | solution.py:1450
  727.1 35.7 %collective-permute-start.13 = (bf16[8,64,1024]{2,1,0:T(8,128)(2,1)S(1)}, bf16[8,64,1024]{2,1,0:T(8,128)(2,1)S(1)}, u32[]{:S(2)}, u32[]{:S(2)}) collective-permute-start(bf16[8,64,1024]{2,1,0:T(8,128)(2,1)S(1)} %dynamic-slice_bitcast_fusion), channel_id=1, source_target_pairs={{0,4},{2,6},{4,0},{6,2},{8,12},{10,14},{12,8},{14,10},{16,20},{18,... | collective-permute-start | bytes 3145736 | tf_op jit(solution)/shard_map/ppermute | solution.py:1450
  730.7 26.4 %collective-permute-start.18 = (bf16[1,256,1024]{2,1,0:T(8,128)(2,1)S(1)}, bf16[1,256,1024]{2,1,0:T(8,128)(2,1)S(1)}, u32[]{:S(2)}, u32[]{:S(2)}) collective-permute-start(bf16[1,256,1024]{2,1,0:T(8,128)(2,1)S(1)} %dynamic-slice_bitcast_fusion.6), channel_id=1, source_target_pairs={{0,1},{1,0},{2,3},{3,2},{4,5},{5,4},{6,7},{7,6},{8,9},{9,8},{10,11... | collective-permute-start | bytes 1572872 | tf_op jit(solution)/shard_map/ppermute | solution.py:1449
  733.7 29.1 %collective-permute-start.16 = (bf16[4,64,1024]{2,1,0:T(8,128)(2,1)S(1)}, bf16[4,64,1024]{2,1,0:T(8,128)(2,1)S(1)}, u32[]{:S(2)}, u32[]{:S(2)}) collective-permute-start(bf16[4,64,1024]{2,1,0:T(8,128)(2,1)S(1)} %dynamic-slice_bitcast_fusion.7), channel_id=1, source_target_pairs={{0,4},{2,6},{4,0},{6,2},{8,12},{10,14},{12,8},{14,10},{16,20},{18,... | collective-permute-start | bytes 1572872 | tf_op jit(solution)/shard_map/ppermute | solution.py:1450
  763.2 25.2 %collective-permute-start.24 = (bf16[8,64,384]{2,1,0:T(8,128)(2,1)S(1)}, bf16[8,64,384]{2,1,0:T(8,128)(2,1)S(1)}, u32[]{:S(2)}, u32[]{:S(2)}) collective-permute-start(bf16[8,64,384]{2,1,0:T(8,128)(2,1)S(1)} %dynamic-slice_bitcast_fusion.8), channel_id=1, source_target_pairs={{0,4},{2,6},{4,0},{6,2},{8,12},{10,14},{12,8},{14,10},{16,20},{18,... | collective-permute-start | bytes 1179656 | tf_op jit(solution)/shard_map/ppermute | solution.py:1450
  765.2 17.7 %collective-permute-start.23 = (bf16[1,128,1024]{2,1,0:T(8,128)(2,1)S(1)}, bf16[1,128,1024]{2,1,0:T(8,128)(2,1)S(1)}, u32[]{:S(2)}, u32[]{:S(2)}) collective-permute-start(bf16[1,128,1024]{2,1,0:T(8,128)(2,1)S(1)} %dynamic-slice_bitcast_fusion.11), channel_id=1, source_target_pairs={{0,16},{2,18},{4,20},{6,22},{8,24},{10,26},{12,28},{14,30},{16,0},... | collective-permute-start | bytes 786440 | tf_op jit(solution)/shard_map/ppermute | solution.py:1450
  768.3 20.1 %collective-permute-start.21 = (bf16[4,64,1024]{2,1,0:T(8,128)(2,1)S(1)}, bf16[4,64,1024]{2,1,0:T(8,128)(2,1)S(1)}, u32[]{:S(2)}, u32[]{:S(2)}) collective-permute-start(bf16[4,64,1024]{2,1,0:T(8,128)(2,1)S(1)} %dynamic-slice_bitcast_fusion.4), channel_id=1, source_target_pairs={{0,4},{2,6},{4,0},{6,2},{8,12},{10,14},{12,8},{14,10},{16,20},{18,... | collective-permute-start | bytes 1572872 | tf_op jit(solution)/shard_map/ppermute | solution.py:1450
  769.4 19.0 %collective-permute-start.20 = (bf16[1,256,1024]{2,1,0:T(8,128)(2,1)S(1)}, bf16[1,256,1024]{2,1,0:T(8,128)(2,1)S(1)}, u32[]{:S(2)}, u32[]{:S(2)}) collective-permute-start(bf16[1,256,1024]{2,1,0:T(8,128)(2,1)S(1)} %dynamic-slice_bitcast_fusion.5), channel_id=1, source_target_pairs={{0,1},{1,0},{2,3},{3,2},{4,5},{5,4},{6,7},{7,6},{8,9},{9,8},{10,11... | collective-permute-start | bytes 1572872 | tf_op jit(solution)/shard_map/ppermute | solution.py:1449
  770.9 17.5 %collective-permute-start.22 = (bf16[1,128,1024]{2,1,0:T(8,128)(2,1)S(1)}, bf16[1,128,1024]{2,1,0:T(8,128)(2,1)S(1)}, u32[]{:S(2)}, u32[]{:S(2)}) collective-permute-start(bf16[1,128,1024]{2,1,0:T(8,128)(2,1)S(1)} %dynamic-slice_bitcast_fusion.12), channel_id=1, source_target_pairs={{0,16},{2,18},{4,20},{6,22},{8,24},{10,26},{12,28},{14,30},{16,0},... | collective-permute-start | bytes 786440 | tf_op jit(solution)/shard_map/ppermute | solution.py:1450
  788.6 18.1 %collective-permute-start.29 = (bf16[1,256,384]{2,1,0:T(8,128)(2,1)S(1)}, bf16[1,256,384]{2,1,0:T(8,128)(2,1)S(1)}, u32[]{:S(2)}, u32[]{:S(2)}) collective-permute-start(bf16[1,256,384]{2,1,0:T(8,128)(2,1)S(1)} %dynamic-slice_bitcast_fusion.13), channel_id=1, source_target_pairs={{0,1},{1,0},{2,3},{3,2},{4,5},{5,4},{6,7},{7,6},{8,9},{9,8},{10,11... | collective-permute-start | bytes 589832 | tf_op jit(solution)/shard_map/ppermute | solution.py:1449
  790.0 21.4 %collective-permute-start.26 = (bf16[1,128,1024]{2,1,0:T(8,128)(2,1)S(1)}, bf16[1,128,1024]{2,1,0:T(8,128)(2,1)S(1)}, u32[]{:S(2)}, u32[]{:S(2)}) collective-permute-start(bf16[1,128,1024]{2,1,0:T(8,128)(2,1)S(1)} %dynamic-slice_bitcast_fusion.9), channel_id=1, source_target_pairs={{0,16},{2,18},{4,20},{6,22},{8,24},{10,26},{12,28},{14,30},{16,0},... | collective-permute-start | bytes 786440 | tf_op jit(solution)/shard_map/ppermute | solution.py:1450
  792.5 23.3 %collective-permute-start.25 = (bf16[1,128,1024]{2,1,0:T(8,128)(2,1)S(1)}, bf16[1,128,1024]{2,1,0:T(8,128)(2,1)S(1)}, u32[]{:S(2)}, u32[]{:S(2)}) collective-permute-start(bf16[1,128,1024]{2,1,0:T(8,128)(2,1)S(1)} %dynamic-slice_bitcast_fusion.10), channel_id=1, source_target_pairs={{0,16},{2,18},{4,20},{6,22},{8,24},{10,26},{12,28},{14,30},{16,0},... | collective-permute-start | bytes 786440 | tf_op jit(solution)/shard_map/ppermute | solution.py:1450
  793.3 13.4 %collective-permute-start.27 = (bf16[1,64,1024]{2,1,0:T(8,128)(2,1)S(1)}, bf16[1,64,1024]{2,1,0:T(8,128)(2,1)S(1)}, u32[]{:S(2)}, u32[]{:S(2)}) collective-permute-start(bf16[1,64,1024]{2,1,0:T(8,128)(2,1)S(1)} %dynamic-slice_bitcast_fusion.17), channel_id=1, source_target_pairs={{0,8},{2,10},{4,12},{6,14},{8,0},{10,2},{12,4},{14,6},{16,24},{18,... | collective-permute-start | bytes 393224 | tf_op jit(solution)/shard_map/ppermute | solution.py:1450
  796.8 45.6 %collective-permute-start.11 = (bf16[4,256,1024]{2,1,0:T(8,128)(2,1)S(1)}, bf16[4,256,1024]{2,1,0:T(8,128)(2,1)S(1)}, u32[]{:S(2)}, u32[]{:S(2)}) collective-permute-start(bf16[4,256,1024]{2,1,0:T(8,128)(2,1)S(1)} %select_bitcast_fusion), channel_id=1, source_target_pairs={{0,1},{1,0},{2,3},{3,2},{4,5},{5,4},{6,7},{7,6},{8,9},{9,8},{10,11... | collective-permute-start | bytes 6291464 | tf_op jit(solution)/shard_map/ppermute | solution.py:1576
  816.1 7.9 collective-permute-start.31
  (29 other events, 241.6 us)
Sparse Core Ops, SparseCore 0:
  13.8 140.0 all-gather.2
  156.8 143.5 all-gather.4
  469.3 203.2 reduce-scatter.1

commit v4 on v3

--- a/solution.py
+++ b/solution.py
@@ -1455,7 +1455,7 @@
     middle = ["tensor"] + ([1] if bits > 1 else [])
     if turn:
         middle = middle[::-1]
-    return ([0] if bits else []) + middle + list(reversed(range(2, bits)))
+    return ([0] if bits else []) + middle + list(range(2, bits))
 
 
 class Halving:

time: 859 us -> 852 us (level)
  waiting for transfers between devices: 207 us -> 198 us
    ppermute x24, waiting for transfers between devices: 98.7 us -> 85 us  [trade(): return lax.ppermute(values, 'dp', [(i, i ^ 1 << axis) for i in range(dp)])]
where the time goes in v4:
time: 852 us; the launch traced here: 844 us
  Pallas kernels  501 us (59%)
  waiting for transfers between devices  198 us (23%)
  other arithmetic  60.9 us (7%)
  starting transfers between devices  39.4 us (5%)
  local copies, waits for them, and re-layouts  29.5 us (3%)
  between operations  14.7 us (2%)
    pallas_call x1, Pallas kernels, backward(): pl.pallas_call(backward_kernel, grid_spec=pltpu.PrefetchScalarGridSpec(nu...  143 us
    pallas_call x1, Pallas kernels, mlp(): pl.pallas_call(mlp_kernel, grid=(2 * across,), in_specs=[rows, turned, ro...  128 us
    pallas_call x1, Pallas kernels, forward(): pl.pallas_call(forward_kernel, grid_spec=pltpu.PrefetchScalarGridSpec(num...  90.9 us
    ppermute x24, waiting for transfers between devices, trade(): return lax.ppermute(values, 'dp', [(i, i ^ 1 << axis) for i in range(dp)])  85 us
    ppermute x6, waiting for transfers between devices, trade(): return lax.ppermute(values, 'tensor', [(0, 1), (1, 0)])  74.9 us
    pallas_call x5, Pallas kernels, weight_grads(): pl.pallas_call(functools.partial(weight_grad_kernel, dp), grid_spec=pltpu...  57.8 us
    ppermute x24, starting transfers between devices, trade(): return lax.ppermute(values, 'dp', [(i, i ^ 1 << axis) for i in range(dp)])  26.3 us
    pallas_call x1, Pallas kernels, token_grad(): pl.pallas_call(token_grad_kernel, grid=(tokens // W,), in_specs=[pl.Block...  21.8 us
  transfers between devices with their start and end apart: 37, of which 22 were waited for; matrix products, arithmetic and copies ran while one was open for 9% of the time, Pallas kernels for 39%

profile of v4, /device:TPU:0, one launch (start us, length us, event | category | flops | bytes accessed | tf_op | source)
XLA Modules:
  0.0 844.1 jit_solution(8306601793173071774)
XLA Ops:
  15.3 4.0 collective-permute-start.1
  23.5 5.4 collective-permute-done.1
  29.9 3.7 collective-permute-start.2
  33.6 13.4 %collective-permute-done.2 = bf16[128,1536]{1,0:T(8,128)(2,1)S(1)} collective-permute-done((bf16[128,1536]{1,0:T(8,128)(2,1)S(1)}, bf16[128,1536]{1,0:T(8,128)(2,1)S(1)}, u32[]{:S(2)}, u32[]{:S(2)}) %collective-permute-start.2) | collective-permute-done | bytes 393248 | tf_op jit(solution)/shard_map/ppermute | solution.py:1450
  51.4 20.6 %collective-permute-done.3 = bf16[256,1536]{1,0:T(8,128)(2,1)} collective-permute-done((bf16[256,1536]{1,0:T(8,128)(2,1)S(1)}, bf16[256,1536]{1,0:T(8,128)(2,1)}, u32[]{:S(2)}, u32[]{:S(2)}) %collective-permute-start.3) | collective-permute-done | bytes 786464 | tf_op jit(solution)/shard_map/ppermute | solution.py:1450
  73.5 9.0 %collective-permute-done = bf16[4,256,1024]{2,1,0:T(8,128)(2,1)} collective-permute-done((bf16[4,256,1024]{2,1,0:T(8,128)(2,1)S(1)}, bf16[4,256,1024]{2,1,0:T(8,128)(2,1)}, u32[]{:S(2)}, u32[]{:S(2)}) %collective-permute-start) | collective-permute-done | bytes 2097184 | tf_op jit(solution)/shard_map/ppermute | solution.py:1564
  88.9 53.3 %collective-permute-done.4 = bf16[512,1536]{1,0:T(8,128)(2,1)S(1)} collective-permute-done((bf16[512,1536]{1,0:T(8,128)(2,1)S(1)}, bf16[512,1536]{1,0:T(8,128)(2,1)S(1)}, u32[]{:S(2)}, u32[]{:S(2)}) %collective-permute-start.4) | collective-permute-done | bytes 1572896 | tf_op jit(solution)/shard_map/ppermute | solution.py:1449
  143.0 6.2 collective-permute-done.5
  155.3 3.9 select_bitcast_fusion.2
  166.2 19.0 %project.1 = (bf16[1024,2048]{1,0:T(8,128)(2,1)}, bf16[2048,1024]{1,0:T(8,128)(2,1)}, bf16[2048,1024]{1,0:T(8,128)(2,1)}, bf16[2048,1024]{1,0:T(8,128)(2,1)}) custom-call(bf16[2048,1024]{1,0:T(8,128)(2,1)} %bitcast.283, f32[1,1024]{1,0:T(1,128)} %squeeze.138.gain, ...), custom_call_target="tpu_custom_call" | custom-call | flops 12884901888 | bytes 27262976 | tf_op jit(solution)/shard_map/project/pallas_call | solution.py:675
  185.1 90.9 %forward.1 = (bf16[2048,1024]{1,0:T(8,128)(2,1)}, bf16[2048,1024]{1,0:T(8,128)(2,1)}, bf16[1024,2048]{1,0:T(8,128)(2,1)}, bf16[2048,1024]{1,0:T(8,128)(2,1)}, bf...) custom-call(s32[8]{0:T(128)} %convert_element_type.383.flags, ...), custom_call_target="tpu_custom_call" | custom-call | flops 41999998976 | bytes 100000000 | tf_op jit(solution)/shard_map/forward/pallas_call | solution.py:811
  276.7 3.5 bitcast_select_fusion.5
  282.6 16.3 %all-gather.5.cloned.1.call-done.w0.w1.weights = bf16[2048,4608]{1,0:T(8,128)(2,1)} async-done(((bf16[64,4608]{1,0:T(8,128)(2,1)}), bf16[2048,4608]{1,0:T(8,128)(2,1)}) %all-gather.5.cloned.1.call-update) | async-done | bytes 18874384 | tf_op jit(solution)/shard_map/all_gather | solution.py:1430
  298.9 14.7 %middle.1 = (f32[2048,1024]{1,0:T(8,128)}, bf16[2048,1024]{1,0:T(8,128)(2,1)}, bf16[1024,2048]{1,0:T(8,128)(2,1)}, bf16[1024,2048]{1,0:T(8,128)(2,1)}) custom-call(bf16[2048,1024]{1,0:T(8,128)(2,1)} %bitcast.284, bf16[2048,1024]{1,0:T(8,128)(2,1)} %get-tuple-element.102.mixed.right.token_mixed, ...), custom_call_target="tpu_custom_call" | custom-call | flops 4294967296 | bytes 33554432 | tf_op jit(solution)/shard_map/middle/pallas_call | solution.py:887
  313.6 127.5 %mlp.1 = (bf16[2048,1024]{1,0:T(8,128)(2,1)}, bf16[2048,1024]{1,0:T(8,128)(2,1)}, bf16[2048,4608]{1,0:T(8,128)(2,1)}) custom-call(bf16[2048,1024]{1,0:T(8,128)(2,1)} %get-tuple-element.107.mlp_in, bf16[1024,2048]{1,0:T(8,128)(2,1)} %get-tuple-element.108.mlp_turned, bf16[2048,1024]{1,0:T(8,128)(2,1)} %bitcast.281, ...), custom_call_target="tpu_custom_call" | custom-call | flops 102999998464 | bytes 60000000 | tf_op jit(solution)/shard_map/mlp/pallas_call | solution.py:961
  441.1 18.0 %after_mlp.1 = (bf16[2048,1024]{1,0:T(8,128)(2,1)}, bf16[2048,1024]{1,0:T(8,128)(2,1)}, bf16[1024,2048]{1,0:T(8,128)(2,1)}, bf16[2048,1024]{1,0:T(8,128)(2,1)}, f32[1,1024]{1,0:T(1,128)}) custom-call(f32[2048,1024]{1,0:T(8,128)} %get-tuple-element.106.middle, bf16[2048,1024]{1,0:T(8,128)(2,1)} %get-tuple-element.110.mlp_out, ...), custom_call_target="tpu_custom_call" | custom-call | flops 4294967296 | bytes 33554432 | tf_op jit(solution)/shard_map/after_mlp/pallas_call | solution.py:1010
  459.1 8.5 %whole_weight_grad.1 = bf16[2048,4608]{1,0:T(8,128)(2,1)} custom-call(bf16[1024,2048]{1,0:T(8,128)(2,1)} %get-tuple-element.118.turned, bf16[2048,1024]{1,0:T(8,128)(2,1)} %get-tuple-element.102.mixed.right.token_mixed, bf16[2048,4608]{1,0:T(8,128)(2,1)} %get-tuple-element.119.into), custom_call_target="tpu_custom_call", output_to_operand_aliasing={{}: (2, {})} | custom-call | flops 4294967296 | bytes 8388608 | tf_op jit(solution)/shard_map/whole_weight_grad/pallas_call | solution.py:1322
  471.6 143.0 %backward.1 = (bf16[3,2048,1024]{2,1,0:T(8,128)(2,1)}, bf16[4,2048,1024]{2,1,0:T(8,128)(2,1)}, bf16[1024,2048]{1,0:T(8,128)(2,1)}, bf16[512,1024]{1,0:T(8,128)(2...) custom-call(s32[8]{0:T(128)} %convert_element_type.383.flags, bf16[2048,1024]{1,0:T(8,128)(2,1)} %get-tuple-element.98.query, ...), custom_call_target="tpu_custom_call" | custom-call | flops 70000001024 | bytes 100000000 | tf_op jit(solution)/shard_map/backward/pallas_call | solution.py:1243
  620.2 13.3 %weight_grads.5 = (bf16[1024,1024]{1,0:T(8,128)(2,1)}, bf16[1024,1024]{1,0:T(8,128)(2,1)}) custom-call(s32[1]{0:T(128)} %bitcast.41.core, bf16[1024,2048]{1,0:T(8,128)(2,1)} %get-tuple-element.129.turned, bf16[4,2048,1024]{2,1,0:T(8,128)(2,1)} %get-tuple-element.134.right), custom_call_target="tpu_custom_call" | custom-call | flops 8589934592 | bytes 12582912 | tf_op jit(solution)/shard_map/weight_grads/pallas_call | solution.py:1359
  633.6 13.5 %weight_grads.6 = (bf16[1024,1024]{1,0:T(8,128)(2,1)}, bf16[1024,1024]{1,0:T(8,128)(2,1)}) custom-call(s32[1]{0:T(128)} %bitcast.41.core, bf16[1024,2048]{1,0:T(8,128)(2,1)} %get-tuple-element.129.turned, bf16[4,2048,1024]{2,1,0:T(8,128)(2,1)} %get-tuple-element.134.right), custom_call_target="tpu_custom_call" | custom-call | flops 8589934592 | bytes 12582912 | tf_op jit(solution)/shard_map/weight_grads/pallas_call | solution.py:1359
  652.5 13.8 %weight_grads.7 = (bf16[1024,1024]{1,0:T(8,128)(2,1)}, bf16[1024,1024]{1,0:T(8,128)(2,1)}) custom-call(s32[1]{0:T(128)} %bitcast.41.core, bf16[1024,2048]{1,0:T(8,128)(2,1)} %get-tuple-element.128.turned, bf16[3,2048,1024]{2,1,0:T(8,128)(2,1)} %get-tuple-element.148.right.grads), custom_call_target="tpu_custom_call" | custom-call | flops 8589934592 | bytes 12582912 | tf_op jit(solution)/shard_map/weight_grads/pallas_call | solution.py:1359
  671.4 8.5 %weight_grads.8 = (bf16[1024,1024]{1,0:T(8,128)(2,1)}, bf16[1024,1024]{1,0:T(8,128)(2,1)}) custom-call(s32[1]{0:T(128)} %bitcast.41.core, bf16[1024,2048]{1,0:T(8,128)(2,1)} %get-tuple-element.128.turned, bf16[3,2048,1024]{2,1,0:T(8,128)(2,1)} %get-tuple-element.148.right.grads), custom_call_target="tpu_custom_call" | custom-call | flops 4294967296 | bytes 8388608 | tf_op jit(solution)/shard_map/weight_grads/pallas_call | solution.py:1359
  684.3 8.6 %weight_grads.9 = (bf16[1024,1024]{1,0:T(8,128)(2,1)}, bf16[1024,1024]{1,0:T(8,128)(2,1)}) custom-call(s32[1]{0:T(128)} %bitcast.41.core, bf16[1024,2048]{1,0:T(8,128)(2,1)} %get-tuple-element.146.turned, bf16[1,2048,1024]{2,1,0:T(8,128)(2,1)} %bitcast.353, ...), custom_call_target="tpu_custom_call", output_to_operand_aliasing={{0}: (3, {}), {1}: (4, {})} | custom-call | flops 4294967296 | bytes 8388608 | tf_op jit(solution)/shard_map/weight_grads/pallas_call | solution.py:1359
  698.7 21.8 %token_grad.1 = (bf16[2048,1024]{1,0:T(8,128)(2,1)}, f32[1,1024]{1,0:T(1,128)}) custom-call(bf16[3,2048,1024]{2,1,0:T(8,128)(2,1)} %get-tuple-element.148.right.grads, bf16[2048,2944]{1,0:T(8,128)(2,1)} %all-gather.3.cloned.1.call-done.w0.w1.query0.query1.key0.key1.weight_query.weight_key, ...), custom_call_target="tpu_custom_call" | custom-call | flops 12884901888 | bytes 25165824 | tf_op jit(solution)/shard_map/token_grad/pallas_call | solution.py:1410
  733.9 11.6 %collective-permute-done.14 = bf16[1,512,1024]{2,1,0:T(8,128)(2,1)} collective-permute-done((bf16[1,512,1024]{2,1,0:T(8,128)(2,1)}, bf16[1,512,1024]{2,1,0:T(8,128)(2,1)}, u32[]{:S(2)}, u32[]{:S(2)}) %collective-permute-start.14) | collective-permute-done | bytes 1048608 | tf_op jit(solution)/shard_map/ppermute | solution.py:1449
  745.5 10.0 %collective-permute-done.18 = bf16[1,256,1024]{2,1,0:T(8,128)(2,1)S(1)} collective-permute-done((bf16[1,256,1024]{2,1,0:T(8,128)(2,1)S(1)}, bf16[1,256,1024]{2,1,0:T(8,128)(2,1)S(1)}, u32[]{:S(2)}, u32[]{:S(2)}) %collective-permute-start.18) | collective-permute-done | bytes 524320 | tf_op jit(solution)/shard_map/ppermute | solution.py:1449
  755.5 5.8 collective-permute-done.16
  772.0 3.7 collective-permute-done.22
  775.8 6.6 collective-permute-done.21
  793.1 6.7 collective-permute-done.27
  807.6 6.3 collective-permute-done.31
  821.6 13.0 %collective-permute-done.11 = bf16[4,256,1024]{2,1,0:T(8,128)(2,1)S(1)} collective-permute-done((bf16[4,256,1024]{2,1,0:T(8,128)(2,1)S(1)}, bf16[4,256,1024]{2,1,0:T(8,128)(2,1)S(1)}, u32[]{:S(2)}, u32[]{:S(2)}) %collective-permute-start.11) | collective-permute-done | bytes 2097184 | tf_op jit(solution)/shard_map/ppermute | solution.py:1576
  (223 shorter events, 125.2 us)
Async XLA Ops:
  7.2 147.4 %all-gather.3.cloned.1.call-start = ((), (), s32[]{:S(2)}) async-start(), calls=%async_computation.1 | async-start | bytes 12435456 | tf_op jit(solution)/shard_map/all_gather | solution.py:1430
  13.7 285.2 %all-gather.5.cloned.1.call-start = ((), (), s32[]{:S(2)}) async-start(), calls=%async_computation.2 | async-start | bytes 19464192 | tf_op jit(solution)/shard_map/all_gather | solution.py:1430
  15.3 13.5 %collective-permute-start.1 = (bf16[64,1536]{1,0:T(8,128)(2,1)}, bf16[64,1536]{1,0:T(8,128)(2,1)}, u32[]{:S(2)}, u32[]{:S(2)}) collective-permute-start(bf16[64,1536]{1,0:T(8,128)(2,1)} %pad_maximum_fusion.10), channel_id=1, source_target_pairs={{0,16},{2,18},{4,20},{6,22},{8,24},{10,26},{12,28},{14,30},{16,0},... | collective-permute-start | bytes 589832 | tf_op jit(solution)/shard_map/ppermute | solution.py:1450
  21.9 60.7 %collective-permute-start = (bf16[4,256,1024]{2,1,0:T(8,128)(2,1)S(1)}, bf16[4,256,1024]{2,1,0:T(8,128)(2,1)}, u32[]{:S(2)}, u32[]{:S(2)}) collective-permute-start(bf16[4,256,1024]{2,1,0:T(8,128)(2,1)S(1)} %select_bitcast_fusion.3), channel_id=1, source_target_pairs={{0,1},{1,0},{2,3},{3,2},{4,5},{5,4},{6,7},{7,6},{8,9},{9,8},{10,11... | collective-permute-start | bytes 6291464 | tf_op jit(solution)/shard_map/ppermute | solution.py:1564
  29.9 17.0 %collective-permute-start.2 = (bf16[128,1536]{1,0:T(8,128)(2,1)S(1)}, bf16[128,1536]{1,0:T(8,128)(2,1)S(1)}, u32[]{:S(2)}, u32[]{:S(2)}) collective-permute-start(bf16[128,1536]{1,0:T(8,128)(2,1)S(1)} %bitcast.332), channel_id=1, source_target_pairs={{0,8},{2,10},{4,12},{6,14},{8,0},{10,2},{12,4},{14,6},{16,24},{18,... | collective-permute-start | bytes 1179656 | tf_op jit(solution)/shard_map/ppermute | solution.py:1450
  47.1 24.8 %collective-permute-start.3 = (bf16[256,1536]{1,0:T(8,128)(2,1)S(1)}, bf16[256,1536]{1,0:T(8,128)(2,1)}, u32[]{:S(2)}, u32[]{:S(2)}) collective-permute-start(bf16[256,1536]{1,0:T(8,128)(2,1)S(1)} %bitcast.320), channel_id=1, source_target_pairs={{0,4},{2,6},{4,0},{6,2},{8,12},{10,14},{12,8},{14,10},{16,20},{18,... | collective-permute-start | bytes 2359304 | tf_op jit(solution)/shard_map/ppermute | solution.py:1450
  87.0 55.1 %collective-permute-start.4 = (bf16[512,1536]{1,0:T(8,128)(2,1)S(1)}, bf16[512,1536]{1,0:T(8,128)(2,1)S(1)}, u32[]{:S(2)}, u32[]{:S(2)}) collective-permute-start(bf16[512,1536]{1,0:T(8,128)(2,1)S(1)} %bitcast.306), channel_id=1, source_target_pairs={{0,1},{1,0},{2,3},{3,2},{4,5},{5,4},{6,7},{7,6},{8,9},{9,8},{10,11... | collective-permute-start | bytes 4718600 | tf_op jit(solution)/shard_map/ppermute | solution.py:1449
  154.7 544.0 %reduce-scatter.2.cloned.1.call-start = ((), (), s32[]{:S(2)}) async-start(), calls=%async_computation.3 | async-start | bytes 19464192 | tf_op jit(solution)/shard_map/reduce_scatter | solution.py:1434
  159.3 116.8 %collective-permute-start.6 = (bf16[4,256,1024]{2,1,0:T(8,128)(2,1)}, bf16[4,256,1024]{2,1,0:T(8,128)(2,1)}, u32[]{:S(2)}, u32[]{:S(2)}) collective-permute-start(bf16[4,256,1024]{2,1,0:T(8,128)(2,1)} %select_bitcast_fusion.2), channel_id=1, source_target_pairs={{0,1},{1,0},{2,3},{3,2},{4,5},{5,4},{6,7},{7,6},{8,9},{9,8},{10,11... | collective-permute-start | bytes 6291464 | tf_op jit(solution)/shard_map/ppermute | solution.py:1564
  470.1 144.5 %collective-permute-start.7 = (bf16[4,256,1024]{2,1,0:T(8,128)(2,1)S(1)}, bf16[4,256,1024]{2,1,0:T(8,128)(2,1)}, u32[]{:S(2)}, u32[]{:S(2)}) collective-permute-start(bf16[4,256,1024]{2,1,0:T(8,128)(2,1)S(1)} %select_bitcast_fusion.1), channel_id=1, source_target_pairs={{0,1},{1,0},{2,3},{3,2},{4,5},{5,4},{6,7},{7,6},{8,9},{9,8},{10,11... | collective-permute-start | bytes 6291464 | tf_op jit(solution)/shard_map/ppermute | solution.py:1576
  633.5 14.0 %collective-permute-start.8 = (bf16[1024,1024]{1,0:T(8,128)(2,1)}, bf16[1024,1024]{1,0:T(8,128)(2,1)}, u32[]{:S(2)}, u32[]{:S(2)}) collective-permute-start(bf16[1024,1024]{1,0:T(8,128)(2,1)} %get-tuple-element.133), channel_id=1, source_target_pairs={{0,2},{2,0},{4,6},{6,4},{8,10},{10,8},{12,14},{14,12},{16,18},{18,... | collective-permute-start | bytes 6291464 | tf_op jit(solution)/shard_map/ppermute | solution.py:1450
  647.1 19.3 %collective-permute-start.10 = (bf16[1024,1024]{1,0:T(8,128)(2,1)}, bf16[1024,1024]{1,0:T(8,128)(2,1)}, u32[]{:S(2)}, u32[]{:S(2)}) collective-permute-start(bf16[1024,1024]{1,0:T(8,128)(2,1)} %get-tuple-element.137), channel_id=1, source_target_pairs={{0,2},{2,0},{4,6},{6,4},{8,10},{10,8},{12,14},{14,12},{16,18},{18,... | collective-permute-start | bytes 6291464 | tf_op jit(solution)/shard_map/ppermute | solution.py:1450
  666.3 13.6 %collective-permute-start.9 = (bf16[1024,1024]{1,0:T(8,128)(2,1)}, bf16[1024,1024]{1,0:T(8,128)(2,1)}, u32[]{:S(2)}, u32[]{:S(2)}) collective-permute-start(bf16[1024,1024]{1,0:T(8,128)(2,1)} %get-tuple-element.140), channel_id=1, source_target_pairs={{0,2},{2,0},{4,6},{6,4},{8,10},{10,8},{12,14},{14,12},{16,18},{18,... | collective-permute-start | bytes 6291464 | tf_op jit(solution)/shard_map/ppermute | solution.py:1450
  692.9 29.0 %collective-permute-start.12 = (bf16[1024,1024]{1,0:T(8,128)(2,1)}, bf16[1024,1024]{1,0:T(8,128)(2,1)}, u32[]{:S(2)}, u32[]{:S(2)}) collective-permute-start(bf16[1024,1024]{1,0:T(8,128)(2,1)} %get-tuple-element.147), channel_id=1, source_target_pairs={{0,2},{2,0},{4,6},{6,4},{8,10},{10,8},{12,14},{14,12},{16,18},{18,... | collective-permute-start | bytes 6291464 | tf_op jit(solution)/shard_map/ppermute | solution.py:1450
  696.3 25.5 %collective-permute-start.17 = (bf16[8,64,1024]{2,1,0:T(8,128)(2,1)}, bf16[8,64,1024]{2,1,0:T(8,128)(2,1)}, u32[]{:S(2)}, u32[]{:S(2)}) collective-permute-start(bf16[8,64,1024]{2,1,0:T(8,128)(2,1)} %dynamic-slice_bitcast_fusion.2), channel_id=1, source_target_pairs={{0,4},{2,6},{4,0},{6,2},{8,12},{10,14},{12,8},{14,10},{16,20},{18,... | collective-permute-start | bytes 3145736 | tf_op jit(solution)/shard_map/ppermute | solution.py:1450
  696.6 33.7 %collective-permute-start.15 = (bf16[1,512,1024]{2,1,0:T(8,128)(2,1)}, bf16[1,512,1024]{2,1,0:T(8,128)(2,1)}, u32[]{:S(2)}, u32[]{:S(2)}) collective-permute-start(bf16[1,512,1024]{2,1,0:T(8,128)(2,1)} %dynamic-slice_bitcast_fusion.3), channel_id=1, source_target_pairs={{0,1},{1,0},{2,3},{3,2},{4,5},{5,4},{6,7},{7,6},{8,9},{9,8},{10,11... | collective-permute-start | bytes 3145736 | tf_op jit(solution)/shard_map/ppermute | solution.py:1449
  698.2 47.3 %collective-permute-start.14 = (bf16[1,512,1024]{2,1,0:T(8,128)(2,1)}, bf16[1,512,1024]{2,1,0:T(8,128)(2,1)}, u32[]{:S(2)}, u32[]{:S(2)}) collective-permute-start(bf16[1,512,1024]{2,1,0:T(8,128)(2,1)} %dynamic-slice_bitcast_fusion.1), channel_id=1, source_target_pairs={{0,1},{1,0},{2,3},{3,2},{4,5},{5,4},{6,7},{7,6},{8,9},{9,8},{10,11... | collective-permute-start | bytes 3145736 | tf_op jit(solution)/shard_map/ppermute | solution.py:1449
  721.7 39.7 %collective-permute-start.19 = (bf16[1024,384]{1,0:T(8,128)(2,1)S(1)}, bf16[1024,384]{1,0:T(8,128)(2,1)S(1)}, u32[]{:S(2)}, u32[]{:S(2)}) collective-permute-start(bf16[1024,384]{1,0:T(8,128)(2,1)S(1)} %bitcast.338), channel_id=1, source_target_pairs={{0,2},{2,0},{4,6},{6,4},{8,10},{10,8},{12,14},{14,12},{16,18},{18,... | collective-permute-start | bytes 2359304 | tf_op jit(solution)/shard_map/ppermute | solution.py:1450
  725.6 35.7 %collective-permute-start.13 = (bf16[8,64,1024]{2,1,0:T(8,128)(2,1)S(1)}, bf16[8,64,1024]{2,1,0:T(8,128)(2,1)S(1)}, u32[]{:S(2)}, u32[]{:S(2)}) collective-permute-start(bf16[8,64,1024]{2,1,0:T(8,128)(2,1)S(1)} %dynamic-slice_bitcast_fusion), channel_id=1, source_target_pairs={{0,4},{2,6},{4,0},{6,2},{8,12},{10,14},{12,8},{14,10},{16,20},{18,... | collective-permute-start | bytes 3145736 | tf_op jit(solution)/shard_map/ppermute | solution.py:1450
  729.1 26.4 %collective-permute-start.18 = (bf16[1,256,1024]{2,1,0:T(8,128)(2,1)S(1)}, bf16[1,256,1024]{2,1,0:T(8,128)(2,1)S(1)}, u32[]{:S(2)}, u32[]{:S(2)}) collective-permute-start(bf16[1,256,1024]{2,1,0:T(8,128)(2,1)S(1)} %dynamic-slice_bitcast_fusion.6), channel_id=1, source_target_pairs={{0,1},{1,0},{2,3},{3,2},{4,5},{5,4},{6,7},{7,6},{8,9},{9,8},{10,11... | collective-permute-start | bytes 1572872 | tf_op jit(solution)/shard_map/ppermute | solution.py:1449
  732.2 29.1 %collective-permute-start.16 = (bf16[4,64,1024]{2,1,0:T(8,128)(2,1)S(1)}, bf16[4,64,1024]{2,1,0:T(8,128)(2,1)S(1)}, u32[]{:S(2)}, u32[]{:S(2)}) collective-permute-start(bf16[4,64,1024]{2,1,0:T(8,128)(2,1)S(1)} %dynamic-slice_bitcast_fusion.7), channel_id=1, source_target_pairs={{0,4},{2,6},{4,0},{6,2},{8,12},{10,14},{12,8},{14,10},{16,20},{18,... | collective-permute-start | bytes 1572872 | tf_op jit(solution)/shard_map/ppermute | solution.py:1450
  761.7 14.1 %collective-permute-start.24 = (bf16[8,64,384]{2,1,0:T(8,128)(2,1)S(1)}, bf16[8,64,384]{2,1,0:T(8,128)(2,1)S(1)}, u32[]{:S(2)}, u32[]{:S(2)}) collective-permute-start(bf16[8,64,384]{2,1,0:T(8,128)(2,1)S(1)} %dynamic-slice_bitcast_fusion.8), channel_id=1, source_target_pairs={{0,4},{2,6},{4,0},{6,2},{8,12},{10,14},{12,8},{14,10},{16,20},{18,... | collective-permute-start | bytes 1179656 | tf_op jit(solution)/shard_map/ppermute | solution.py:1450
  763.7 8.3 collective-permute-start.23
  765.7 16.7 %collective-permute-start.21 = (bf16[4,64,1024]{2,1,0:T(8,128)(2,1)S(1)}, bf16[4,64,1024]{2,1,0:T(8,128)(2,1)S(1)}, u32[]{:S(2)}, u32[]{:S(2)}) collective-permute-start(bf16[4,64,1024]{2,1,0:T(8,128)(2,1)S(1)} %dynamic-slice_bitcast_fusion.4), channel_id=1, source_target_pairs={{0,4},{2,6},{4,0},{6,2},{8,12},{10,14},{12,8},{14,10},{16,20},{18,... | collective-permute-start | bytes 1572872 | tf_op jit(solution)/shard_map/ppermute | solution.py:1450
  766.6 15.8 %collective-permute-start.20 = (bf16[1,256,1024]{2,1,0:T(8,128)(2,1)S(1)}, bf16[1,256,1024]{2,1,0:T(8,128)(2,1)S(1)}, u32[]{:S(2)}, u32[]{:S(2)}) collective-permute-start(bf16[1,256,1024]{2,1,0:T(8,128)(2,1)S(1)} %dynamic-slice_bitcast_fusion.5), channel_id=1, source_target_pairs={{0,1},{1,0},{2,3},{3,2},{4,5},{5,4},{6,7},{7,6},{8,9},{9,8},{10,11... | collective-permute-start | bytes 1572872 | tf_op jit(solution)/shard_map/ppermute | solution.py:1449
  782.6 17.2 %collective-permute-start.29 = (bf16[1,256,384]{2,1,0:T(8,128)(2,1)S(1)}, bf16[1,256,384]{2,1,0:T(8,128)(2,1)S(1)}, u32[]{:S(2)}, u32[]{:S(2)}) collective-permute-start(bf16[1,256,384]{2,1,0:T(8,128)(2,1)S(1)} %dynamic-slice_bitcast_fusion.13), channel_id=1, source_target_pairs={{0,1},{1,0},{2,3},{3,2},{4,5},{5,4},{6,7},{7,6},{8,9},{9,8},{10,11... | collective-permute-start | bytes 589832 | tf_op jit(solution)/shard_map/ppermute | solution.py:1449
  785.9 13.9 %collective-permute-start.26 = (bf16[2,64,1024]{2,1,0:T(8,128)(2,1)S(1)}, bf16[2,64,1024]{2,1,0:T(8,128)(2,1)S(1)}, u32[]{:S(2)}, u32[]{:S(2)}) collective-permute-start(bf16[2,64,1024]{2,1,0:T(8,128)(2,1)S(1)} %dynamic-slice_bitcast_fusion.9), channel_id=1, source_target_pairs={{0,8},{2,10},{4,12},{6,14},{8,0},{10,2},{12,4},{14,6},{16,24},{18,... | collective-permute-start | bytes 786440 | tf_op jit(solution)/shard_map/ppermute | solution.py:1450
  786.6 15.6 %collective-permute-start.25 = (bf16[2,64,1024]{2,1,0:T(8,128)(2,1)S(1)}, bf16[2,64,1024]{2,1,0:T(8,128)(2,1)S(1)}, u32[]{:S(2)}, u32[]{:S(2)}) collective-permute-start(bf16[2,64,1024]{2,1,0:T(8,128)(2,1)S(1)} %dynamic-slice_bitcast_fusion.10), channel_id=1, source_target_pairs={{0,8},{2,10},{4,12},{6,14},{8,0},{10,2},{12,4},{14,6},{16,24},{18,... | collective-permute-start | bytes 786440 | tf_op jit(solution)/shard_map/ppermute | solution.py:1450
  788.3 11.5 %collective-permute-start.27 = (bf16[1,64,1024]{2,1,0:T(8,128)(2,1)S(1)}, bf16[1,64,1024]{2,1,0:T(8,128)(2,1)S(1)}, u32[]{:S(2)}, u32[]{:S(2)}) collective-permute-start(bf16[1,64,1024]{2,1,0:T(8,128)(2,1)S(1)} %constant_dynamic-slice_fusion.4), channel_id=1, source_target_pairs={{0,16},{2,18},{4,20},{6,22},{8,24},{10,26},{12,28},{14,30},{16,0},... | collective-permute-start | bytes 393224 | tf_op jit(solution)/shard_map/ppermute | solution.py:1450
  792.5 42.2 %collective-permute-start.11 = (bf16[4,256,1024]{2,1,0:T(8,128)(2,1)S(1)}, bf16[4,256,1024]{2,1,0:T(8,128)(2,1)S(1)}, u32[]{:S(2)}, u32[]{:S(2)}) collective-permute-start(bf16[4,256,1024]{2,1,0:T(8,128)(2,1)S(1)} %select_bitcast_fusion), channel_id=1, source_target_pairs={{0,1},{1,0},{2,3},{3,2},{4,5},{5,4},{6,7},{7,6},{8,9},{9,8},{10,11... | collective-permute-start | bytes 6291464 | tf_op jit(solution)/shard_map/ppermute | solution.py:1576
  802.7 11.2 %collective-permute-start.31 = (bf16[1,64,1024]{2,1,0:T(8,128)(2,1)S(1)}, bf16[1,64,1024]{2,1,0:T(8,128)(2,1)S(1)}, u32[]{:S(2)}, u32[]{:S(2)}) collective-permute-start(bf16[1,64,1024]{2,1,0:T(8,128)(2,1)S(1)} %constant_dynamic-slice_fusion.1), channel_id=1, source_target_pairs={{0,16},{2,18},{4,20},{6,22},{8,24},{10,26},{12,28},{14,30},{16,0},... | collective-permute-start | bytes 393224 | tf_op jit(solution)/shard_map/ppermute | solution.py:1450
  803.9 11.4 %collective-permute-start.30 = (bf16[1,64,1024]{2,1,0:T(8,128)(2,1)S(1)}, bf16[1,64,1024]{2,1,0:T(8,128)(2,1)S(1)}, u32[]{:S(2)}, u32[]{:S(2)}) collective-permute-start(bf16[1,64,1024]{2,1,0:T(8,128)(2,1)S(1)} %constant_dynamic-slice_fusion.2), channel_id=1, source_target_pairs={{0,16},{2,18},{4,20},{6,22},{8,24},{10,26},{12,28},{14,30},{16,0},... | collective-permute-start | bytes 393224 | tf_op jit(solution)/shard_map/ppermute | solution.py:1450
  (29 other events, 252.2 us)
Sparse Core Ops, SparseCore 0:
  13.8 136.1 all-gather.2
  154.8 144.0 all-gather.4
  467.8 203.2 reduce-scatter.1

commit v5 on v4

--- a/solution.py
+++ b/solution.py
@@ -870,7 +870,7 @@
     here = (
         rows[...].astype(F32) + nt(mixed[:, :width], w0[...]) + nt(mixed[:, width:], w1[...])
     )
-    middle[...] = here
+    middle[...] = here.astype(BF)
     low = (here * inverse_rms(here) * gain[...]).astype(BF)
     mlp_in[...] = low
     mlp_turned[...] = low.T
@@ -897,7 +897,7 @@
         ],
         out_specs=[block, block, turned, turned],
         out_shape=[
-            jax.ShapeDtypeStruct((tokens, D), F32),
+            low,
             low,
             jax.ShapeDtypeStruct((D, tokens), BF),
             jax.ShapeDtypeStruct((D, tokens), BF),
@@ -980,7 +980,7 @@
     middle, mlp_out, grad_in, cot, gain, w0, w1, output, grad_middle, turned, grad_mixed, grad_gain
 ):
     width = w0.shape[1]
-    here = middle[...]
+    here = middle[...].astype(F32)
     inverse = inverse_rms(here)
     scaled = here * inverse
     grad = grad_in[...].astype(F32)
@@ -1560,8 +1560,8 @@
     across = w_up.shape[1] // units
     swap = [(0, 1), (1, 0)]
 
-    def other_half(pair):
-        return lax.ppermute(jnp.where(first, pair[1, 0], pair[0, 0]), "tensor", swap)
+    def half_of(pair):
+        return jnp.where(first, pair[1, 0], pair[0, 0])
 
     def bring(pair, come):
         keep = jnp.where(first, pair[0, 0], pair[1, 0])
@@ -1596,9 +1596,10 @@
     for unit in range(0, across * units, units):
         late += [w_up[:, unit : unit + units], turned_down[:, unit : unit + units]]
     late = jnp.concatenate(late + [w_out.T], axis=1)
-    rows = bring(tokens_in, other_half(tokens_in))
+    rows = bring(tokens_in, lax.ppermute(half_of(tokens_in), "tensor", swap))
+    cot_send = half_of(cotangent)
     full_state1 = gather_steps(
-        jnp.concatenate([w_state_value, w_gate, w_state_out.T], axis=1), dp, False, (rows, late)
+        jnp.concatenate([w_state_value, w_gate, w_state_out.T], axis=1), dp, False, (rows, late, cot_send)
     )
     full_late = gather(after(late, (full_qkv, full_state1)))
     side = width // 2
@@ -1607,7 +1608,7 @@
     gains = full_small[:D, side:].reshape(dp, local_rows, 128)[:, :4, :local_rows]
     gains = jnp.transpose(gains, (1, 0, 2)).reshape(4, 1, D).astype(F32)
 
-    cot_half = other_half(after(cotangent, rows))
+    cot_half = lax.ppermute(after(cot_send, full_qkv), "tensor", swap)
     starts = jnp.where(first, piece_starts[0, 0], piece_starts[1, 0])
     flags = jnp.any(
         starts[:, None] == PIECE * jnp.arange(NB * W // PIECE, dtype=jnp.int32)[None], axis=0

time: 852 us -> 850 us (level)
  no operation moved by 1% of the time
where the time goes in v5:
time: 850 us; the launch traced here: 843 us
  Pallas kernels  500 us (59%)
  waiting for transfers between devices  199 us (23%)
  other arithmetic  60.8 us (7%)
  starting transfers between devices  39.1 us (5%)
  local copies, waits for them, and re-layouts  29 us (3%)
  between operations  14.7 us (2%)
    pallas_call x1, Pallas kernels, backward(): pl.pallas_call(backward_kernel, grid_spec=pltpu.PrefetchScalarGridSpec(nu...  143 us
    pallas_call x1, Pallas kernels, mlp(): pl.pallas_call(mlp_kernel, grid=(2 * across,), in_specs=[rows, turned, ro...  127 us
    pallas_call x1, Pallas kernels, forward(): pl.pallas_call(forward_kernel, grid_spec=pltpu.PrefetchScalarGridSpec(num...  90.9 us
    ppermute x24, waiting for transfers between devices, trade(): return lax.ppermute(values, 'dp', [(i, i ^ 1 << axis) for i in range(dp)])  82.2 us
    ppermute x6, waiting for transfers between devices, trade(): return lax.ppermute(values, 'tensor', [(0, 1), (1, 0)])  74.9 us
    pallas_call x5, Pallas kernels, weight_grads(): pl.pallas_call(functools.partial(weight_grad_kernel, dp), grid_spec=pltpu...  57.8 us
    ppermute x24, starting transfers between devices, trade(): return lax.ppermute(values, 'dp', [(i, i ^ 1 << axis) for i in range(dp)])  26.2 us
    pallas_call x1, Pallas kernels, token_grad(): pl.pallas_call(token_grad_kernel, grid=(tokens // W,), in_specs=[pl.Block...  21.8 us
  transfers between devices with their start and end apart: 37, of which 22 were waited for; matrix products, arithmetic and copies ran while one was open for 9% of the time, Pallas kernels for 39%

profile of v5, /device:TPU:0, one launch (start us, length us, event | category | flops | bytes accessed | tf_op | source)
XLA Modules:
  0.0 842.8 jit_solution(1946149953229210502)
XLA Ops:
  15.3 4.0 collective-permute-start.1
  23.5 5.3 collective-permute-done.1
  29.9 3.7 collective-permute-start.2
  33.6 13.4 %collective-permute-done.2 = bf16[128,1536]{1,0:T(8,128)(2,1)S(1)} collective-permute-done((bf16[128,1536]{1,0:T(8,128)(2,1)S(1)}, bf16[128,1536]{1,0:T(8,128)(2,1)S(1)}, u32[]{:S(2)}, u32[]{:S(2)}) %collective-permute-start.2) | collective-permute-done | bytes 393248 | tf_op jit(solution)/shard_map/ppermute | solution.py:1450
  50.5 4.0 select_bitcast_fusion.2
  54.5 17.4 %collective-permute-done.3 = bf16[256,1536]{1,0:T(8,128)(2,1)} collective-permute-done((bf16[256,1536]{1,0:T(8,128)(2,1)S(1)}, bf16[256,1536]{1,0:T(8,128)(2,1)}, u32[]{:S(2)}, u32[]{:S(2)}) %collective-permute-start.3) | collective-permute-done | bytes 786464 | tf_op jit(solution)/shard_map/ppermute | solution.py:1450
  73.5 9.1 %collective-permute-done = bf16[4,256,1024]{2,1,0:T(8,128)(2,1)} collective-permute-done((bf16[4,256,1024]{2,1,0:T(8,128)(2,1)S(1)}, bf16[4,256,1024]{2,1,0:T(8,128)(2,1)}, u32[]{:S(2)}, u32[]{:S(2)}) %collective-permute-start) | collective-permute-done | bytes 2097184 | tf_op jit(solution)/shard_map/ppermute | solution.py:1599
  88.9 53.3 %collective-permute-done.4 = bf16[512,1536]{1,0:T(8,128)(2,1)S(1)} collective-permute-done((bf16[512,1536]{1,0:T(8,128)(2,1)S(1)}, bf16[512,1536]{1,0:T(8,128)(2,1)S(1)}, u32[]{:S(2)}, u32[]{:S(2)}) %collective-permute-start.4) | collective-permute-done | bytes 1572896 | tf_op jit(solution)/shard_map/ppermute | solution.py:1449
  143.0 6.2 collective-permute-done.5
  163.3 19.1 %project.1 = (bf16[1024,2048]{1,0:T(8,128)(2,1)}, bf16[2048,1024]{1,0:T(8,128)(2,1)}, bf16[2048,1024]{1,0:T(8,128)(2,1)}, bf16[2048,1024]{1,0:T(8,128)(2,1)}) custom-call(bf16[2048,1024]{1,0:T(8,128)(2,1)} %bitcast.283, f32[1,1024]{1,0:T(1,128)} %squeeze.138.gain, ...), custom_call_target="tpu_custom_call" | custom-call | flops 12884901888 | bytes 27262976 | tf_op jit(solution)/shard_map/project/pallas_call | solution.py:675
  182.4 90.9 %forward.1 = (bf16[2048,1024]{1,0:T(8,128)(2,1)}, bf16[2048,1024]{1,0:T(8,128)(2,1)}, bf16[1024,2048]{1,0:T(8,128)(2,1)}, bf16[2048,1024]{1,0:T(8,128)(2,1)}, bf...) custom-call(s32[8]{0:T(128)} %convert_element_type.383.flags, ...), custom_call_target="tpu_custom_call" | custom-call | flops 41999998976 | bytes 100000000 | tf_op jit(solution)/shard_map/forward/pallas_call | solution.py:811
  278.9 20.0 %all-gather.5.cloned.1.call-done.w0.w1.weights = bf16[2048,4608]{1,0:T(8,128)(2,1)} async-done(((bf16[64,4608]{1,0:T(8,128)(2,1)}), bf16[2048,4608]{1,0:T(8,128)(2,1)}) %all-gather.5.cloned.1.call-update) | async-done | bytes 18874384 | tf_op jit(solution)/shard_map/all_gather | solution.py:1430
  298.9 14.4 %middle.1 = (bf16[2048,1024]{1,0:T(8,128)(2,1)}, bf16[2048,1024]{1,0:T(8,128)(2,1)}, bf16[1024,2048]{1,0:T(8,128)(2,1)}, bf16[1024,2048]{1,0:T(8,128)(2,1)}) custom-call(bf16[2048,1024]{1,0:T(8,128)(2,1)} %bitcast.284, bf16[2048,1024]{1,0:T(8,128)(2,1)} %get-tuple-element.102.mixed.right.token_mixed, ...), custom_call_target="tpu_custom_call" | custom-call | flops 4294967296 | bytes 33554432 | tf_op jit(solution)/shard_map/middle/pallas_call | solution.py:887
  313.3 127.5 %mlp.1 = (bf16[2048,1024]{1,0:T(8,128)(2,1)}, bf16[2048,1024]{1,0:T(8,128)(2,1)}, bf16[2048,4608]{1,0:T(8,128)(2,1)}) custom-call(bf16[2048,1024]{1,0:T(8,128)(2,1)} %get-tuple-element.107.mlp_in, bf16[1024,2048]{1,0:T(8,128)(2,1)} %get-tuple-element.108.mlp_turned, bf16[2048,1024]{1,0:T(8,128)(2,1)} %bitcast.281, ...), custom_call_target="tpu_custom_call" | custom-call | flops 102999998464 | bytes 60000000 | tf_op jit(solution)/shard_map/mlp/pallas_call | solution.py:961
  440.8 17.0 %after_mlp.1 = (bf16[2048,1024]{1,0:T(8,128)(2,1)}, bf16[2048,1024]{1,0:T(8,128)(2,1)}, bf16[1024,2048]{1,0:T(8,128)(2,1)}, bf16[2048,1024]{1,0:T(8,128)(2,1)}, f32[1,1024]{1,0:T(1,128)}) custom-call(bf16[2048,1024]{1,0:T(8,128)(2,1)} %get-tuple-element.106.middle, bf16[2048,1024]{1,0:T(8,128)(2,1)} %get-tuple-element.110.mlp_out, ...), custom_call_target="tpu_custom_call" | custom-call | flops 4294967296 | bytes 33554432 | tf_op jit(solution)/shard_map/after_mlp/pallas_call | solution.py:1010
  457.7 8.5 %whole_weight_grad.1 = bf16[2048,4608]{1,0:T(8,128)(2,1)} custom-call(bf16[1024,2048]{1,0:T(8,128)(2,1)} %get-tuple-element.118.turned, bf16[2048,1024]{1,0:T(8,128)(2,1)} %get-tuple-element.102.mixed.right.token_mixed, bf16[2048,4608]{1,0:T(8,128)(2,1)} %get-tuple-element.119.into), custom_call_target="tpu_custom_call", output_to_operand_aliasing={{}: (2, {})} | custom-call | flops 4294967296 | bytes 8388608 | tf_op jit(solution)/shard_map/whole_weight_grad/pallas_call | solution.py:1322
  470.3 143.0 %backward.1 = (bf16[3,2048,1024]{2,1,0:T(8,128)(2,1)}, bf16[4,2048,1024]{2,1,0:T(8,128)(2,1)}, bf16[1024,2048]{1,0:T(8,128)(2,1)}, bf16[512,1024]{1,0:T(8,128)(2...) custom-call(s32[8]{0:T(128)} %convert_element_type.383.flags, bf16[2048,1024]{1,0:T(8,128)(2,1)} %get-tuple-element.98.query, ...), custom_call_target="tpu_custom_call" | custom-call | flops 70000001024 | bytes 100000000 | tf_op jit(solution)/shard_map/backward/pallas_call | solution.py:1243
  618.9 13.3 %weight_grads.5 = (bf16[1024,1024]{1,0:T(8,128)(2,1)}, bf16[1024,1024]{1,0:T(8,128)(2,1)}) custom-call(s32[1]{0:T(128)} %bitcast.41.core, bf16[1024,2048]{1,0:T(8,128)(2,1)} %get-tuple-element.129.turned, bf16[4,2048,1024]{2,1,0:T(8,128)(2,1)} %get-tuple-element.134.right), custom_call_target="tpu_custom_call" | custom-call | flops 8589934592 | bytes 12582912 | tf_op jit(solution)/shard_map/weight_grads/pallas_call | solution.py:1359
  632.2 13.5 %weight_grads.6 = (bf16[1024,1024]{1,0:T(8,128)(2,1)}, bf16[1024,1024]{1,0:T(8,128)(2,1)}) custom-call(s32[1]{0:T(128)} %bitcast.41.core, bf16[1024,2048]{1,0:T(8,128)(2,1)} %get-tuple-element.129.turned, bf16[4,2048,1024]{2,1,0:T(8,128)(2,1)} %get-tuple-element.134.right), custom_call_target="tpu_custom_call" | custom-call | flops 8589934592 | bytes 12582912 | tf_op jit(solution)/shard_map/weight_grads/pallas_call | solution.py:1359
  651.2 13.8 %weight_grads.7 = (bf16[1024,1024]{1,0:T(8,128)(2,1)}, bf16[1024,1024]{1,0:T(8,128)(2,1)}) custom-call(s32[1]{0:T(128)} %bitcast.41.core, bf16[1024,2048]{1,0:T(8,128)(2,1)} %get-tuple-element.128.turned, bf16[3,2048,1024]{2,1,0:T(8,128)(2,1)} %get-tuple-element.148.right.grads), custom_call_target="tpu_custom_call" | custom-call | flops 8589934592 | bytes 12582912 | tf_op jit(solution)/shard_map/weight_grads/pallas_call | solution.py:1359
  670.0 8.5 %weight_grads.8 = (bf16[1024,1024]{1,0:T(8,128)(2,1)}, bf16[1024,1024]{1,0:T(8,128)(2,1)}) custom-call(s32[1]{0:T(128)} %bitcast.41.core, bf16[1024,2048]{1,0:T(8,128)(2,1)} %get-tuple-element.128.turned, bf16[3,2048,1024]{2,1,0:T(8,128)(2,1)} %get-tuple-element.148.right.grads), custom_call_target="tpu_custom_call" | custom-call | flops 4294967296 | bytes 8388608 | tf_op jit(solution)/shard_map/weight_grads/pallas_call | solution.py:1359
  682.9 8.6 %weight_grads.9 = (bf16[1024,1024]{1,0:T(8,128)(2,1)}, bf16[1024,1024]{1,0:T(8,128)(2,1)}) custom-call(s32[1]{0:T(128)} %bitcast.41.core, bf16[1024,2048]{1,0:T(8,128)(2,1)} %get-tuple-element.146.turned, bf16[1,2048,1024]{2,1,0:T(8,128)(2,1)} %bitcast.353, ...), custom_call_target="tpu_custom_call", output_to_operand_aliasing={{0}: (3, {}), {1}: (4, {})} | custom-call | flops 4294967296 | bytes 8388608 | tf_op jit(solution)/shard_map/weight_grads/pallas_call | solution.py:1359
  697.4 21.8 %token_grad.1 = (bf16[2048,1024]{1,0:T(8,128)(2,1)}, f32[1,1024]{1,0:T(1,128)}) custom-call(bf16[3,2048,1024]{2,1,0:T(8,128)(2,1)} %get-tuple-element.148.right.grads, bf16[2048,2944]{1,0:T(8,128)(2,1)} %all-gather.3.cloned.1.call-done.w0.w1.query0.query1.key0.key1.weight_query.weight_key, ...), custom_call_target="tpu_custom_call" | custom-call | flops 12884901888 | bytes 25165824 | tf_op jit(solution)/shard_map/token_grad/pallas_call | solution.py:1410
  732.6 11.6 %collective-permute-done.14 = bf16[1,512,1024]{2,1,0:T(8,128)(2,1)} collective-permute-done((bf16[1,512,1024]{2,1,0:T(8,128)(2,1)}, bf16[1,512,1024]{2,1,0:T(8,128)(2,1)}, u32[]{:S(2)}, u32[]{:S(2)}) %collective-permute-start.14) | collective-permute-done | bytes 1048608 | tf_op jit(solution)/shard_map/ppermute | solution.py:1449
  744.1 10.0 %collective-permute-done.18 = bf16[1,256,1024]{2,1,0:T(8,128)(2,1)S(1)} collective-permute-done((bf16[1,256,1024]{2,1,0:T(8,128)(2,1)S(1)}, bf16[1,256,1024]{2,1,0:T(8,128)(2,1)S(1)}, u32[]{:S(2)}, u32[]{:S(2)}) %collective-permute-start.18) | collective-permute-done | bytes 524320 | tf_op jit(solution)/shard_map/ppermute | solution.py:1449
  754.2 5.8 collective-permute-done.16
  770.8 3.6 collective-permute-done.22
  774.4 6.6 collective-permute-done.21
  791.7 6.8 collective-permute-done.27
  806.3 6.3 collective-permute-done.31
  815.6 3.5 collective-permute-done.33
  820.3 13.0 %collective-permute-done.11 = bf16[4,256,1024]{2,1,0:T(8,128)(2,1)S(1)} collective-permute-done((bf16[4,256,1024]{2,1,0:T(8,128)(2,1)S(1)}, bf16[4,256,1024]{2,1,0:T(8,128)(2,1)S(1)}, u32[]{:S(2)}, u32[]{:S(2)}) %collective-permute-start.11) | collective-permute-done | bytes 2097184 | tf_op jit(solution)/shard_map/ppermute | solution.py:1576
  (225 shorter events, 124.6 us)
Async XLA Ops:
  7.2 147.4 %all-gather.3.cloned.1.call-start = ((), (), s32[]{:S(2)}) async-start(), calls=%async_computation.1 | async-start | bytes 12435456 | tf_op jit(solution)/shard_map/all_gather | solution.py:1430
  13.7 285.2 %all-gather.5.cloned.1.call-start = ((), (), s32[]{:S(2)}) async-start(), calls=%async_computation.2 | async-start | bytes 19464192 | tf_op jit(solution)/shard_map/all_gather | solution.py:1430
  15.3 13.5 %collective-permute-start.1 = (bf16[64,1536]{1,0:T(8,128)(2,1)}, bf16[64,1536]{1,0:T(8,128)(2,1)}, u32[]{:S(2)}, u32[]{:S(2)}) collective-permute-start(bf16[64,1536]{1,0:T(8,128)(2,1)} %pad_maximum_fusion.10), channel_id=1, source_target_pairs={{0,16},{2,18},{4,20},{6,22},{8,24},{10,26},{12,28},{14,30},{16,0},... | collective-permute-start | bytes 589832 | tf_op jit(solution)/shard_map/ppermute | solution.py:1450
  21.9 60.7 %collective-permute-start = (bf16[4,256,1024]{2,1,0:T(8,128)(2,1)S(1)}, bf16[4,256,1024]{2,1,0:T(8,128)(2,1)}, u32[]{:S(2)}, u32[]{:S(2)}) collective-permute-start(bf16[4,256,1024]{2,1,0:T(8,128)(2,1)S(1)} %select_bitcast_fusion.3), channel_id=1, source_target_pairs={{0,1},{1,0},{2,3},{3,2},{4,5},{5,4},{6,7},{7,6},{8,9},{9,8},{10,11... | collective-permute-start | bytes 6291464 | tf_op jit(solution)/shard_map/ppermute | solution.py:1599
  29.9 17.0 %collective-permute-start.2 = (bf16[128,1536]{1,0:T(8,128)(2,1)S(1)}, bf16[128,1536]{1,0:T(8,128)(2,1)S(1)}, u32[]{:S(2)}, u32[]{:S(2)}) collective-permute-start(bf16[128,1536]{1,0:T(8,128)(2,1)S(1)} %bitcast.332), channel_id=1, source_target_pairs={{0,8},{2,10},{4,12},{6,14},{8,0},{10,2},{12,4},{14,6},{16,24},{18,... | collective-permute-start | bytes 1179656 | tf_op jit(solution)/shard_map/ppermute | solution.py:1450
  47.1 24.8 %collective-permute-start.3 = (bf16[256,1536]{1,0:T(8,128)(2,1)S(1)}, bf16[256,1536]{1,0:T(8,128)(2,1)}, u32[]{:S(2)}, u32[]{:S(2)}) collective-permute-start(bf16[256,1536]{1,0:T(8,128)(2,1)S(1)} %bitcast.320), channel_id=1, source_target_pairs={{0,4},{2,6},{4,0},{6,2},{8,12},{10,14},{12,8},{14,10},{16,20},{18,... | collective-permute-start | bytes 2359304 | tf_op jit(solution)/shard_map/ppermute | solution.py:1450
  87.0 55.1 %collective-permute-start.4 = (bf16[512,1536]{1,0:T(8,128)(2,1)S(1)}, bf16[512,1536]{1,0:T(8,128)(2,1)S(1)}, u32[]{:S(2)}, u32[]{:S(2)}) collective-permute-start(bf16[512,1536]{1,0:T(8,128)(2,1)S(1)} %bitcast.306), channel_id=1, source_target_pairs={{0,1},{1,0},{2,3},{3,2},{4,5},{5,4},{6,7},{7,6},{8,9},{9,8},{10,11... | collective-permute-start | bytes 4718600 | tf_op jit(solution)/shard_map/ppermute | solution.py:1449
  154.7 542.7 %reduce-scatter.2.cloned.1.call-start = ((), (), s32[]{:S(2)}) async-start(), calls=%async_computation.3 | async-start | bytes 19464192 | tf_op jit(solution)/shard_map/reduce_scatter | solution.py:1434
  161.3 112.0 %collective-permute-start.6 = (bf16[4,256,1024]{2,1,0:T(8,128)(2,1)S(1)}, bf16[4,256,1024]{2,1,0:T(8,128)(2,1)}, u32[]{:S(2)}, u32[]{:S(2)}) collective-permute-start(bf16[4,256,1024]{2,1,0:T(8,128)(2,1)S(1)} %copy-done.7), channel_id=1, source_target_pairs={{0,1},{1,0},{2,3},{3,2},{4,5},{5,4},{6,7},{7,6},{8,9},{9,8},{10,11... | collective-permute-start | bytes 6291464 | tf_op jit(solution)/shard_map/ppermute | solution.py:1611
  468.8 144.5 %collective-permute-start.7 = (bf16[4,256,1024]{2,1,0:T(8,128)(2,1)S(1)}, bf16[4,256,1024]{2,1,0:T(8,128)(2,1)}, u32[]{:S(2)}, u32[]{:S(2)}) collective-permute-start(bf16[4,256,1024]{2,1,0:T(8,128)(2,1)S(1)} %select_bitcast_fusion.1), channel_id=1, source_target_pairs={{0,1},{1,0},{2,3},{3,2},{4,5},{5,4},{6,7},{7,6},{8,9},{9,8},{10,11... | collective-permute-start | bytes 6291464 | tf_op jit(solution)/shard_map/ppermute | solution.py:1576
  632.2 14.1 %collective-permute-start.8 = (bf16[1024,1024]{1,0:T(8,128)(2,1)}, bf16[1024,1024]{1,0:T(8,128)(2,1)}, u32[]{:S(2)}, u32[]{:S(2)}) collective-permute-start(bf16[1024,1024]{1,0:T(8,128)(2,1)} %get-tuple-element.133), channel_id=1, source_target_pairs={{0,2},{2,0},{4,6},{6,4},{8,10},{10,8},{12,14},{14,12},{16,18},{18,... | collective-permute-start | bytes 6291464 | tf_op jit(solution)/shard_map/ppermute | solution.py:1450
  645.8 19.3 %collective-permute-start.10 = (bf16[1024,1024]{1,0:T(8,128)(2,1)}, bf16[1024,1024]{1,0:T(8,128)(2,1)}, u32[]{:S(2)}, u32[]{:S(2)}) collective-permute-start(bf16[1024,1024]{1,0:T(8,128)(2,1)} %get-tuple-element.137), channel_id=1, source_target_pairs={{0,2},{2,0},{4,6},{6,4},{8,10},{10,8},{12,14},{14,12},{16,18},{18,... | collective-permute-start | bytes 6291464 | tf_op jit(solution)/shard_map/ppermute | solution.py:1450
  665.0 13.6 %collective-permute-start.9 = (bf16[1024,1024]{1,0:T(8,128)(2,1)}, bf16[1024,1024]{1,0:T(8,128)(2,1)}, u32[]{:S(2)}, u32[]{:S(2)}) collective-permute-start(bf16[1024,1024]{1,0:T(8,128)(2,1)} %get-tuple-element.140), channel_id=1, source_target_pairs={{0,2},{2,0},{4,6},{6,4},{8,10},{10,8},{12,14},{14,12},{16,18},{18,... | collective-permute-start | bytes 6291464 | tf_op jit(solution)/shard_map/ppermute | solution.py:1450
  691.5 29.0 %collective-permute-start.12 = (bf16[1024,1024]{1,0:T(8,128)(2,1)}, bf16[1024,1024]{1,0:T(8,128)(2,1)}, u32[]{:S(2)}, u32[]{:S(2)}) collective-permute-start(bf16[1024,1024]{1,0:T(8,128)(2,1)} %get-tuple-element.147), channel_id=1, source_target_pairs={{0,2},{2,0},{4,6},{6,4},{8,10},{10,8},{12,14},{14,12},{16,18},{18,... | collective-permute-start | bytes 6291464 | tf_op jit(solution)/shard_map/ppermute | solution.py:1450
  695.0 25.5 %collective-permute-start.17 = (bf16[8,64,1024]{2,1,0:T(8,128)(2,1)}, bf16[8,64,1024]{2,1,0:T(8,128)(2,1)}, u32[]{:S(2)}, u32[]{:S(2)}) collective-permute-start(bf16[8,64,1024]{2,1,0:T(8,128)(2,1)} %dynamic-slice_bitcast_fusion.2), channel_id=1, source_target_pairs={{0,4},{2,6},{4,0},{6,2},{8,12},{10,14},{12,8},{14,10},{16,20},{18,... | collective-permute-start | bytes 3145736 | tf_op jit(solution)/shard_map/ppermute | solution.py:1450
  695.3 33.6 %collective-permute-start.15 = (bf16[1,512,1024]{2,1,0:T(8,128)(2,1)}, bf16[1,512,1024]{2,1,0:T(8,128)(2,1)}, u32[]{:S(2)}, u32[]{:S(2)}) collective-permute-start(bf16[1,512,1024]{2,1,0:T(8,128)(2,1)} %dynamic-slice_bitcast_fusion.3), channel_id=1, source_target_pairs={{0,1},{1,0},{2,3},{3,2},{4,5},{5,4},{6,7},{7,6},{8,9},{9,8},{10,11... | collective-permute-start | bytes 3145736 | tf_op jit(solution)/shard_map/ppermute | solution.py:1449
  696.7 47.4 %collective-permute-start.14 = (bf16[1,512,1024]{2,1,0:T(8,128)(2,1)}, bf16[1,512,1024]{2,1,0:T(8,128)(2,1)}, u32[]{:S(2)}, u32[]{:S(2)}) collective-permute-start(bf16[1,512,1024]{2,1,0:T(8,128)(2,1)} %dynamic-slice_bitcast_fusion.1), channel_id=1, source_target_pairs={{0,1},{1,0},{2,3},{3,2},{4,5},{5,4},{6,7},{7,6},{8,9},{9,8},{10,11... | collective-permute-start | bytes 3145736 | tf_op jit(solution)/shard_map/ppermute | solution.py:1449
  720.3 39.6 %collective-permute-start.19 = (bf16[1024,384]{1,0:T(8,128)(2,1)S(1)}, bf16[1024,384]{1,0:T(8,128)(2,1)S(1)}, u32[]{:S(2)}, u32[]{:S(2)}) collective-permute-start(bf16[1024,384]{1,0:T(8,128)(2,1)S(1)} %bitcast.338), channel_id=1, source_target_pairs={{0,2},{2,0},{4,6},{6,4},{8,10},{10,8},{12,14},{14,12},{16,18},{18,... | collective-permute-start | bytes 2359304 | tf_op jit(solution)/shard_map/ppermute | solution.py:1450
  724.3 35.7 %collective-permute-start.13 = (bf16[8,64,1024]{2,1,0:T(8,128)(2,1)S(1)}, bf16[8,64,1024]{2,1,0:T(8,128)(2,1)S(1)}, u32[]{:S(2)}, u32[]{:S(2)}) collective-permute-start(bf16[8,64,1024]{2,1,0:T(8,128)(2,1)S(1)} %dynamic-slice_bitcast_fusion), channel_id=1, source_target_pairs={{0,4},{2,6},{4,0},{6,2},{8,12},{10,14},{12,8},{14,10},{16,20},{18,... | collective-permute-start | bytes 3145736 | tf_op jit(solution)/shard_map/ppermute | solution.py:1450
  727.8 26.4 %collective-permute-start.18 = (bf16[1,256,1024]{2,1,0:T(8,128)(2,1)S(1)}, bf16[1,256,1024]{2,1,0:T(8,128)(2,1)S(1)}, u32[]{:S(2)}, u32[]{:S(2)}) collective-permute-start(bf16[1,256,1024]{2,1,0:T(8,128)(2,1)S(1)} %dynamic-slice_bitcast_fusion.6), channel_id=1, source_target_pairs={{0,1},{1,0},{2,3},{3,2},{4,5},{5,4},{6,7},{7,6},{8,9},{9,8},{10,11... | collective-permute-start | bytes 1572872 | tf_op jit(solution)/shard_map/ppermute | solution.py:1449
  730.8 29.2 %collective-permute-start.16 = (bf16[4,64,1024]{2,1,0:T(8,128)(2,1)S(1)}, bf16[4,64,1024]{2,1,0:T(8,128)(2,1)S(1)}, u32[]{:S(2)}, u32[]{:S(2)}) collective-permute-start(bf16[4,64,1024]{2,1,0:T(8,128)(2,1)S(1)} %dynamic-slice_bitcast_fusion.7), channel_id=1, source_target_pairs={{0,4},{2,6},{4,0},{6,2},{8,12},{10,14},{12,8},{14,10},{16,20},{18,... | collective-permute-start | bytes 1572872 | tf_op jit(solution)/shard_map/ppermute | solution.py:1450
  760.3 14.1 %collective-permute-start.24 = (bf16[8,64,384]{2,1,0:T(8,128)(2,1)S(1)}, bf16[8,64,384]{2,1,0:T(8,128)(2,1)S(1)}, u32[]{:S(2)}, u32[]{:S(2)}) collective-permute-start(bf16[8,64,384]{2,1,0:T(8,128)(2,1)S(1)} %dynamic-slice_bitcast_fusion.8), channel_id=1, source_target_pairs={{0,4},{2,6},{4,0},{6,2},{8,12},{10,14},{12,8},{14,10},{16,20},{18,... | collective-permute-start | bytes 1179656 | tf_op jit(solution)/shard_map/ppermute | solution.py:1450
  764.3 16.7 %collective-permute-start.21 = (bf16[4,64,1024]{2,1,0:T(8,128)(2,1)S(1)}, bf16[4,64,1024]{2,1,0:T(8,128)(2,1)S(1)}, u32[]{:S(2)}, u32[]{:S(2)}) collective-permute-start(bf16[4,64,1024]{2,1,0:T(8,128)(2,1)S(1)} %dynamic-slice_bitcast_fusion.4), channel_id=1, source_target_pairs={{0,4},{2,6},{4,0},{6,2},{8,12},{10,14},{12,8},{14,10},{16,20},{18,... | collective-permute-start | bytes 1572872 | tf_op jit(solution)/shard_map/ppermute | solution.py:1450
  765.2 15.8 %collective-permute-start.20 = (bf16[1,256,1024]{2,1,0:T(8,128)(2,1)S(1)}, bf16[1,256,1024]{2,1,0:T(8,128)(2,1)S(1)}, u32[]{:S(2)}, u32[]{:S(2)}) collective-permute-start(bf16[1,256,1024]{2,1,0:T(8,128)(2,1)S(1)} %dynamic-slice_bitcast_fusion.5), channel_id=1, source_target_pairs={{0,1},{1,0},{2,3},{3,2},{4,5},{5,4},{6,7},{7,6},{8,9},{9,8},{10,11... | collective-permute-start | bytes 1572872 | tf_op jit(solution)/shard_map/ppermute | solution.py:1449
  781.2 17.3 %collective-permute-start.29 = (bf16[1,256,384]{2,1,0:T(8,128)(2,1)S(1)}, bf16[1,256,384]{2,1,0:T(8,128)(2,1)S(1)}, u32[]{:S(2)}, u32[]{:S(2)}) collective-permute-start(bf16[1,256,384]{2,1,0:T(8,128)(2,1)S(1)} %dynamic-slice_bitcast_fusion.13), channel_id=1, source_target_pairs={{0,1},{1,0},{2,3},{3,2},{4,5},{5,4},{6,7},{7,6},{8,9},{9,8},{10,11... | collective-permute-start | bytes 589832 | tf_op jit(solution)/shard_map/ppermute | solution.py:1449
  782.7 8.4 %collective-permute-start.28 = (bf16[1,64,1024]{2,1,0:T(8,128)(2,1)S(1)}, bf16[1,64,1024]{2,1,0:T(8,128)(2,1)S(1)}, u32[]{:S(2)}, u32[]{:S(2)}) collective-permute-start(bf16[1,64,1024]{2,1,0:T(8,128)(2,1)S(1)} %constant_dynamic-slice_fusion.3), channel_id=1, source_target_pairs={{0,16},{2,18},{4,20},{6,22},{8,24},{10,26},{12,28},{14,30},{16,0},... | collective-permute-start | bytes 393224 | tf_op jit(solution)/shard_map/ppermute | solution.py:1450
  784.6 13.9 %collective-permute-start.26 = (bf16[2,64,1024]{2,1,0:T(8,128)(2,1)S(1)}, bf16[2,64,1024]{2,1,0:T(8,128)(2,1)S(1)}, u32[]{:S(2)}, u32[]{:S(2)}) collective-permute-start(bf16[2,64,1024]{2,1,0:T(8,128)(2,1)S(1)} %dynamic-slice_bitcast_fusion.9), channel_id=1, source_target_pairs={{0,8},{2,10},{4,12},{6,14},{8,0},{10,2},{12,4},{14,6},{16,24},{18,... | collective-permute-start | bytes 786440 | tf_op jit(solution)/shard_map/ppermute | solution.py:1450
  785.2 15.7 %collective-permute-start.25 = (bf16[2,64,1024]{2,1,0:T(8,128)(2,1)S(1)}, bf16[2,64,1024]{2,1,0:T(8,128)(2,1)S(1)}, u32[]{:S(2)}, u32[]{:S(2)}) collective-permute-start(bf16[2,64,1024]{2,1,0:T(8,128)(2,1)S(1)} %dynamic-slice_bitcast_fusion.10), channel_id=1, source_target_pairs={{0,8},{2,10},{4,12},{6,14},{8,0},{10,2},{12,4},{14,6},{16,24},{18,... | collective-permute-start | bytes 786440 | tf_op jit(solution)/shard_map/ppermute | solution.py:1450
  787.0 11.5 %collective-permute-start.27 = (bf16[1,64,1024]{2,1,0:T(8,128)(2,1)S(1)}, bf16[1,64,1024]{2,1,0:T(8,128)(2,1)S(1)}, u32[]{:S(2)}, u32[]{:S(2)}) collective-permute-start(bf16[1,64,1024]{2,1,0:T(8,128)(2,1)S(1)} %constant_dynamic-slice_fusion.4), channel_id=1, source_target_pairs={{0,16},{2,18},{4,20},{6,22},{8,24},{10,26},{12,28},{14,30},{16,0},... | collective-permute-start | bytes 393224 | tf_op jit(solution)/shard_map/ppermute | solution.py:1450
  791.2 42.2 %collective-permute-start.11 = (bf16[4,256,1024]{2,1,0:T(8,128)(2,1)S(1)}, bf16[4,256,1024]{2,1,0:T(8,128)(2,1)S(1)}, u32[]{:S(2)}, u32[]{:S(2)}) collective-permute-start(bf16[4,256,1024]{2,1,0:T(8,128)(2,1)S(1)} %select_bitcast_fusion), channel_id=1, source_target_pairs={{0,1},{1,0},{2,3},{3,2},{4,5},{5,4},{6,7},{7,6},{8,9},{9,8},{10,11... | collective-permute-start | bytes 6291464 | tf_op jit(solution)/shard_map/ppermute | solution.py:1576
  801.3 11.3 %collective-permute-start.31 = (bf16[1,64,1024]{2,1,0:T(8,128)(2,1)S(1)}, bf16[1,64,1024]{2,1,0:T(8,128)(2,1)S(1)}, u32[]{:S(2)}, u32[]{:S(2)}) collective-permute-start(bf16[1,64,1024]{2,1,0:T(8,128)(2,1)S(1)} %constant_dynamic-slice_fusion.1), channel_id=1, source_target_pairs={{0,16},{2,18},{4,20},{6,22},{8,24},{10,26},{12,28},{14,30},{16,0},... | collective-permute-start | bytes 393224 | tf_op jit(solution)/shard_map/ppermute | solution.py:1450
  802.6 11.4 %collective-permute-start.30 = (bf16[1,64,1024]{2,1,0:T(8,128)(2,1)S(1)}, bf16[1,64,1024]{2,1,0:T(8,128)(2,1)S(1)}, u32[]{:S(2)}, u32[]{:S(2)}) collective-permute-start(bf16[1,64,1024]{2,1,0:T(8,128)(2,1)S(1)} %constant_dynamic-slice_fusion.2), channel_id=1, source_target_pairs={{0,16},{2,18},{4,20},{6,22},{8,24},{10,26},{12,28},{14,30},{16,0},... | collective-permute-start | bytes 393224 | tf_op jit(solution)/shard_map/ppermute | solution.py:1450
  (30 other events, 234.7 us)
Sparse Core Ops, SparseCore 0:
  13.8 136.1 all-gather.2
  154.8 144.0 all-gather.4
  466.4 203.3 reduce-scatter.1
